TPU v7x, 32 devices: a whole 2x2x4 slice. The times are simulated.
32 devices in a mesh: win: 8 (over z, y), tmpl: 4 (over x, core).
Axes of the slice: x: 2, y: 2, z: 4, core: 2. Of those that a mesh axis runs over, the one named last changes fastest.
Arguments:
- raw: bfloat16 [512, 16384], P(('win', 'tmpl')), may hold values from -160 to 160
- ids: int32 [512], replicated, may hold values from -1 to 303, as said below
- fir: bfloat16 [64], replicated, may hold values from -0.75 to 0.75
- taps: bfloat16 [512, 30, 400], P('tmpl'), may hold values from -0.3125 to 0.3125
- channels: int32 [512, 30], P('tmpl'), may hold values from 0 to 303, all different within a row
- shifts: int32 [512, 30], P('tmpl'), may hold values from 0 to 255
Outputs:
- stack: float32 [512, 8192], P('tmpl', 'win')
Inputs may be any that keep to these rules, and one draw needn't show every extreme that they name: `ids`: each station channel 0 to 303 stands in exactly one slot, the others hold -1; the owners of one index of tmpl hold exactly 76 live slots together, and one owner of each holds 16 live slots. Each template names 30 different channels; every channel is named by some template.
All inputs are finite; a program needn't handle non-finite values.
Results may differ from a plain program's by a relative error of at most 0.007.
Values may be sent and summed in bfloat16 or wider, within the bound.
No kernel may reach another device: no remote copies, remote signals or barrier semaphores. Data moves between devices by JAX's collectives and lax.ppermute only.
A program may use at most 128 MiB of HBM per device.

v0:
```python
import math

import jax
import jax.numpy as jnp
from jax import lax
from jax.sharding import PartitionSpec as P

WIN_DEV = 1024
MARGIN = 768
TL = 400
CH = 30
DEC = 2
NTAP = 64
NS = 1792
NF = 896


def passed_along(shard, axis, by):
    devices = lax.axis_size(axis)
    pairs = [(i, i + by) for i in range(devices) if 0 <= i + by < devices]
    return lax.ppermute(shard, axis, pairs)


def band_matrix(fir, block):
    in_index = jnp.arange(DEC * block + NTAP, dtype=jnp.int32)[:, None]
    out_index = jnp.arange(block, dtype=jnp.int32)[None, :]
    offset = in_index - DEC * out_index
    onehot = offset[:, :, None] == jnp.arange(NTAP, dtype=jnp.int32)[None, None, :]
    values = jnp.where(onehot, fir.astype(jnp.float32)[None, None, :], jnp.float32(0.0))
    return jnp.sum(values, axis=2).astype(jnp.bfloat16)


def decimate(raw_ext, fir, count):
    block = math.gcd(count, 128)
    pieces = count // block
    length = DEC * block
    height = raw_ext.shape[0]
    padded = jnp.pad(raw_ext, ((0, 0), (0, (pieces + 1) * length - raw_ext.shape[1])))
    blocks = padded.reshape(height, pieces + 1, length)
    segments = jnp.concatenate([blocks[:, :pieces], blocks[:, 1:, :NTAP]], axis=2)
    band = band_matrix(fir, block)
    result = jnp.einsum("rbi,in->rbn", segments, band, preferred_element_type=jnp.float32)
    return result.reshape(height, count)


def forward_table():
    sample_index = jnp.arange(NS, dtype=jnp.int32)[:, None]
    frequency = jnp.arange(NF, dtype=jnp.int32)[None, :]
    angle = (sample_index * frequency % NS).astype(jnp.float32) * jnp.float32(2.0 * math.pi / NS)
    return jnp.concatenate([jnp.cos(angle), jnp.sin(angle)], axis=1).astype(jnp.bfloat16)


def inverse_table():
    frequency = jnp.arange(NF, dtype=jnp.int32)[:, None]
    time_index = jnp.arange(WIN_DEV, dtype=jnp.int32)[None, :]
    angle = (frequency * time_index % NS).astype(jnp.float32) * jnp.float32(2.0 * math.pi / NS)
    return jnp.concatenate([jnp.cos(angle), -jnp.sin(angle)], axis=0).astype(jnp.bfloat16)


def spectra(tiles, table):
    values = tiles.astype(jnp.float32)
    scale = lax.rsqrt(jnp.mean(values * values, axis=1, keepdims=True) + 1e-05)
    return (jnp.dot(tiles, table, preferred_element_type=jnp.float32) * scale).astype(jnp.bfloat16)


def stack_block(template_spec, data_spec, shift_block, inverse):
    tmpl_cos = template_spec[:, :NF].astype(jnp.float32)
    tmpl_sin = template_spec[:, NF:].astype(jnp.float32)
    data_cos = data_spec[:, :NF].astype(jnp.float32)
    data_sin = data_spec[:, NF:].astype(jnp.float32)
    real_part = tmpl_cos * data_cos + tmpl_sin * data_sin
    imag_part = tmpl_sin * data_cos - tmpl_cos * data_sin
    frequency = jnp.arange(NF, dtype=jnp.int32)[None, :]
    angle = (shift_block[:, None] * frequency % NS).astype(jnp.float32) * jnp.float32(
        2.0 * math.pi / NS
    )
    phase_cos = jnp.cos(angle)
    phase_sin = jnp.sin(angle)
    rotated_real = real_part * phase_cos - imag_part * phase_sin
    rotated_imag = real_part * phase_sin + imag_part * phase_cos
    group = shift_block.shape[0] // CH
    summed_real = jnp.sum(rotated_real.reshape(group, CH, NF), axis=1)
    summed_imag = jnp.sum(rotated_imag.reshape(group, CH, NF), axis=1)
    weight = jnp.where(jnp.arange(NF) == 0, 1.0, 2.0).astype(jnp.float32) / jnp.float32(CH * NS)
    packed = jnp.concatenate([summed_real * weight, summed_imag * weight], axis=1).astype(
        jnp.bfloat16
    )
    return jnp.dot(packed, inverse, preferred_element_type=jnp.float32)


def on_device(raw, ids, fir, taps, channels, shifts):
    win_count = lax.axis_size("win")
    tmpl_count = lax.axis_size("tmpl")
    slot_count = raw.shape[0]
    live_col = 3 * slot_count * win_count // 5
    chan_total = live_col * tmpl_count
    local_raw = lax.all_to_all(raw, "win", split_axis=1, concat_axis=0, tiled=True)
    extra = DEC * MARGIN + NTAP
    margin = passed_along(local_raw[:, :extra], "win", -1)
    tiles = decimate(jnp.concatenate([local_raw, margin], axis=1), fir, NS).astype(jnp.bfloat16)
    forward = forward_table()
    inverse = inverse_table()
    local_spec = spectra(tiles, forward)
    grid = (
        ids.reshape(win_count, tmpl_count, slot_count)
        .transpose(1, 0, 2)
        .reshape(tmpl_count, win_count * slot_count)
    )
    gathered = lax.all_gather(local_spec, "tmpl", axis=0, tiled=True)
    labels = grid.reshape(-1)
    position = jnp.arange(labels.shape[0], dtype=jnp.int32)
    keyed = jnp.where(labels >= 0, labels, chan_total + position)
    row_of = jnp.argsort(keyed)[:chan_total]
    flat_taps = taps.reshape(-1, TL)
    head = forward[:TL]
    template_spec = jnp.dot(flat_taps, head, preferred_element_type=jnp.float32).astype(
        jnp.bfloat16
    )
    data_rows = jnp.take(row_of, channels.reshape(-1))
    data_all = lax.optimization_barrier(jnp.take(gathered, data_rows, axis=0))
    flat_shifts = shifts.reshape(-1)
    templates_here = taps.shape[0]
    group = math.gcd(templates_here, 32)
    count = templates_here // group

    def one_block(block_index):
        start = block_index * group * CH
        spec_block = lax.dynamic_slice_in_dim(template_spec, start, group * CH, 0)
        data_spec = lax.dynamic_slice_in_dim(data_all, start, group * CH, 0)
        shift_block = lax.dynamic_slice_in_dim(flat_shifts, start, group * CH, 0)
        return stack_block(spec_block, data_spec, shift_block, inverse)

    result = lax.map(one_block, jnp.arange(count, dtype=jnp.int32))
    return result.reshape(templates_here, WIN_DEV)


def solution(mesh):
    return jax.shard_map(
        on_device,
        mesh=mesh,
        in_specs=(
            P(("win", "tmpl"), None),
            P(),
            P(),
            P("tmpl", None, None),
            P("tmpl", None),
            P("tmpl", None),
        ),
        out_specs=P("tmpl", "win"),
        check_vma=False,
    )
```

profile of v0, /device:TPU:0, one launch (start us, length us, event | category | flops | bytes accessed | tf_op | source)
XLA Modules:
  0.0 354.1 jit_solution(3715796404567599489)
XLA Ops:
  6.5 1.9 copy.42
  8.4 7.3 %all-to-all-start = ((bf16[16,8,2048]{2,0,1:T(8,128)(2,1)}), bf16[16,8,2048]{2,0,1:T(8,128)(2,1)S(1)}, u32[]{:S(2)}, u32[]{:S(2)}) async-start(bf16[16,8,2048]{2,0,1:T(8,128)(2,1)} %bitcast.25), calls=%async_computation | async-start | bytes 1048576 | tf_op jit(solution)/shard_map/all_to_all | solution.py:97
  15.8 28.3 %sine_convert_fusion = (bf16[1792,896]{1,0:T(8,128)(2,1)}, bf16[1792,896]{1,0:T(8,128)(2,1)}) fusion(), kind=kLoop, calls=%fused_computation.41 | loop fusion | flops 17661952 | bytes 6422528 | tf_op jit(solution)/shard_map/convert.5
  44.1 1.3 collective-permute-start
  45.5 3.7 %select_reduce_fusion = bf16[320,128]{1,0:T(8,128)(2,1)S(1)} fusion(f32[64]{0:T(128)S(1)} %convert_element_type.77, s32[320,128]{1,0:T(8,128)S(1)} %iota_subtract_fusion), kind=kLoop, calls=%fused_computation.32 | loop fusion | flops 7823360 | bytes 246016 | tf_op jit(solution)/shard_map/reduce_sum | solution.py:30
  49.2 8.1 %collective-permute-done = bf16[128,1600]{1,0:T(8,128)(2,1)S(1)} collective-permute-done((bf16[128,1600]{1,0:T(8,128)(2,1)S(1)}, bf16[128,1600]{1,0:T(8,128)(2,1)S(1)}, u32[]{:S(2)}, u32[]{:S(2)}) %collective-permute-start) | collective-permute-done | bytes 409632 | tf_op jit(solution)/shard_map/ppermute | solution.py:21
  57.3 0.1 pad_maximum_fusion.1
  57.4 1.3 copy.39
  58.7 0.1 pad.4.clone
  58.9 0.6 multiply_reduce_fusion
  59.4 1.1 copy-done
  60.6 1.0 copy-done.2
  61.6 1.8 fusion.32
  63.4 0.1 copy.32
  63.5 0.1 reshape.158
  63.7 0.1 reshape.156
  63.8 0.1 reshape.157
  63.9 0.1 reshape_reshape.3
  64.0 8.8 %copy.31 = bf16[128,30,400]{2,1,0:T(8,128)(2,1)} copy(bf16[128,30,400]{0,2,1:T(8,128)(2,1)S(1)} %copy-done.3) | data formatting | bytes 6144000 | tf_op args[3]
  72.9 7.1 %reshape.155 = bf16[3840,400]{1,0:T(8,128)(2,1)} reshape(bf16[128,30,400]{2,1,0:T(8,128)(2,1)} %copy.31) | data formatting | bytes 6144000 | tf_op jit(solution)/shard_map/reshape | solution.py:114
  79.9 15.3 %fusion.14 = bf16[3840,1792]{0,1:T(8,128)(2,1)} fusion(bf16[3840,400]{1,0:T(8,128)(2,1)} %reshape.155, bf16[1792,896]{1,0:T(8,128)(2,1)S(1)} %copy-done.1, bf16[1792,896]{1,0:T(8,128)(2,1)} %get-tuple-element.155), kind=kOutput, calls=%fused_computation.31 | convolution fusion | flops 5514772480 | bytes 23257088 | tf_op jit(solution)/shard_map/dot_general | solution.py:116
  95.2 18.3 %copy.38 = bf16[3840,1792]{1,0:T(8,128)(2,1)} copy(bf16[3840,1792]{0,1:T(8,128)(2,1)} %fusion.14) | data formatting | bytes 27525120 | tf_op jit(solution)/shard_map/while | solution.py:133
  113.5 0.1 copy.37
  113.6 0.1 reshape.160
  113.7 3.7 %sort.17 = (s32[512]{0:T(512)}, s32[512]{0:T(512)S(1)}) sort(s32[512]{0:T(512)S(1)} %compare_select_fusion.4, s32[512]{0:T(512)S(1)} %iota.62), dimensions={0}, to_apply=%region_0.1 | sort | flops 4608 | bytes 8192 | tf_op jit(solution)/shard_map/jit(argsort)/sort | solution.py:113
  117.5 22.9 %gather_fusion = s32[3840]{0:T(1024)S(1)} fusion(s32[304]{0:T(512)S(1)} %bitcast.33, s32[4096]{0:T(1024)S(1)} %pad_clamp_fusion.1), kind=kCustom, calls=%fused_computation | custom fusion | bytes 46080 | tf_op jit(solution)/shard_map/jit(_take)/gather | solution.py:119
  140.4 0.1 fusion.43
  140.6 15.8 %negate_convert_fusion = (bf16[896,1024]{1,0:T(8,128)(2,1)S(1)}, bf16[896,1024]{1,0:T(8,128)(2,1)S(1)}) fusion(), kind=kLoop, calls=%fused_computation.51 | loop fusion | flops 11010048 | bytes 3670016 | tf_op jit(solution)/shard_map/convert.3
  156.3 2.3 pad_maximum_fusion
  158.6 28.2 %gather_fusion.1 = bf16[3840,1792]{1,0:T(8,128)(2,1)} fusion(bf16[512,1792]{1,0:T(8,128)(2,1)} %all-gather.2.cloned.1.call-done, s32[4096]{0:T(1024)S(1)} %pad_clamp_fusion), kind=kCustom, calls=%fused_computation.1 | custom fusion | bytes 27540480 | tf_op jit(solution)/shard_map/jit(_take)/gather | solution.py:120
  186.8 13.5 %broadcast_select_fusion = bf16[3840,1792]{1,0:T(8,128)(2,1)} fusion(bf16[3840,1792]{1,0:T(8,128)(2,1)} %gather_fusion.1, pred[3840]{0:T(1024)(128)(4,1)S(1)} %compare_and_fusion), kind=kLoop, calls=%fused_computation.30 | loop fusion | flops 6881280 | bytes 27528960 | tf_op jit(solution)/shard_map/jit(_take)/select_n | solution.py:120
  200.2 147.0 %while.12 = (s32[]{:T(128)}, f32[4,32,1024]{2,1,0:T(8,128)}, s32[4]{0:T(128)S(1)}, bf16[3840,1792]{1,0:T(8,128)(2,1)}, bf16[3840,1792]{1,0:T(8,128)(2,1)}, /*ind...) while((s32[]{:T(128)}, f32[4,32,1024]{2,1,0:T(8,128)}, ...), condition=%wide.region_6.7_spmd, body=%wide.region_3.6_spmd.sunk | while | flops 140954240 | bytes 39038152 | solution.py:133
  200.2 0.7 dynamic_slice.27
  201.6 0.1 dynamic_slice.28
  201.7 20.4 %multiply_subtract_fusion.2 = (f32[960,896]{1,0:T(8,128)}, f32[960,896]{1,0:T(8,128)S(1)}) fusion(s32[960]{0:T(1024)S(1)} %dynamic_slice.28, bf16[3840,1792]{1,0:T(8,128)(2,1)} %get-tuple-element.239, s32[]{:T(128)S(6)} %select_n.188, s32[]{:T(128)S(6)} %add.212, bf16[3840,1792]{1,0:T(8,128)(2,1)} %get-tuple-element.238), kind=kLoop, calls=%fused_computation.12.clone.1 | loop fusion | flops 21504000 | bytes 13766408 | tf_op jit(solution)/shard_map/while/body/eval_jaxpr/sub | solution.py:79
  222.1 4.4 %reshape.183 = f32[32,30,896]{2,1,0:T(8,128)} reshape(f32[960,896]{1,0:T(8,128)} %get-tuple-element.205) | data formatting | bytes 6881280 | tf_op jit(solution)/shard_map/while/body/eval_jaxpr/reshape | solution.py:82
  226.5 2.5 reduce_sum.48
  229.0 2.0 reshape.184
  231.0 2.5 reduce_sum.49
  233.5 3.4 fusion.56
  237.0 0.7 dynamic_slice.27
  238.4 0.1 dynamic_slice.28
  238.4 20.4 %multiply_subtract_fusion.2 = (f32[960,896]{1,0:T(8,128)}, f32[960,896]{1,0:T(8,128)S(1)}) fusion(s32[960]{0:T(1024)S(1)} %dynamic_slice.28, bf16[3840,1792]{1,0:T(8,128)(2,1)} %get-tuple-element.239, s32[]{:T(128)S(6)} %select_n.188, s32[]{:T(128)S(6)} %add.212, bf16[3840,1792]{1,0:T(8,128)(2,1)} %get-tuple-element.238), kind=kLoop, calls=%fused_computation.12.clone.1 | loop fusion | flops 21504000 | bytes 13766408 | tf_op jit(solution)/shard_map/while/body/eval_jaxpr/sub | solution.py:79
  258.9 4.4 %reshape.183 = f32[32,30,896]{2,1,0:T(8,128)} reshape(f32[960,896]{1,0:T(8,128)} %get-tuple-element.205) | data formatting | bytes 6881280 | tf_op jit(solution)/shard_map/while/body/eval_jaxpr/reshape | solution.py:82
  263.3 2.5 reduce_sum.48
  265.7 2.0 reshape.184
  267.7 2.5 reduce_sum.49
  270.3 3.4 fusion.56
  273.7 0.7 dynamic_slice.27
  275.1 0.1 dynamic_slice.28
  275.2 20.4 %multiply_subtract_fusion.2 = (f32[960,896]{1,0:T(8,128)}, f32[960,896]{1,0:T(8,128)S(1)}) fusion(s32[960]{0:T(1024)S(1)} %dynamic_slice.28, bf16[3840,1792]{1,0:T(8,128)(2,1)} %get-tuple-element.239, s32[]{:T(128)S(6)} %select_n.188, s32[]{:T(128)S(6)} %add.212, bf16[3840,1792]{1,0:T(8,128)(2,1)} %get-tuple-element.238), kind=kLoop, calls=%fused_computation.12.clone.1 | loop fusion | flops 21504000 | bytes 13766408 | tf_op jit(solution)/shard_map/while/body/eval_jaxpr/sub | solution.py:79
  295.6 4.4 %reshape.183 = f32[32,30,896]{2,1,0:T(8,128)} reshape(f32[960,896]{1,0:T(8,128)} %get-tuple-element.205) | data formatting | bytes 6881280 | tf_op jit(solution)/shard_map/while/body/eval_jaxpr/reshape | solution.py:82
  300.0 2.5 reduce_sum.48
  302.5 2.0 reshape.184
  304.5 2.5 reduce_sum.49
  307.0 3.4 fusion.56
  310.5 0.7 dynamic_slice.27
  311.9 0.1 dynamic_slice.28
  311.9 20.4 %multiply_subtract_fusion.2 = (f32[960,896]{1,0:T(8,128)}, f32[960,896]{1,0:T(8,128)S(1)}) fusion(s32[960]{0:T(1024)S(1)} %dynamic_slice.28, bf16[3840,1792]{1,0:T(8,128)(2,1)} %get-tuple-element.239, s32[]{:T(128)S(6)} %select_n.188, s32[]{:T(128)S(6)} %add.212, bf16[3840,1792]{1,0:T(8,128)(2,1)} %get-tuple-element.238), kind=kLoop, calls=%fused_computation.12.clone.1 | loop fusion | flops 21504000 | bytes 13766408 | tf_op jit(solution)/shard_map/while/body/eval_jaxpr/sub | solution.py:79
  332.4 4.4 %reshape.183 = f32[32,30,896]{2,1,0:T(8,128)} reshape(f32[960,896]{1,0:T(8,128)} %get-tuple-element.205) | data formatting | bytes 6881280 | tf_op jit(solution)/shard_map/while/body/eval_jaxpr/reshape | solution.py:82
  336.8 2.5 reduce_sum.48
  339.2 2.0 reshape.184
  341.2 2.5 reduce_sum.49
  343.8 3.4 fusion.56
  (74 shorter events, 0.5 us)
Async XLA Ops:
  8.4 35.6 %all-to-all-start = ((bf16[16,8,2048]{2,0,1:T(8,128)(2,1)}), bf16[16,8,2048]{2,0,1:T(8,128)(2,1)S(1)}, u32[]{:S(2)}, u32[]{:S(2)}) async-start(bf16[16,8,2048]{2,0,1:T(8,128)(2,1)} %bitcast.25), calls=%async_computation | async-start | bytes 1048576 | tf_op jit(solution)/shard_map/all_to_all | solution.py:97
  15.7 142.9 %all-gather.2.cloned.1.call-start = ((), (), s32[]{:S(2)}) async-start(), calls=%async_computation.1 | async-start | bytes 2293760 | tf_op jit(solution)/shard_map/all_gather | solution.py:109
  15.8 29.7 %copy-start.9 = (bf16[64]{0:T(256)(128)(2,1)S(1)}, bf16[64]{0:T(256)(128)(2,1)}, u32[]{:S(2)}) copy-start(bf16[64]{0:T(256)(128)(2,1)} %param.10) | copy-start | bytes 388
  44.1 13.2 %collective-permute-start = (bf16[128,1600]{1,0:T(8,128)(2,1)S(1)}, bf16[128,1600]{1,0:T(8,128)(2,1)S(1)}, u32[]{:S(2)}, u32[]{:S(2)}) collective-permute-start(bf16[128,1600]{1,0:T(8,128)(2,1)S(1)} %slice.48), channel_id=1, source_target_pairs={{4,0},{8,4},{12,8},{16,12},{20,16},{24,20},{28,24},{5,1},{9,5},{13... | collective-permute-start | bytes 1228808 | tf_op jit(solution)/shard_map/ppermute | solution.py:21
  58.7 1.9 copy-start
  58.7 2.9 copy-start.2
  61.6 1.9 copy-start.6
  61.6 2.3 copy-start.8
  61.6 2.4 copy-start.3
  72.9 7.1 %copy-start.1 = (bf16[1792,896]{1,0:T(8,128)(2,1)S(1)}, bf16[1792,896]{1,0:T(8,128)(2,1)}, u32[]{:S(2)}) copy-start(bf16[1792,896]{1,0:T(8,128)(2,1)} %get-tuple-element.154) | copy-start | bytes 9633796
  95.2 18.3 %copy-start.7 = (s32[128,30]{0,1:T(8,128)S(1)}, s32[128,30]{0,1:T(8,128)}, u32[]{:S(2)}) copy-start(s32[128,30]{0,1:T(8,128)} %param.13) | copy-start | bytes 46084
  200.2 1.5 copy-start.4
  200.2 1.5 copy-start.10
  231.0 6.0 %copy-start.5 = (s32[3840]{0:T(1024)S(1)}, s32[3840]{0:T(1024)}, u32[]{:S(2)}) copy-start(s32[3840]{0:T(1024)} %copy-done.4) | copy-start | bytes 46084 | tf_op jit(solution)/shard_map/while
  233.5 3.5 copy-start.11
  237.0 1.5 copy-start.4
  237.0 1.5 copy-start.10
  267.7 6.0 %copy-start.5 = (s32[3840]{0:T(1024)S(1)}, s32[3840]{0:T(1024)}, u32[]{:S(2)}) copy-start(s32[3840]{0:T(1024)} %copy-done.4) | copy-start | bytes 46084 | tf_op jit(solution)/shard_map/while
  270.3 3.5 copy-start.11
  273.7 1.5 copy-start.4
  273.7 1.5 copy-start.10
  304.5 6.0 %copy-start.5 = (s32[3840]{0:T(1024)S(1)}, s32[3840]{0:T(1024)}, u32[]{:S(2)}) copy-start(s32[3840]{0:T(1024)} %copy-done.4) | copy-start | bytes 46084 | tf_op jit(solution)/shard_map/while
  307.0 3.5 copy-start.11
  310.5 1.5 copy-start.4
  310.5 1.5 copy-start.10
  341.2 6.0 %copy-start.5 = (s32[3840]{0:T(1024)S(1)}, s32[3840]{0:T(1024)}, u32[]{:S(2)}) copy-start(s32[3840]{0:T(1024)} %copy-done.4) | copy-start | bytes 46084 | tf_op jit(solution)/shard_map/while
  343.8 3.5 copy-start.11
Sparse Core Ops, SparseCore 0:
  63.5 22.1 all-gather.1
where the time goes:
time: 356 us; the launch traced here: 354 us
  other arithmetic  169 us (47%)
  local copies, waits for them, and re-layouts  120 us (34%)
  matrix products  31.4 us (9%)
  between operations  13.6 us (4%)
  starting transfers between devices  8.61 us (2%)
  waiting for transfers between devices  8.12 us (2%)
    sub x4, other arithmetic, stack_block(): rotated_real = real_part * phase_cos - imag_part * phase_sin  81.6 us
    another operation x6, other arithmetic  44.1 us
    gather x1, local copies, waits for them, and re-layouts, on_device(): data_all = lax.optimization_barrier(jnp.take(gathered, data_rows, axis=0))  28.2 us
    gather x1, local copies, waits for them, and re-layouts, on_device(): data_rows = jnp.take(row_of, channels.reshape(-1))  22.9 us
    while x1, local copies, waits for them, and re-layouts, on_device(): result = lax.map(one_block, jnp.arange(count, dtype=jnp.int32))  18.3 us
    reshape x4, local copies, waits for them, and re-layouts, stack_block(): summed_real = jnp.sum(rotated_real.reshape(group, CH, NF), axis=1)  17.6 us
    dot_general x1, matrix products, on_device(): jnp.dot(flat_taps, head, preferred_element_type=jnp.float32)  15.3 us
    dot_general x4, matrix products, stack_block(): return jnp.dot(packed, inverse, preferred_element_type=jnp.float32)  13.8 us
  transfers between devices with their start and end apart: 3, of which 1 were waited for; matrix products, arithmetic and copies ran while one was open for 36% of the time, Pallas kernels for 0%

commit v1 on v0

v1 whole, which is shorter than its diff:
```python
import functools
import math

import jax
import jax.numpy as jnp
import ml_dtypes
import numpy as np
from jax import lax
from jax.experimental import pallas as pl
from jax.experimental.pallas import tpu as pltpu
from jax.sharding import PartitionSpec as P

WIN_DEV = 1024
TL = 400
CH = 30
DEC = 2
NTAP = 64
MOVE = 256
NS = 1792
NF = 896
LANE = 128
TILES = NF // LANE
BLOCK = 128
SPAN = 384
MIB = 2**20
BF16 = jnp.bfloat16
F32 = jnp.float32


def angles(rows, columns):
    step = np.float32(2.0 * math.pi / NS)
    turns = np.arange(rows)[:, None] * np.arange(columns)[None, :] % NS
    return (turns.astype(np.float32) * step).astype(np.float64)


def forward_table():
    angle = angles(NS, NF)
    return np.concatenate([np.cos(angle), np.sin(angle)], axis=1).astype(ml_dtypes.bfloat16)


def inverse_table():
    angle = angles(NF, WIN_DEV)
    return np.concatenate([np.cos(angle), -np.sin(angle)], axis=0).astype(ml_dtypes.bfloat16)


def phase_table():
    angle = angles(MOVE, NF)
    slab = np.zeros((MOVE, 16, LANE), np.float32)
    slab[:, :TILES] = np.cos(angle).reshape(MOVE, TILES, LANE)
    slab[:, 8 : 8 + TILES] = np.sin(angle).reshape(MOVE, TILES, LANE)
    return slab


def spectra_kernel(win_ref, raw_ref, fir_ref, table_hbm, *rest):
    win_count = (len(rest) - 4) if len(rest) > 4 else 0
    outs = rest[:win_count]
    table, filt, tile, sem = rest[win_count:]
    slots, raw_t = raw_ref.shape
    blocks = raw_t // (DEC * BLOCK)
    load = pltpu.make_async_copy(table_hbm, table, sem)
    load.start()
    spread = jnp.broadcast_to(fir_ref[...], (BLOCK, SPAN))
    band = pltpu.roll(spread, 0, 1, stride=DEC, stride_axis=0).astype(BF16)
    pieces = []
    for b in range(blocks):
        begin = b * DEC * BLOCK
        if begin + SPAN <= raw_t:
            pieces.append(raw_ref[:, begin : begin + SPAN])
        else:
            pad = jnp.zeros((slots, begin + SPAN - raw_t), BF16)
            pieces.append(jnp.concatenate([raw_ref[:, begin:raw_t], pad], axis=1))
    segments = jnp.concatenate(pieces, axis=0)
    result = lax.dot_general(segments, band, (((1,), (1,)), ((), ())), preferred_element_type=F32)
    filt[0 : blocks * slots] = result.astype(BF16)
    per_win = WIN_DEV // BLOCK
    per_tile = NS // BLOCK
    extra = per_tile - per_win
    filt[blocks * slots :] = jnp.zeros((extra * slots, BLOCK), BF16)
    for d in range(win_count):
        first = (win_ref[0] ^ d) * per_win
        for m in range(per_tile):
            start = pl.multiple_of((first + m) * slots, slots)
            tile[d * slots : (d + 1) * slots, m * BLOCK : (m + 1) * BLOCK] = filt[pl.ds(start, slots), :]
    values = tile[...].astype(F32)
    scale = lax.rsqrt(jnp.mean(values * values, axis=1, keepdims=True) + 1e-05)
    load.wait()
    spec = jnp.dot(tile[...], table[...], preferred_element_type=F32) * scale
    spec = spec.astype(BF16)
    for d in range(win_count):
        outs[d][...] = spec[d * slots : (d + 1) * slots]


def compact_kernel(ids_ref, *rest):
    blocks, out_ref = rest[:-1], rest[-1]
    rows = out_ref.shape[0]
    count = ids_ref.shape[1]
    live = ids_ref[...] >= 0
    above = lax.broadcasted_iota(jnp.int32, (count, count), 0) < lax.broadcasted_iota(
        jnp.int32, (count, count), 1
    )
    marks = jnp.broadcast_to(jnp.where(live, 1.0, 0.0), (16, count)).astype(BF16)
    rank = jnp.dot(marks, jnp.where(above, 1.0, 0.0).astype(BF16), preferred_element_type=F32)
    rank = jnp.where(live, rank[0:1], -1.0)
    wanted = lax.broadcasted_iota(jnp.int32, (rows, count), 0).astype(F32)
    pick = jnp.where(wanted == rank, 1.0, 0.0).astype(BF16)
    data = jnp.concatenate([block[...] for block in blocks], axis=0)
    out_ref[...] = jnp.dot(pick, data, preferred_element_type=F32).astype(BF16)


def template_kernel(sizes, shift_ref, ids_ref, place_ref, taps_ref, table_ref, phase_ref, u_ref, label_ref, flat):
    templates = taps_ref.shape[2]
    win_count, tmpl_count, slots, rows = sizes

    def channel(j, carry):
        wave = jnp.transpose(taps_ref[j])
        for m in range(TILES):
            part = jnp.dot(wave, table_ref[:, 2 * m * LANE : 2 * (m + 1) * LANE], preferred_element_type=F32)
            for g in range(templates // 8):
                for h in range(2):
                    at = (g * 2 * TILES + 2 * m + h) * 8
                    flat[at : at + 8, :] = part[g * 8 : (g + 1) * 8, h * LANE : (h + 1) * LANE]

        def eight(g, inner):
            for r in range(8):
                k = g * 8 + r
                at = g * (2 * TILES * 8) + r
                t_cos = flat[pl.ds(at, 8, stride=8), :]
                t_sin = flat[pl.ds(at + TILES * 8, 8, stride=8), :]
                shift = shift_ref[j, k]
                p_cos = phase_ref[shift, 0:8]
                p_sin = phase_ref[shift, 8:16]
                u_ref[k * CH + j, 0:8] = (t_cos * p_cos - t_sin * p_sin).astype(u_ref.dtype)
                u_ref[k * CH + j, 8:16] = (t_sin * p_cos + t_cos * p_sin).astype(u_ref.dtype)
            return inner

        return lax.fori_loop(0, templates // 8, eight, carry)

    lax.fori_loop(0, CH, channel, 0)

    def column(d, carry):
        def slot(q, count):
            owner = place_ref[0] ^ (q // slots)
            at = (owner * tmpl_count + (place_ref[1] ^ d)) * slots + q % slots
            label = ids_ref[at]
            label_ref[d * rows + jnp.minimum(count, rows - 1)] = label
            return count + (label >= 0).astype(jnp.int32)

        lax.fori_loop(0, win_count * slots, slot, 0)
        return carry

    lax.fori_loop(0, tmpl_count, column, 0)


def stack_kernel(live, chan_ref, label_ref, u_ref, inverse_hbm, *rest):
    pieces, (out_ref, inverse, flat, slabs, z, packed, sem) = rest[:-7], rest[-7:]
    templates = out_ref.shape[0]
    load = pltpu.make_async_copy(inverse_hbm, inverse, sem)
    load.start()
    rows = pieces[0].shape[0]
    for d, piece in enumerate(pieces):
        for g in range(rows // 16):
            for m in range(2 * TILES):
                value = piece[g * 16 : (g + 1) * 16, m * LANE : (m + 1) * LANE].astype(F32)
                for h in range(2):
                    at = ((2 * g + h) * 2 * TILES + m) * 8
                    flat[at : at + 8, :] = value[h * 8 : (h + 1) * 8]
        for r in range(live):
            at = (r // 8) * (2 * TILES * 8) + r % 8
            label = label_ref[d * rows + r]
            slabs[label, 0:8] = flat[pl.ds(at, 8, stride=8), :]
            slabs[label, 8:16] = flat[pl.ds(at + TILES * 8, 8, stride=8), :]

    step = 8

    def some(i, carry):
        for q in range(step):
            k = i * step + q
            real, imag = [None, None], [None, None]
            for j in range(CH):
                c = chan_ref[i * (step * 32) + (q * 32 + j)]
                u_cos = u_ref[k * CH + j, 0:8].astype(F32)
                u_sin = u_ref[k * CH + j, 8:16].astype(F32)
                x_cos = slabs[c, 0:8]
                x_sin = slabs[c, 8:16]
                re = u_cos * x_cos + u_sin * x_sin
                im = u_sin * x_cos - u_cos * x_sin
                p = j % 2
                real[p] = re if real[p] is None else real[p] + re
                imag[p] = im if imag[p] is None else imag[p] + im
            at = pl.multiple_of(k * 16, 16)
            z[pl.ds(at, 8), :] = real[0] + real[1]
            z[pl.ds(at + 8, 8), :] = imag[0] + imag[1]
        return carry

    lax.fori_loop(0, templates // step, some, 0)
    first = lax.broadcasted_iota(jnp.int32, (16, LANE), 1) == 0
    base = jnp.float32(CH * NS)
    for m in range(2 * TILES):
        row = m if m < TILES else m - TILES + 8
        weight = jnp.float32(2.0) / base
        if m % TILES == 0:
            weight = jnp.where(first, jnp.float32(1.0), jnp.float32(2.0)) / base
        for g in range(templates // 16):
            low = z[pl.ds(g * 256 + row, 8, stride=16), :]
            high = z[pl.ds(g * 256 + 128 + row, 8, stride=16), :]
            value = jnp.concatenate([low, high], axis=0) * weight
            packed[g * 16 : (g + 1) * 16, m * LANE : (m + 1) * LANE] = value.astype(BF16)
    load.wait()
    out_ref[...] = jnp.dot(packed[...], inverse[...], preferred_element_type=F32)


def full(space=pltpu.VMEM):
    return pl.BlockSpec(memory_space=space)


def on_device(raw, ids, fir, taps, channels, shifts):
    win_count = lax.axis_size("win")
    tmpl_count = lax.axis_size("tmpl")
    win = lax.axis_index("win")
    tmpl = lax.axis_index("tmpl")
    slots, raw_t = raw.shape
    templates = taps.shape[0]
    live = 3 * slots * win_count // 5
    rows = -(-live // 16) * 16
    chan_total = live * tmpl_count
    table = jnp.asarray(forward_table())
    inverse = jnp.asarray(inverse_table())
    phase = jnp.asarray(phase_table())

    blocks = raw_t // (DEC * BLOCK)
    fir_row = jnp.pad(fir.astype(F32), (0, SPAN - NTAP))[None, :]
    extra = (NS - WIN_DEV) // BLOCK
    mine = pl.pallas_call(
        spectra_kernel,
        out_shape=[jax.ShapeDtypeStruct((slots, NS), BF16)] * win_count,
        in_specs=[full(pltpu.SMEM), full(), full(), full(pl.ANY)],
        out_specs=[full()] * win_count,
        scratch_shapes=[
            pltpu.VMEM((NS, 2 * NF), BF16),
            pltpu.VMEM(((blocks + extra) * slots, BLOCK), BF16),
            pltpu.VMEM((win_count * slots, NS), BF16),
            pltpu.SemaphoreType.DMA,
        ],
        compiler_params=pltpu.CompilerParams(vmem_limit_bytes=20 * MIB),
        name="spectra",
    )(win.reshape(1), raw, fir_row, table)

    parts = [mine[0]]
    for d in range(1, win_count):
        parts.append(lax.ppermute(mine[d], "win", [(i, i ^ d) for i in range(win_count)]))

    grid = ids.reshape(win_count, tmpl_count, slots)
    owners = win ^ jnp.arange(win_count, dtype=jnp.int32)
    column = jnp.take(lax.dynamic_index_in_dim(grid, tmpl, 1, keepdims=False), owners, axis=0)
    packed_rows = pl.pallas_call(
        compact_kernel,
        out_shape=jax.ShapeDtypeStruct((rows, NS), BF16),
        in_specs=[full()] * (1 + win_count),
        out_specs=full(),
        compiler_params=pltpu.CompilerParams(vmem_limit_bytes=20 * MIB),
        name="compact",
    )(column.reshape(1, win_count * slots), *parts)

    held = {0: packed_rows}
    bit = tmpl_count // 2
    while bit:
        for d in list(held):
            held[d | bit] = lax.ppermute(held[d], "tmpl", [(i, i ^ bit) for i in range(tmpl_count)])
        bit //= 2
    pieces = [held[d] for d in range(tmpl_count)]

    slab_type = F32 if chan_total <= 1024 else BF16
    sizes = (win_count, tmpl_count, slots, rows)
    place = jnp.stack([win, tmpl]).astype(jnp.int32)
    slabs, labels = pl.pallas_call(
        functools.partial(template_kernel, sizes),
        out_shape=[
            pltpu.VMEM((templates * CH, 16, LANE), slab_type),
            jax.ShapeDtypeStruct((tmpl_count * rows,), jnp.int32),
        ],
        in_specs=[full(pltpu.SMEM)] * 3 + [full()] * 3,
        out_specs=[full(), full(pltpu.SMEM)],
        scratch_shapes=[pltpu.VMEM((templates // 8 * 2 * TILES * 8 + 64, LANE), F32)],
        compiler_params=pltpu.CompilerParams(vmem_limit_bytes=16 * MIB),
        name="templates",
    )(shifts.T, ids, place, taps.transpose(1, 2, 0), table[:TL], phase)

    slabs = pltpu.with_memory_space_constraint(slabs, pltpu.VMEM)
    chan = jnp.pad(channels, ((0, 0), (0, 32 - CH))).reshape(-1)
    return pl.pallas_call(
        functools.partial(stack_kernel, live),
        out_shape=jax.ShapeDtypeStruct((templates, WIN_DEV), F32),
        in_specs=[full(pltpu.SMEM)] * 2 + [full(), full(pl.ANY)] + [full()] * tmpl_count,
        out_specs=full(),
        scratch_shapes=[
            pltpu.VMEM((2 * NF, WIN_DEV), BF16),
            pltpu.VMEM((rows * 2 * TILES + 64, LANE), F32),
            pltpu.VMEM((chan_total, 16, LANE), F32),
            pltpu.VMEM((templates * 16, LANE), F32),
            pltpu.VMEM((templates, NS), BF16),
            pltpu.SemaphoreType.DMA,
        ],
        compiler_params=pltpu.CompilerParams(vmem_limit_bytes=(20 if slab_type == F32 else 42) * MIB),
        name="stacks",
    )(chan, labels, slabs, inverse, *pieces)


def solution(mesh):
    return jax.shard_map(
        on_device,
        mesh=mesh,
        in_specs=(
            P(("win", "tmpl"), None),
            P(),
            P(),
            P("tmpl", None, None),
            P("tmpl", None),
            P("tmpl", None),
        ),
        out_specs=P("tmpl", "win"),
        check_vma=False,
    )
```

time: 356 us -> 113 us (0.32)
  other arithmetic: 169 us -> 2.69 us
  local copies, waits for them, and re-layouts: 120 us -> 39.3 us
  Pallas kernels: 0 us -> 47.9 us
  matrix products: 31.4 us -> 0 us
  between operations: 13.6 us -> 0.09 us
  starting transfers between devices: 8.61 us -> 14.1 us
    sub x5 -> x0, other arithmetic: 81.6 us -> none  [the longest x4 81.6 us: stack_block(): rotated_real = real_part * phase_cos - imag_part * phase_sin]
    gather x2 -> x1, local copies, waits for them, and re-layouts: 51 us -> 1.26 us  [on_device(): jnp.take(lax.dynamic_index_in_dim(grid, tmpl, 1, keepdims=False), owners,...]
    pallas_call x0 -> x4, Pallas kernels: none -> 47.9 us  [the longest x1 36.2 us: on_device(): pl.pallas_call(functools.partial(template_kernel, sizes), out_shape=[pltp...]
    another operation x6 -> x1, other arithmetic: 44.1 us -> 0.08 us  [on_device(): place = jnp.stack([win, tmpl]).astype(jnp.int32)]
    reshape x13 -> x2, local copies, waits for them, and re-layouts: 33.1 us -> 0.77 us  [the longest x1 0.69 us: on_device(): grid = ids.reshape(win_count, tmpl_count, slots)]
    dot_general x7 -> x0, matrix products: 31.4 us -> none  [the longest x1 15.3 us: on_device(): jnp.dot(flat_taps, head, preferred_element_type=jnp.float32)]
    reduce_sum x9 -> x0, other arithmetic: 23.7 us -> none  [the longest x4 9.98 us: stack_block(): summed_imag = jnp.sum(rotated_imag.reshape(group, CH, NF), axis=1)]
    unnamed x20 -> x41, local copies, waits for them, and re-layouts: 12.5 us -> 35.7 us
  transfers between devices with their start and end apart: 3 -> 10, of which waited for: 1 -> 2; matrix products, arithmetic and copies ran while one was open for 36% -> 6% of each run, Pallas kernels for 0% -> 32%
where the time goes in v1:
time: 113 us; the launch traced here: 112 us
  Pallas kernels  47.9 us (42%)
  local copies, waits for them, and re-layouts  39.3 us (35%)
  starting transfers between devices  14.1 us (12%)
  waiting for transfers between devices  7.73 us (7%)
  other arithmetic  2.69 us (2%)
    pallas_call x1, Pallas kernels, on_device(): pl.pallas_call(functools.partial(template_kernel, sizes), out_shape=[pltp...  36.2 us
    unnamed x41, local copies, waits for them, and re-layouts  35.7 us
    ppermute x7, starting transfers between devices, on_device(): lax.ppermute(mine[d], 'win', [(i, i ^ d) for i in range(win_count)])  12.5 us
    pallas_call x1, Pallas kernels, on_device(): pl.pallas_call(functools.partial(stack_kernel, live), out_shape=jax.Shape...  8.15 us
    ppermute x3, waiting for transfers between devices, on_device(): lax.ppermute(held[d], 'tmpl', [(i, i ^ bit) for i in range(tmpl_count)])  5.24 us
    pallas_call x1, Pallas kernels, on_device(): pl.pallas_call(spectra_kernel, out_shape=[jax.ShapeDtypeStruct((slots, NS...  3.19 us
    ppermute x7, waiting for transfers between devices, on_device(): lax.ppermute(mine[d], 'win', [(i, i ^ d) for i in range(win_count)])  2.49 us
  transfers between devices with their start and end apart: 10, of which 2 were waited for; matrix products, arithmetic and copies ran while one was open for 6% of the time, Pallas kernels for 32%

profile of v1, /device:TPU:0, one launch (start us, length us, event | category | flops | bytes accessed | tf_op | source)
XLA Modules:
  0.0 111.7 jit_solution(4377849298544763839)
XLA Ops:
  0.0 0.0 copy-start.18
  0.0 0.7 pad_convert_fusion
  0.7 0.0 copy-start.2
  0.7 2.8 %copy-done.2 = bf16[1792,1792]{1,0:T(8,128)(2,1)S(1)} copy-done((bf16[1792,1792]{1,0:T(8,128)(2,1)S(1)}, bf16[1792,1792]{1,0:T(8,128)(2,1)}, u32[]{:S(2)}) %copy-start.2) | copy-done | bytes 6422552
  3.5 0.0 copy-start.6
  3.5 1.0 copy-done.6
  4.5 0.0 copy-start.3
  4.5 0.0 copy-start.17
  4.5 3.2 %spectra.1 = (bf16[16,1792]{1,0:T(8,128)(2,1)S(1)}, bf16[16,1792]{1,0:T(8,128)(2,1)S(1)}, bf16[16,1792]{1,0:T(8,128)(2,1)S(1)}, bf16[16,1792]{1,0:T(8,128)(2,1)}...) custom-call(s32[1]{0:T(128)} %bitcast.1.win_ref, ...), custom_call_target="tpu_custom_call" | custom-call | tf_op jit(solution)/shard_map/spectra/pallas_call | solution.py:233
  7.7 0.0 copy-start.19
  7.8 0.6 copy-done.19
  8.4 3.0 %collective-permute-start = (bf16[16,1792]{1,0:T(8,128)(2,1)S(1)}, bf16[16,1792]{1,0:T(8,128)(2,1)S(1)}, u32[]{:S(2)}, u32[]{:S(2)}) collective-permute-start(bf16[16,1792]{1,0:T(8,128)(2,1)S(1)} %get-tuple-element.18), channel_id=1, source_target_pairs={{0,4},{4,0},{8,12},{12,8},{16,20},{20,16},{24,28},{28,24},{1,5},{5... | collective-permute-start | bytes 172040 | tf_op jit(solution)/shard_map/ppermute | solution.py:250
  11.3 1.6 %collective-permute-start.1 = (bf16[16,1792]{1,0:T(8,128)(2,1)S(1)}, bf16[16,1792]{1,0:T(8,128)(2,1)S(1)}, u32[]{:S(2)}, u32[]{:S(2)}) collective-permute-start(bf16[16,1792]{1,0:T(8,128)(2,1)S(1)} %get-tuple-element.19), channel_id=1, source_target_pairs={{0,8},{4,12},{8,0},{12,4},{16,24},{20,28},{24,16},{28,20},{1,9},{5... | collective-permute-start | bytes 172040 | tf_op jit(solution)/shard_map/ppermute | solution.py:250
  12.9 0.0 collective-permute-start.2
  12.9 3.0 %collective-permute-start.3 = (bf16[16,1792]{1,0:T(8,128)(2,1)}, bf16[16,1792]{1,0:T(8,128)(2,1)S(1)}, u32[]{:S(2)}, u32[]{:S(2)}) collective-permute-start(bf16[16,1792]{1,0:T(8,128)(2,1)} %get-tuple-element.21), channel_id=1, source_target_pairs={{0,16},{4,20},{8,24},{12,28},{16,0},{20,4},{24,8},{28,12},{1,17},{... | collective-permute-start | bytes 172040 | tf_op jit(solution)/shard_map/ppermute | solution.py:250
  15.9 1.3 %collective-permute-start.4 = (bf16[16,1792]{1,0:T(8,128)(2,1)}, bf16[16,1792]{1,0:T(8,128)(2,1)S(1)}, u32[]{:S(2)}, u32[]{:S(2)}) collective-permute-start(bf16[16,1792]{1,0:T(8,128)(2,1)} %get-tuple-element.22), channel_id=1, source_target_pairs={{0,20},{4,16},{8,28},{12,24},{16,4},{20,0},{24,12},{28,8},{1,21},{... | collective-permute-start | bytes 172040 | tf_op jit(solution)/shard_map/ppermute | solution.py:250
  17.2 0.6 pad_clamp_fusion
  17.8 0.0 copy-done.18
  17.8 0.7 reshape.51
  18.5 0.7 constant_dynamic-slice_fusion
  19.2 1.3 %gather_fusion = s32[8,16]{1,0:T(8,128)} fusion(s32[8,16]{1,0:T(8,128)S(1)} %bitcast.9, s32[1024]{0:T(1024)} %pad_clamp_fusion), kind=kCustom, calls=%fused_computation | custom fusion | bytes 1056 | tf_op jit(solution)/shard_map/jit(_take)/gather | solution.py:254
  20.5 0.0 collective-permute-done.rest_1_
  20.5 3.7 %collective-permute-start.5 = (bf16[16,1792]{1,0:T(8,128)(2,1)}, bf16[16,1792]{1,0:T(8,128)(2,1)S(1)}, u32[]{:S(2)}, u32[]{:S(2)}) collective-permute-start(bf16[16,1792]{1,0:T(8,128)(2,1)} %get-tuple-element.23), channel_id=1, source_target_pairs={{0,24},{4,28},{8,16},{12,20},{16,8},{20,12},{24,0},{28,4},{1,25},{... | collective-permute-start | bytes 172040 | tf_op jit(solution)/shard_map/ppermute | solution.py:250
  24.1 0.0 collective-permute-done.1.rest_2_
  24.1 0.0 collective-permute-start.6
  24.2 1.3 %broadcast_select_fusion = s32[8,16]{1,0:T(8,128)} fusion(s32[8,16]{1,0:T(8,128)} %gather_fusion, pred[8]{0:T(512)(128)(4,1)S(1)} %compare_and_fusion), kind=kLoop, calls=%fused_computation.4 | loop fusion | flops 128 | bytes 1032 | tf_op jit(solution)/shard_map/jit(_take)/select_n | solution.py:254
  25.5 0.8 select_n.38.ids_ref
  26.2 0.0 collective-permute-done.2.rest_3_
  26.3 0.0 copy-start.7
  26.3 0.6 copy-done.7
  26.9 0.0 collective-permute-done.3.rest_4_
  26.9 0.0 copy-start.9
  26.9 0.6 copy-done.9
  27.5 0.0 collective-permute-done.4.rest_5_
  27.5 0.0 copy-start.11
  27.5 0.6 copy-done.11
  28.1 0.0 collective-permute-done.5.rest_6_
  28.1 0.6 copy-done.13
  28.7 2.5 %collective-permute-done.6.rest_7_ = bf16[16,1792]{1,0:T(8,128)(2,1)S(1)} collective-permute-done((bf16[16,1792]{1,0:T(8,128)(2,1)}, bf16[16,1792]{1,0:T(8,128)(2,1)S(1)}, u32[]{:S(2)}, u32[]{:S(2)}) %collective-permute-start.6) | collective-permute-done | bytes 57376 | tf_op jit(solution)/shard_map/ppermute | solution.py:250
  31.2 0.6 copy-done.15
  31.8 0.8 copy-done.8
  32.7 0.8 copy-done.10
  33.5 0.8 copy-done.12
  34.3 0.8 copy-done.14
  35.1 0.8 copy-done.16
  35.9 0.3 compact.1.rest_0_
  36.3 1.6 %collective-permute-start.8 = (bf16[80,1792]{1,0:T(8,128)(2,1)S(1)}, bf16[80,1792]{1,0:T(8,128)(2,1)}, u32[]{:S(2)}, u32[]{:S(2)}) collective-permute-start(bf16[80,1792]{1,0:T(8,128)(2,1)S(1)} %compact.1.rest_0_), channel_id=1, source_target_pairs={{0,2},{1,3},{2,0},{3,1},{4,6},{5,7},{6,4},{7,5},{8,10},{9,11},{10,... | collective-permute-start | bytes 860168 | tf_op jit(solution)/shard_map/ppermute | solution.py:268
  37.9 0.0 collective-permute-start.7
  37.9 5.2 %collective-permute-done.8.rest_2_ = bf16[80,1792]{1,0:T(8,128)(2,1)} collective-permute-done((bf16[80,1792]{1,0:T(8,128)(2,1)S(1)}, bf16[80,1792]{1,0:T(8,128)(2,1)}, u32[]{:S(2)}, u32[]{:S(2)}) %collective-permute-start.8) | collective-permute-done | bytes 286752 | tf_op jit(solution)/shard_map/ppermute | solution.py:268
  43.1 0.0 collective-permute-start.9
  43.1 0.8 copy.11
  43.9 0.1 reshape.50.chan_ref
  44.0 0.1 pad_add_fusion.place_ref
  44.1 0.0 copy-done.3
  44.1 0.0 copy-done.17
  44.1 1.6 %copy-done.4 = f32[256,16,128]{2,1,0:T(8,128)S(1)} copy-done((f32[256,16,128]{2,1,0:T(8,128)S(1)}, f32[256,16,128]{2,1,0:T(8,128)}, u32[]{:S(2)}) %copy-start.4) | copy-done | bytes 2097176
  45.7 1.4 %copy-done.5 = bf16[400,1792]{1,0:T(8,128)(2,1)S(1)} copy-done((bf16[400,1792]{1,0:T(8,128)(2,1)S(1)}, bf16[400,1792]{1,0:T(8,128)(2,1)}, u32[]{:S(2)}) %copy-start.5) | copy-done | bytes 1433624
  47.0 36.2 %templates.1 = (f32[3840,16,128]{2,1,0:T(8,128)S(1)}, s32[320]{0:T(512)S(1)}) custom-call(s32[30,128]{1,0:T(8,128)S(1)} %bitcast.8, s32[512]{0:T(512)S(1)} %copy-done.18, s32[2]{0:T(128)S(1)} %pad_add_fusion.place_ref, bf16[30,400,128]{2,1,0:T(8,128)(2,1)S(1)} %bitcast.7, bf16[400,1792]{1,0:T(8,128)(2,1)S(1)} %copy-done.5, f32[256,16,128]{2,1,0:T(8,128)S(1)} %copy-done.4), custom_call_target="tpu_custom_call" | custom-call | tf_op jit(solution)/shard_map/templates/pallas_call | solution.py:275
  83.2 0.0 copy-start
  83.3 10.4 %copy-done = f32[3840,16,128]{2,1,0:T(8,128)} copy-done((f32[3840,16,128]{2,1,0:T(8,128)}, f32[3840,16,128]{2,1,0:T(8,128)S(1)}, u32[]{:S(2)}) %copy-start) | copy-done | bytes 31457304
  93.6 0.0 collective-permute-done.7.rest_1_
  93.6 0.0 collective-permute-done.9.rest_3_
  93.6 9.9 %copy-done.1 = f32[3840,16,128]{2,1,0:T(8,128)S(1)} copy-done((f32[3840,16,128]{2,1,0:T(8,128)S(1)}, f32[3840,16,128]{2,1,0:T(8,128)}, u32[]{:S(2)}) %copy-start.1) | copy-done | bytes 31457304
  103.6 8.2 %stacks.1 = f32[128,1024]{1,0:T(8,128)} custom-call(s32[4096]{0:T(1024)S(1)} %reshape.50.chan_ref, s32[320]{0:T(512)S(1)} %get-tuple-element.15.label_ref, f32[3840,16,128]{2,1,0:T(8,128)S(1)} %copy-done.1, bf16[1792,1024]{1,0:T(8,128)(2,1)} %constant.41.clone.inverse_hbm, bf16[80,1792]{1,0:T(8,128)(2,1)S(1)} %compact.1.rest_0_, ...), custom_call_target="tpu_custom_call" | custom-call | tf_op jit(solution)/shard_map/stacks/pallas_call | solution.py:290
  (14 shorter events, 0.0 us)
Async XLA Ops:
  0.0 17.8 %copy-start.18 = (s32[512]{0:T(512)S(1)}, s32[512]{0:T(512)}, u32[]{:S(2)}) copy-start(s32[512]{0:T(512)} %ids_ref.1) | copy-start | bytes 6148
  0.7 2.8 %copy-start.2 = (bf16[1792,1792]{1,0:T(8,128)(2,1)S(1)}, bf16[1792,1792]{1,0:T(8,128)(2,1)}, u32[]{:S(2)}) copy-start(bf16[1792,1792]{1,0:T(8,128)(2,1)} %constant.40.clone.table_hbm) | copy-start | bytes 19267588
  3.5 1.0 copy-start.6
  4.5 39.5 %copy-start.3 = (bf16[128,30,400]{0,2,1:T(8,128)(2,1)S(1)}, bf16[128,30,400]{0,2,1:T(8,128)(2,1)}, u32[]{:S(2)}) copy-start(bf16[128,30,400]{0,2,1:T(8,128)(2,1)} %param.12) | copy-start | bytes 9216004
  4.5 39.5 %copy-start.17 = (s32[128,30]{0,1:T(8,128)S(1)}, s32[128,30]{0,1:T(8,128)}, u32[]{:S(2)}) copy-start(s32[128,30]{0,1:T(8,128)} %param.14) | copy-start | bytes 46084
  7.7 0.6 copy-start.19
  8.4 12.1 %collective-permute-start = (bf16[16,1792]{1,0:T(8,128)(2,1)S(1)}, bf16[16,1792]{1,0:T(8,128)(2,1)S(1)}, u32[]{:S(2)}, u32[]{:S(2)}) collective-permute-start(bf16[16,1792]{1,0:T(8,128)(2,1)S(1)} %get-tuple-element.18), channel_id=1, source_target_pairs={{0,4},{4,0},{8,12},{12,8},{16,20},{20,16},{24,28},{28,24},{1,5},{5... | collective-permute-start | bytes 172040 | tf_op jit(solution)/shard_map/ppermute | solution.py:250
  11.3 12.8 %collective-permute-start.1 = (bf16[16,1792]{1,0:T(8,128)(2,1)S(1)}, bf16[16,1792]{1,0:T(8,128)(2,1)S(1)}, u32[]{:S(2)}, u32[]{:S(2)}) collective-permute-start(bf16[16,1792]{1,0:T(8,128)(2,1)S(1)} %get-tuple-element.19), channel_id=1, source_target_pairs={{0,8},{4,12},{8,0},{12,4},{16,24},{20,28},{24,16},{28,20},{1,9},{5... | collective-permute-start | bytes 172040 | tf_op jit(solution)/shard_map/ppermute | solution.py:250
  12.9 13.3 %collective-permute-start.2 = (bf16[16,1792]{1,0:T(8,128)(2,1)}, bf16[16,1792]{1,0:T(8,128)(2,1)S(1)}, u32[]{:S(2)}, u32[]{:S(2)}) collective-permute-start(bf16[16,1792]{1,0:T(8,128)(2,1)} %get-tuple-element.20), channel_id=1, source_target_pairs={{0,12},{4,8},{8,4},{12,0},{16,28},{20,24},{24,20},{28,16},{1,13},{... | collective-permute-start | bytes 172040 | tf_op jit(solution)/shard_map/ppermute | solution.py:250
  12.9 14.0 %collective-permute-start.3 = (bf16[16,1792]{1,0:T(8,128)(2,1)}, bf16[16,1792]{1,0:T(8,128)(2,1)S(1)}, u32[]{:S(2)}, u32[]{:S(2)}) collective-permute-start(bf16[16,1792]{1,0:T(8,128)(2,1)} %get-tuple-element.21), channel_id=1, source_target_pairs={{0,16},{4,20},{8,24},{12,28},{16,0},{20,4},{24,8},{28,12},{1,17},{... | collective-permute-start | bytes 172040 | tf_op jit(solution)/shard_map/ppermute | solution.py:250
  15.9 11.6 %collective-permute-start.4 = (bf16[16,1792]{1,0:T(8,128)(2,1)}, bf16[16,1792]{1,0:T(8,128)(2,1)S(1)}, u32[]{:S(2)}, u32[]{:S(2)}) collective-permute-start(bf16[16,1792]{1,0:T(8,128)(2,1)} %get-tuple-element.22), channel_id=1, source_target_pairs={{0,20},{4,16},{8,28},{12,24},{16,4},{20,0},{24,12},{28,8},{1,21},{... | collective-permute-start | bytes 172040 | tf_op jit(solution)/shard_map/ppermute | solution.py:250
  20.5 7.7 %collective-permute-start.5 = (bf16[16,1792]{1,0:T(8,128)(2,1)}, bf16[16,1792]{1,0:T(8,128)(2,1)S(1)}, u32[]{:S(2)}, u32[]{:S(2)}) collective-permute-start(bf16[16,1792]{1,0:T(8,128)(2,1)} %get-tuple-element.23), channel_id=1, source_target_pairs={{0,24},{4,28},{8,16},{12,20},{16,8},{20,12},{24,0},{28,4},{1,25},{... | collective-permute-start | bytes 172040 | tf_op jit(solution)/shard_map/ppermute | solution.py:250
  24.1 7.1 %collective-permute-start.6 = (bf16[16,1792]{1,0:T(8,128)(2,1)}, bf16[16,1792]{1,0:T(8,128)(2,1)S(1)}, u32[]{:S(2)}, u32[]{:S(2)}) collective-permute-start(bf16[16,1792]{1,0:T(8,128)(2,1)} %copy-done.19), channel_id=1, source_target_pairs={{0,28},{4,24},{8,20},{12,16},{16,12},{20,8},{24,4},{28,0},{1,29},{... | collective-permute-start | bytes 172040 | tf_op jit(solution)/shard_map/ppermute | solution.py:250
  26.3 0.6 copy-start.7
  26.9 0.6 copy-start.9
  27.5 0.6 copy-start.11
  28.1 0.6 copy-start.13
  31.2 0.6 copy-start.15
  31.8 0.8 copy-start.8
  32.7 0.8 copy-start.10
  33.5 0.8 copy-start.12
  34.3 0.8 copy-start.14
  35.1 0.8 copy-start.16
  36.3 6.8 %collective-permute-start.8 = (bf16[80,1792]{1,0:T(8,128)(2,1)S(1)}, bf16[80,1792]{1,0:T(8,128)(2,1)}, u32[]{:S(2)}, u32[]{:S(2)}) collective-permute-start(bf16[80,1792]{1,0:T(8,128)(2,1)S(1)} %compact.1.rest_0_), channel_id=1, source_target_pairs={{0,2},{1,3},{2,0},{3,1},{4,6},{5,7},{6,4},{7,5},{8,10},{9,11},{10,... | collective-permute-start | bytes 860168 | tf_op jit(solution)/shard_map/ppermute | solution.py:268
  37.9 55.8 %collective-permute-start.7 = (bf16[80,1792]{1,0:T(8,128)(2,1)S(1)}, bf16[80,1792]{1,0:T(8,128)(2,1)}, u32[]{:S(2)}, u32[]{:S(2)}) collective-permute-start(bf16[80,1792]{1,0:T(8,128)(2,1)S(1)} %compact.1.rest_0_), channel_id=1, source_target_pairs={{0,1},{1,0},{2,3},{3,2},{4,5},{5,4},{6,7},{7,6},{8,9},{9,8},{10,11... | collective-permute-start | bytes 860168 | tf_op jit(solution)/shard_map/ppermute | solution.py:268
  43.1 50.5 %collective-permute-start.9 = (bf16[80,1792]{1,0:T(8,128)(2,1)}, bf16[80,1792]{1,0:T(8,128)(2,1)}, u32[]{:S(2)}, u32[]{:S(2)}) collective-permute-start(bf16[80,1792]{1,0:T(8,128)(2,1)} %collective-permute-done.8.rest_2_), channel_id=1, source_target_pairs={{0,1},{1,0},{2,3},{3,2},{4,5},{5,4},{6,7},{7,6},{8,9},{9,8},{10,11... | collective-permute-start | bytes 860168 | tf_op jit(solution)/shard_map/ppermute | solution.py:268
  44.1 1.6 %copy-start.4 = (f32[256,16,128]{2,1,0:T(8,128)S(1)}, f32[256,16,128]{2,1,0:T(8,128)}, u32[]{:S(2)}) copy-start(f32[256,16,128]{2,1,0:T(8,128)} %constant.42.clone.phase_ref) | copy-start | bytes 6291460
  45.7 1.4 %copy-start.5 = (bf16[400,1792]{1,0:T(8,128)(2,1)S(1)}, bf16[400,1792]{1,0:T(8,128)(2,1)}, u32[]{:S(2)}) copy-start(bf16[400,1792]{1,0:T(8,128)(2,1)} %constant.48.table_ref) | copy-start | bytes 4300804
  83.2 10.4 %copy-start = (f32[3840,16,128]{2,1,0:T(8,128)}, f32[3840,16,128]{2,1,0:T(8,128)S(1)}, u32[]{:S(2)}) copy-start(f32[3840,16,128]{2,1,0:T(8,128)S(1)} %get-tuple-element.16.u_ref) | copy-start | bytes 94371840
  93.6 9.9 %copy-start.1 = (f32[3840,16,128]{2,1,0:T(8,128)S(1)}, f32[3840,16,128]{2,1,0:T(8,128)}, u32[]{:S(2)}) copy-start(f32[3840,16,128]{2,1,0:T(8,128)} %copy-done) | copy-start | bytes 94371840

commit v2 on v1

v2 whole, which is shorter than its diff:
```python
import functools
import math

import jax
import jax.numpy as jnp
import ml_dtypes
import numpy as np
from jax import lax
from jax.experimental import pallas as pl
from jax.experimental.pallas import tpu as pltpu
from jax.sharding import PartitionSpec as P

WIN_DEV = 1024
TL = 400
CH = 30
DEC = 2
NTAP = 64
MOVE = 256
NS = 1792
NF = 896
LANE = 128
TILES = NF // LANE
BLOCK = 256
SPAN = 640
PITCH = 2 * TILES
MIB = 2**20
BF16 = jnp.bfloat16
F32 = jnp.float32


def angles(rows, columns):
    step = np.float32(2.0 * math.pi / NS)
    turns = np.arange(rows)[:, None] * np.arange(columns)[None, :] % NS
    return (turns.astype(np.float32) * step).astype(np.float64)


def order():
    low = np.arange(3 * LANE)
    high = NF - low
    high[0] = NF // 2
    rest = np.arange(3 * LANE, NF // 2)
    return np.concatenate([low, high, rest, NF - rest])


def forward_tables():
    angle = angles(NS, NF)
    cosine, sine = np.cos(angle), np.sin(angle)
    full = 3 * LANE
    half = NF // 2
    columns = [cosine[:, :full], sine[:, :full], cosine[:, full:half], sine[:, full:half]]
    table = np.concatenate(columns, axis=1)
    even, odd = table[0::2].copy(), table[1::2].copy()
    even[:, full] = cosine[0::2, half]
    odd[:, full] = sine[1::2, half]
    return np.stack([even, odd]).astype(ml_dtypes.bfloat16)


def inverse_table():
    angle = angles(NF, WIN_DEV)[order()]
    return np.concatenate([np.cos(angle), -np.sin(angle)], axis=0).astype(ml_dtypes.bfloat16)


def phase_table():
    angle = angles(MOVE, NF)[:, order()]
    slab = np.zeros((MOVE, 16, LANE), np.float32)
    slab[:, :TILES] = np.cos(angle).reshape(MOVE, TILES, LANE)
    slab[:, 8 : 8 + TILES] = np.sin(angle).reshape(MOVE, TILES, LANE)
    return slab


def tile_of(array, column):
    return array[:, column * LANE : (column + 1) * LANE]


def butterfly(even, odd):
    low = [tile_of(even, c) + tile_of(odd, c) for c in range(TILES)]
    lane = lax.broadcasted_iota(jnp.int32, low[0].shape, 1)
    first, left = lane == 0, lane < LANE // 2
    high_cos = [tile_of(even, c) - tile_of(odd, c) for c in range(3)]
    high_sin = [tile_of(odd, 3 + c) - tile_of(even, 3 + c) for c in range(3)]
    high_cos[0] = jnp.where(first, tile_of(even, 3), high_cos[0])
    high_sin[0] = jnp.where(first, tile_of(odd, 3), high_sin[0])
    low_sin = low[3:6]
    low_sin[0] = jnp.where(first, 0.0, low_sin[0])
    gap = tile_of(even, 6) - tile_of(odd, 6)
    mixed_cos = jnp.where(left, low[6], pltpu.roll(gap, LANE // 2, 1))
    mixed_sin = jnp.where(left, pltpu.roll(low[6], LANE // 2, 1), -gap)
    return low[0:3] + high_cos + [mixed_cos] + low_sin + high_sin + [mixed_sin]


def spectra_kernel(place_ref, raw_hbm, fir_hbm, table_hbm, *rest):
    win_count = len(rest) - 6
    outs = rest[:win_count]
    raw, fir, table, filt, tile, sems = rest[win_count:]
    slots, raw_t = raw_hbm.shape
    length = DEC * BLOCK
    blocks = raw_t // length
    raw_copy = pltpu.make_async_copy(raw_hbm, raw.at[:, 0:raw_t], sems.at[0])
    raw_copy.start()
    fir_copy = pltpu.make_async_copy(fir_hbm, fir, sems.at[1])
    fir_copy.start()
    loads = [pltpu.make_async_copy(table_hbm.at[p], table.at[p], sems.at[2 + p]) for p in range(2)]
    for load in loads:
        load.start()
    raw[:, raw_t:] = jnp.zeros((slots, SPAN - length), BF16)
    fir_copy.wait()
    taps = jnp.concatenate([fir[...].astype(F32), jnp.zeros((1, SPAN - NTAP), F32)], axis=1)
    spread = jnp.broadcast_to(taps, (BLOCK // 2, SPAN))
    even = pltpu.roll(spread, 0, 1, stride=2 * DEC, stride_axis=0)
    odd = pltpu.roll(spread, DEC, 1, stride=2 * DEC, stride_axis=0)
    band = jnp.concatenate([even, odd], axis=0).astype(BF16)
    raw_copy.wait()
    segments = jnp.concatenate([raw[:, b * length : b * length + SPAN] for b in range(blocks)], axis=0)
    result = lax.dot_general(segments, band, (((1,), (1,)), ((), ())), preferred_element_type=F32)
    filt[0 : blocks * slots] = result.astype(BF16)
    per_win = WIN_DEV // BLOCK
    per_tile = NS // BLOCK
    filt[blocks * slots :] = jnp.zeros(((per_tile - per_win) * slots, BLOCK), BF16)
    for d in range(win_count):
        first = (place_ref[0] ^ d) * per_win
        for m in range(per_tile):
            start = pl.multiple_of((first + m) * slots, slots)
            block = filt[pl.ds(start, slots), :]
            for p in range(2):
                tile[p, d * slots : (d + 1) * slots, m * LANE : (m + 1) * LANE] = tile_of(block, p)
    values = tile[...].astype(F32)
    scale = lax.rsqrt(jnp.sum(jnp.sum(values * values, axis=2, keepdims=True), axis=0) / NS + 1e-05)
    sums = []
    for p in range(2):
        loads[p].wait()
        sums.append(jnp.dot(tile[p], table[p], preferred_element_type=F32))
    for column, value in enumerate(butterfly(*sums)):
        value = (value * scale).astype(BF16)
        for d in range(win_count):
            outs[d][:, column * LANE : (column + 1) * LANE] = value[d * slots : (d + 1) * slots]


def column_ids(ids, tmpl, tmpl_count, slots):
    total = ids.shape[1]
    count = total // tmpl_count
    source = lax.broadcasted_iota(jnp.int32, (total, count), 0)
    target = lax.broadcasted_iota(jnp.int32, (total, count), 1)
    wanted = (target // slots * tmpl_count + tmpl) * slots + target % slots
    pick = jnp.where(source == wanted, 1.0, 0.0).astype(BF16)
    digits = jnp.concatenate([(ids + 1) // 64, (ids + 1) % 64], axis=0).astype(F32)
    digits = jnp.concatenate([digits, jnp.zeros((14, total), F32)], axis=0).astype(BF16)
    found = jnp.dot(digits, pick, preferred_element_type=F32)
    return found[0:1], found[1:2]


def picks(high, low, rows):
    count = high.shape[1]
    live = high + low > 0.0
    above = lax.broadcasted_iota(jnp.int32, (count, count), 0) < lax.broadcasted_iota(
        jnp.int32, (count, count), 1
    )
    marks = jnp.broadcast_to(jnp.where(live, 1.0, 0.0), (16, count)).astype(BF16)
    rank = jnp.dot(marks, jnp.where(above, 1.0, 0.0).astype(BF16), preferred_element_type=F32)
    rank = jnp.where(live, rank[0:1], -1.0)
    wanted = lax.broadcasted_iota(jnp.int32, (rows, count), 0).astype(F32)
    return jnp.where(wanted == rank, 1.0, 0.0).astype(BF16)


def compact_kernel(tmpl_count, place_ref, ids_ref, *rest):
    blocks, out_ref, data = rest[:-2], rest[-2], rest[-1]
    slots = blocks[0].shape[0]
    high, low = column_ids(ids_ref[...], place_ref[1], tmpl_count, slots)
    pick = picks(high, low, out_ref.shape[0])
    for d, block in enumerate(blocks):
        start = pl.multiple_of((place_ref[0] ^ d) * slots, slots)
        data[pl.ds(start, slots), :] = block[...]
    out_ref[...] = jnp.dot(pick, data[...], preferred_element_type=F32).astype(BF16)


def template_kernel(slots, shift_ref, after_ref, ids_ref, taps_ref, table_ref, phase_ref, *rest):
    u_ref, label_ref, flat_a, flat_b, wave = rest
    templates = taps_ref.shape[2]
    group = u_ref.shape[1] // 2
    groups = CH // group
    step = pl.program_id(0)

    def transform(index, flat):
        halves = [[], []]
        for j in range(group):
            wave[...] = taps_ref[index * group + j].astype(F32)
            for p in range(2):
                halves[p].append(jnp.transpose(wave[pl.ds(p, TL // 2, stride=2), :]).astype(BF16))
        sums = [
            jnp.dot(jnp.concatenate(halves[p], axis=0), table_ref[p], preferred_element_type=F32) for p in range(2)
        ]
        for column, value in enumerate(butterfly(*sums)):
            for g in range(group * templates // 8):
                flat[pl.ds(g * 8 * PITCH + column, 8, stride=PITCH), :] = value[g * 8 : (g + 1) * 8]

    def turn(index, flat, half):
        for k in range(templates):
            for j in range(group):
                at = (j * templates + k) * PITCH
                t_cos = flat[at : at + 8, :]
                t_sin = flat[at + TILES : at + TILES + 8, :]
                shift = shift_ref[index * group + j, k]
                p_cos = phase_ref[shift, 0:8]
                p_sin = phase_ref[shift, 8:16]
                real = t_cos * p_cos - t_sin * p_sin
                imag = t_sin * p_cos + t_cos * p_sin
                u_ref[k, half * group + j] = jnp.concatenate([real, imag], axis=0).astype(BF16)

    @pl.when(step == 0)
    def _():
        flat_a[group * templates * PITCH :, :] = jnp.zeros((8, LANE), F32)
        flat_b[group * templates * PITCH :, :] = jnp.zeros((8, LANE), F32)
        transform(0, flat_a)
        tmpl_count, width = label_ref.shape
        for t in range(tmpl_count):
            high, low = column_ids(ids_ref[...], t, tmpl_count, slots)
            digits = jnp.concatenate([high, low, jnp.zeros((14, high.shape[1]), F32)], axis=0).astype(BF16)
            pick = picks(high, low, width)
            row = lax.dot_general(digits, pick, (((1,), (1,)), ((), ())), preferred_element_type=F32)
            label_ref[t : t + 1, :] = (row[0:1] * 64.0 + row[1:2]).astype(jnp.int32) - 1

    transform(2 * step + 1, flat_b)
    turn(2 * step, flat_a, 0)
    transform(jnp.minimum(2 * step + 2, groups - 1), flat_a)
    turn(2 * step + 1, flat_b, 1)


def stack_kernel(live, place_ref, chan_ref, label_ref, u_hbm, inverse_hbm, *rest):
    pieces = rest[:-8]
    out_ref, u_all, inverse, flat, slabs, z, packed, sems = rest[-8:]
    templates = out_ref.shape[0]
    parts = 8
    some = templates // parts
    loads = []
    for i in range(parts):
        part = slice(i * some, (i + 1) * some)
        loads.append(pltpu.make_async_copy(u_hbm.at[part], u_all.at[part], sems.at[i]))
        loads[-1].start()
    table_copy = pltpu.make_async_copy(inverse_hbm, inverse, sems.at[parts])
    table_copy.start()
    rows = pieces[0].shape[0]
    tmpl = place_ref[1]
    flat[rows * PITCH :, :] = jnp.zeros((8, LANE), F32)
    for d, piece in enumerate(pieces):
        for g in range(rows // 16):
            for column in range(2 * TILES):
                value = piece[g * 16 : (g + 1) * 16, column * LANE : (column + 1) * LANE].astype(F32)
                for h in range(2):
                    flat[pl.ds((2 * g + h) * 8 * PITCH + column, 8, stride=PITCH), :] = value[h * 8 : (h + 1) * 8]
        for r in range(live):
            label = label_ref[tmpl ^ d, r]
            slabs[label, 0:8] = flat[r * PITCH : r * PITCH + 8]
            slabs[label, 8:16] = flat[r * PITCH + TILES : r * PITCH + TILES + 8]

    step = 4

    def several(i, carry):
        for q in range(step):
            k = i * step + q
            real, imag = [None, None], [None, None]
            for j in range(CH):
                c = chan_ref[j, k]
                u_cos = u_all[k, j, 0:8].astype(F32)
                u_sin = u_all[k, j, 8:16].astype(F32)
                x_cos = slabs[c, 0:8]
                x_sin = slabs[c, 8:16]
                re = u_cos * x_cos + u_sin * x_sin
                im = u_sin * x_cos - u_cos * x_sin
                p = j % 2
                real[p] = re if real[p] is None else real[p] + re
                imag[p] = im if imag[p] is None else imag[p] + im
            z[pl.ds(k, 8, stride=templates + 1), :] = real[0] + real[1]
            z[pl.ds(k + 8 * (templates + 1), 8, stride=templates + 1), :] = imag[0] + imag[1]
        return carry

    for i in range(parts):
        loads[i].wait()
        lax.fori_loop(i * some // step, (i + 1) * some // step, several, 0)

    first = lax.broadcasted_iota(jnp.int32, (templates, LANE), 1) == 0
    base = jnp.float32(CH * NS)
    for column in range(2 * TILES):
        row = column if column < TILES else column - TILES + 8
        weight = jnp.float32(2.0) / base
        if column % TILES == 0:
            weight = jnp.where(first, jnp.float32(1.0), jnp.float32(2.0)) / base
        value = z[row * (templates + 1) : row * (templates + 1) + templates, :] * weight
        packed[:, column * LANE : (column + 1) * LANE] = value.astype(BF16)
    table_copy.wait()
    out_ref[...] = jnp.dot(packed[...], inverse[...], preferred_element_type=F32)


def full(space=pltpu.VMEM):
    return pl.BlockSpec(memory_space=space)


def in_hbm(array):
    return pltpu.with_memory_space_constraint(array, pltpu.HBM)


def on_device(raw, ids, fir, taps, channels, shifts):
    win_count = lax.axis_size("win")
    tmpl_count = lax.axis_size("tmpl")
    win = lax.axis_index("win")
    tmpl = lax.axis_index("tmpl")
    slots, raw_t = raw.shape
    templates = taps.shape[0]
    live = 3 * slots * win_count // 5
    rows = -(-live // 16) * 16
    chan_total = live * tmpl_count
    table = forward_tables()
    inverse = jnp.asarray(inverse_table())
    phase = jnp.asarray(phase_table())

    place = jnp.stack([win, tmpl]).astype(jnp.int32)
    blocks = raw_t // (DEC * BLOCK)
    extra = (NS - WIN_DEV) // BLOCK
    mine = pl.pallas_call(
        spectra_kernel,
        out_shape=[jax.ShapeDtypeStruct((slots, NS), BF16)] * win_count,
        in_specs=[full(pltpu.SMEM)] + [full(pltpu.HBM)] * 3,
        out_specs=[full()] * win_count,
        scratch_shapes=[
            pltpu.VMEM((slots, raw_t + SPAN - DEC * BLOCK), BF16),
            pltpu.VMEM((1, NTAP), BF16),
            pltpu.VMEM((2, NS // 2, NF), BF16),
            pltpu.VMEM(((blocks + extra) * slots, BLOCK), BF16),
            pltpu.VMEM((2, win_count * slots, NS // 2), BF16),
            pltpu.SemaphoreType.DMA((4,)),
        ],
        compiler_params=pltpu.CompilerParams(vmem_limit_bytes=24 * MIB),
        name="spectra",
    )(place, in_hbm(raw), in_hbm(fir[None, :]), in_hbm(jnp.asarray(table)))

    parts = [mine[0]]
    for d in range(1, win_count):
        parts.append(lax.ppermute(mine[d], "win", [(i, i ^ d) for i in range(win_count)]))

    packed_rows = pl.pallas_call(
        functools.partial(compact_kernel, tmpl_count),
        out_shape=jax.ShapeDtypeStruct((rows, NS), BF16),
        in_specs=[full(pltpu.SMEM)] + [full()] * (1 + win_count),
        out_specs=full(),
        scratch_shapes=[pltpu.VMEM((win_count * slots, NS), BF16)],
        compiler_params=pltpu.CompilerParams(vmem_limit_bytes=24 * MIB),
        name="compact",
    )(place, ids[None, :], *parts)

    pair = 6
    slabs, labels = pl.pallas_call(
        functools.partial(template_kernel, slots),
        grid=(CH // pair,),
        out_shape=[
            pltpu.HBM((templates, CH, 16, LANE), BF16),
            pltpu.HBM((tmpl_count, -(-live // LANE) * LANE), jnp.int32),
        ],
        in_specs=[
            full(pltpu.SMEM),
            full(pltpu.HBM),
            full(),
            full(),
            full(),
            full(),
        ],
        out_specs=[
            pl.BlockSpec((templates, pair, 16, LANE), lambda i: (0, i, 0, 0)),
            full(),
        ],
        scratch_shapes=[pltpu.VMEM((pair // 2 * templates * PITCH + 8, LANE), F32)] * 2
        + [pltpu.VMEM((TL, LANE), F32)],
        compiler_params=pltpu.CompilerParams(vmem_limit_bytes=40 * MIB),
        name="templates",
    )(
        shifts.T,
        in_hbm(packed_rows),
        ids[None, :],
        in_hbm(taps.transpose(1, 2, 0)),
        in_hbm(jnp.asarray(table[:, : TL // 2])),
        in_hbm(phase),
    )

    held = {0: packed_rows}
    bit = tmpl_count // 2
    while bit:
        for d in list(held):
            source = held[d]
            if d and bit == 1:
                source, slabs = lax.optimization_barrier((source, slabs))
            held[d | bit] = lax.ppermute(source, "tmpl", [(i, i ^ bit) for i in range(tmpl_count)])
        bit //= 2
    pieces = [held[d] for d in range(tmpl_count)]

    return pl.pallas_call(
        functools.partial(stack_kernel, live),
        out_shape=jax.ShapeDtypeStruct((templates, WIN_DEV), F32),
        in_specs=[full(pltpu.SMEM)] * 3 + [full(pltpu.HBM)] * 2 + [full()] * tmpl_count,
        out_specs=full(),
        scratch_shapes=[
            pltpu.VMEM((templates, CH, 16, LANE), BF16),
            pltpu.VMEM((2 * NF, WIN_DEV), BF16),
            pltpu.VMEM((rows * PITCH + 8, LANE), F32),
            pltpu.VMEM((chan_total, 16, LANE), F32),
            pltpu.VMEM((16 * (templates + 1), LANE), F32),
            pltpu.VMEM((templates, NS), BF16),
            pltpu.SemaphoreType.DMA((9,)),
        ],
        compiler_params=pltpu.CompilerParams(vmem_limit_bytes=(32 if chan_total <= 1024 else 58) * MIB),
        name="stacks",
    )(place, channels.T, labels, in_hbm(slabs), in_hbm(inverse), *pieces)


def solution(mesh):
    return jax.shard_map(
        on_device,
        mesh=mesh,
        in_specs=(
            P(("win", "tmpl"), None),
            P(),
            P(),
            P("tmpl", None, None),
            P("tmpl", None),
            P("tmpl", None),
        ),
        out_specs=P("tmpl", "win"),
        check_vma=False,
    )
```

time: 113 us -> 55.5 us (0.49)
  local copies, waits for them, and re-layouts: 39.3 us -> 1.65 us
  Pallas kernels: 47.9 us -> 30.9 us
  other arithmetic: 2.69 us -> 0.07 us
    unnamed x41 -> x12, local copies, waits for them, and re-layouts: 35.7 us -> 1.65 us
    pallas_call x2, Pallas kernels: 36.5 us -> 17.7 us  [the longest x1 16.7 us: on_device(): pl.pallas_call(functools.partial(template_kernel, slots), grid=(CH // pai...]
    ppermute x7, waiting for transfers between devices: 2.49 us -> 6.86 us  [on_device(): lax.ppermute(mine[d], 'win', [(i, i ^ d) for i in range(win_count)])]
    ppermute x3, waiting for transfers between devices: 5.24 us -> 1.2 us  [on_device(): lax.ppermute(source, 'tmpl', [(i, i ^ bit) for i in range(tmpl_count)])]
    pallas_call x1, Pallas kernels: 8.15 us -> 9.54 us  [on_device(): pl.pallas_call(functools.partial(stack_kernel, live), out_shape=jax.Shape...]
    select_n x2 -> x0, other arithmetic: 1.34 us -> none  [on_device(): jnp.take(lax.dynamic_index_in_dim(grid, tmpl, 1, keepdims=False), owners,...]
    gather x1 -> x0, local copies, waits for them, and re-layouts: 1.26 us -> none  [on_device(): jnp.take(lax.dynamic_index_in_dim(grid, tmpl, 1, keepdims=False), owners,...]
  transfers between devices with their start and end apart: 10 -> 10, of which waited for: 2 -> 3; matrix products, arithmetic and copies ran while one was open for 6% -> 0% of each run, Pallas kernels for 32% -> 30%
where the time goes in v2:
time: 55.5 us; the launch traced here: 55.3 us
  Pallas kernels  30.9 us (56%)
  starting transfers between devices  14.6 us (26%)
  waiting for transfers between devices  8.06 us (15%)
  local copies, waits for them, and re-layouts  1.65 us (3%)
    pallas_call x1, Pallas kernels, on_device(): pl.pallas_call(functools.partial(template_kernel, slots), grid=(CH // pai...  16.7 us
    ppermute x7, starting transfers between devices, on_device(): lax.ppermute(mine[d], 'win', [(i, i ^ d) for i in range(win_count)])  12.5 us
    pallas_call x1, Pallas kernels, on_device(): pl.pallas_call(functools.partial(stack_kernel, live), out_shape=jax.Shape...  9.54 us
    ppermute x7, waiting for transfers between devices, on_device(): lax.ppermute(mine[d], 'win', [(i, i ^ d) for i in range(win_count)])  6.86 us
    pallas_call x1, Pallas kernels, on_device(): pl.pallas_call(spectra_kernel, out_shape=[jax.ShapeDtypeStruct((slots, NS...  3.62 us
    ppermute x3, starting transfers between devices, on_device(): lax.ppermute(source, 'tmpl', [(i, i ^ bit) for i in range(tmpl_count)])  2.1 us
    unnamed x12, local copies, waits for them, and re-layouts  1.65 us
    ppermute x3, waiting for transfers between devices, on_device(): lax.ppermute(source, 'tmpl', [(i, i ^ bit) for i in range(tmpl_count)])  1.2 us
  transfers between devices with their start and end apart: 10, of which 3 were waited for; matrix products, arithmetic and copies ran while one was open for 0% of the time, Pallas kernels for 30%

profile of v2, /device:TPU:0, one launch (start us, length us, event | category | flops | bytes accessed | tf_op | source)
XLA Modules:
  0.0 55.3 jit_solution(8998378083709852295)
XLA Ops:
  0.0 0.0 copy-start.4
  0.0 0.0 copy-start.2
  0.0 0.1 pad_add_fusion.place_ref
  0.1 3.6 %spectra.1 = (bf16[16,1792]{1,0:T(8,128)(2,1)S(1)}, bf16[16,1792]{1,0:T(8,128)(2,1)S(1)}, bf16[16,1792]{1,0:T(8,128)(2,1)S(1)}, bf16[16,1792]{1,0:T(8,128)(2,1)S...) custom-call(s32[2]{0:T(128)S(1)} %pad_add_fusion.place_ref, ...), custom_call_target="tpu_custom_call" | custom-call | tf_op jit(solution)/shard_map/spectra/pallas_call | solution.py:317
  3.7 3.0 %collective-permute-start = (bf16[16,1792]{1,0:T(8,128)(2,1)S(1)}, bf16[16,1792]{1,0:T(8,128)(2,1)S(1)}, u32[]{:S(2)}, u32[]{:S(2)}) collective-permute-start(bf16[16,1792]{1,0:T(8,128)(2,1)S(1)} %get-tuple-element.18), channel_id=1, source_target_pairs={{0,4},{4,0},{8,12},{12,8},{16,20},{20,16},{24,28},{28,24},{1,5},{5... | collective-permute-start | bytes 172040 | tf_op jit(solution)/shard_map/ppermute | solution.py:336
  6.7 1.6 %collective-permute-start.1 = (bf16[16,1792]{1,0:T(8,128)(2,1)S(1)}, bf16[16,1792]{1,0:T(8,128)(2,1)S(1)}, u32[]{:S(2)}, u32[]{:S(2)}) collective-permute-start(bf16[16,1792]{1,0:T(8,128)(2,1)S(1)} %get-tuple-element.19), channel_id=1, source_target_pairs={{0,8},{4,12},{8,0},{12,4},{16,24},{20,28},{24,16},{28,20},{1,9},{5... | collective-permute-start | bytes 172040 | tf_op jit(solution)/shard_map/ppermute | solution.py:336
  8.3 0.0 collective-permute-start.2
  8.3 3.0 %collective-permute-start.3 = (bf16[16,1792]{1,0:T(8,128)(2,1)S(1)}, bf16[16,1792]{1,0:T(8,128)(2,1)S(1)}, u32[]{:S(2)}, u32[]{:S(2)}) collective-permute-start(bf16[16,1792]{1,0:T(8,128)(2,1)S(1)} %get-tuple-element.21), channel_id=1, source_target_pairs={{0,16},{4,20},{8,24},{12,28},{16,0},{20,4},{24,8},{28,12},{1,17},{... | collective-permute-start | bytes 172040 | tf_op jit(solution)/shard_map/ppermute | solution.py:336
  11.3 1.3 %collective-permute-start.4 = (bf16[16,1792]{1,0:T(8,128)(2,1)S(1)}, bf16[16,1792]{1,0:T(8,128)(2,1)S(1)}, u32[]{:S(2)}, u32[]{:S(2)}) collective-permute-start(bf16[16,1792]{1,0:T(8,128)(2,1)S(1)} %get-tuple-element.22), channel_id=1, source_target_pairs={{0,20},{4,16},{8,28},{12,24},{16,4},{20,0},{24,12},{28,8},{1,21},{... | collective-permute-start | bytes 172040 | tf_op jit(solution)/shard_map/ppermute | solution.py:336
  12.6 0.0 collective-permute-done.rest_1_
  12.6 3.6 %collective-permute-start.5 = (bf16[16,1792]{1,0:T(8,128)(2,1)S(1)}, bf16[16,1792]{1,0:T(8,128)(2,1)S(1)}, u32[]{:S(2)}, u32[]{:S(2)}) collective-permute-start(bf16[16,1792]{1,0:T(8,128)(2,1)S(1)} %get-tuple-element.23), channel_id=1, source_target_pairs={{0,24},{4,28},{8,16},{12,20},{16,8},{20,12},{24,0},{28,4},{1,25},{... | collective-permute-start | bytes 172040 | tf_op jit(solution)/shard_map/ppermute | solution.py:336
  16.2 0.0 collective-permute-done.1.rest_2_
  16.2 0.0 collective-permute-start.6
  16.2 0.0 collective-permute-done.2.rest_3_
  16.2 0.0 collective-permute-done.3.rest_4_
  16.2 4.3 %collective-permute-done.4.rest_5_ = bf16[16,1792]{1,0:T(8,128)(2,1)S(1)} collective-permute-done((bf16[16,1792]{1,0:T(8,128)(2,1)S(1)}, bf16[16,1792]{1,0:T(8,128)(2,1)S(1)}, u32[]{:S(2)}, u32[]{:S(2)}) %collective-permute-start.4) | collective-permute-done | bytes 57376 | tf_op jit(solution)/shard_map/ppermute | solution.py:336
  20.5 0.0 collective-permute-done.5.rest_6_
  20.5 2.6 %collective-permute-done.6.rest_7_ = bf16[16,1792]{1,0:T(8,128)(2,1)S(1)} collective-permute-done((bf16[16,1792]{1,0:T(8,128)(2,1)S(1)}, bf16[16,1792]{1,0:T(8,128)(2,1)S(1)}, u32[]{:S(2)}, u32[]{:S(2)}) %collective-permute-start.6) | collective-permute-done | bytes 57376 | tf_op jit(solution)/shard_map/ppermute | solution.py:336
  23.1 0.0 copy-done.4
  23.1 1.0 %compact.1.after_ref.rest_0_ = bf16[80,1792]{1,0:T(8,128)(2,1)S(1)} custom-call(s32[2]{0:T(128)S(1)} %pad_add_fusion.place_ref, s32[1,512]{1,0:T(1,128)S(1)} %bitcast.9, bf16[16,1792]{1,0:T(8,128)(2,1)S(1)} %get-tuple-element.17.rest_0_, bf16[16,1792]{1,0:T(8,128)(2,1)S(1)} %collective-permute-done.rest_1_, ...), custom_call_target="tpu_custom_call" | custom-call | tf_op jit(solution)/shard_map/compact/pallas_call | solution.py:338
  24.1 0.0 copy-start
  24.1 0.0 copy-start.3
  24.1 1.6 %collective-permute-start.7 = (bf16[80,1792]{1,0:T(8,128)(2,1)S(1)}, bf16[80,1792]{1,0:T(8,128)(2,1)S(1)}, u32[]{:S(2)}, u32[]{:S(2)}) collective-permute-start(bf16[80,1792]{1,0:T(8,128)(2,1)S(1)} %compact.1.after_ref.rest_0_), channel_id=1, source_target_pairs={{0,2},{1,3},{2,0},{3,1},{4,6},{5,7},{6,4},{7,5},{8,10},{9,11},{10,... | collective-permute-start | bytes 860168 | tf_op jit(solution)/shard_map/ppermute | solution.py:388
  25.7 0.0 collective-permute-start.8
  25.7 0.0 copy-done
  25.7 0.0 copy-done.2
  25.7 16.7 %templates.1 = (bf16[128,30,16,128]{3,2,1,0:T(8,128)(2,1)}, s32[4,128]{1,0:T(4,128)}) custom-call(s32[30,128]{1,0:T(8,128)S(1)} %bitcast.7, bf16[80,1792]{1,0:T(8,128)(2,1)} %copy-done, s32[1,512]{1,0:T(1,128)S(1)} %bitcast.10, bf16[30,400,128]{2,1,0:T(8,128)(2,1)} %bitcast.11, bf16[2,200,896]{2,1,0:T(8,128)(2,1)} %constant.20.clone.table_ref, ...), custom_call_target="tpu_custom_call" | custom-call | tf_op jit(solution)/shard_map/templates/pallas_call | solution.py:349
  42.4 0.0 collective-permute-done.7.rest_2_
  42.4 0.5 collective-permute-start.9
  43.0 0.0 collective-permute-done.8.rest_1_
  43.0 1.2 %collective-permute-done.9.rest_3_ = bf16[80,1792]{1,0:T(8,128)(2,1)S(1)} collective-permute-done((bf16[80,1792]{1,0:T(8,128)(2,1)S(1)}, bf16[80,1792]{1,0:T(8,128)(2,1)S(1)}, u32[]{:S(2)}, u32[]{:S(2)}) %collective-permute-start.9) | collective-permute-done | bytes 286752 | tf_op jit(solution)/shard_map/ppermute | solution.py:388
  44.2 0.0 copy-done.3
  44.2 0.0 copy-start.1
  44.2 1.0 %copy-done.1 = bf16[80,1792]{1,0:T(8,128)(2,1)S(1)} copy-done((bf16[80,1792]{1,0:T(8,128)(2,1)S(1)}, bf16[80,1792]{1,0:T(8,128)(2,1)}, u32[]{:S(2)}) %copy-start.1) | copy-done | bytes 286744
  45.1 0.0 copy-start.5
  45.1 0.7 %copy-done.5 = s32[4,128]{1,0:T(4,128)S(1)} copy-done((s32[4,128]{1,0:T(4,128)S(1)}, s32[4,128]{1,0:T(4,128)}, u32[]{:S(2)}) %copy-start.5) | copy-done | bytes 2072
  45.8 9.5 %stacks.1 = f32[128,1024]{1,0:T(8,128)} custom-call(s32[2]{0:T(128)S(1)} %pad_add_fusion.place_ref, s32[30,128]{1,0:T(8,128)S(1)} %bitcast.8, s32[4,128]{1,0:T(4,128)S(1)} %copy-done.5, bf16[128,30,16,128]{3,2,1,0:T(8,128)(2,1)} %get-tuple-element.27.u_hbm, bf16[1792,1024]{1,0:T(8,128)(2,1)} %constant.17.clone.inverse_hbm, bf16[80,1792]{1,0:T(8,128)(2,1)S(1)} %copy-done.1, ...), custom_call_target="tpu_custom_call" | custom-call | tf_op jit(solution)/shard_map/stacks/pallas_call | solution.py:392
Async XLA Ops:
  0.0 23.1 %copy-start.4 = (s32[512]{0:T(512)S(1)}, s32[512]{0:T(512)}, u32[]{:S(2)}) copy-start(s32[512]{0:T(512)} %param.11) | copy-start | bytes 6148
  0.0 25.7 %copy-start.2 = (s32[128,30]{0,1:T(8,128)S(1)}, s32[128,30]{0,1:T(8,128)}, u32[]{:S(2)}) copy-start(s32[128,30]{0,1:T(8,128)} %param.15) | copy-start | bytes 46084
  3.7 8.9 %collective-permute-start = (bf16[16,1792]{1,0:T(8,128)(2,1)S(1)}, bf16[16,1792]{1,0:T(8,128)(2,1)S(1)}, u32[]{:S(2)}, u32[]{:S(2)}) collective-permute-start(bf16[16,1792]{1,0:T(8,128)(2,1)S(1)} %get-tuple-element.18), channel_id=1, source_target_pairs={{0,4},{4,0},{8,12},{12,8},{16,20},{20,16},{24,28},{28,24},{1,5},{5... | collective-permute-start | bytes 172040 | tf_op jit(solution)/shard_map/ppermute | solution.py:336
  6.7 9.5 %collective-permute-start.1 = (bf16[16,1792]{1,0:T(8,128)(2,1)S(1)}, bf16[16,1792]{1,0:T(8,128)(2,1)S(1)}, u32[]{:S(2)}, u32[]{:S(2)}) collective-permute-start(bf16[16,1792]{1,0:T(8,128)(2,1)S(1)} %get-tuple-element.19), channel_id=1, source_target_pairs={{0,8},{4,12},{8,0},{12,4},{16,24},{20,28},{24,16},{28,20},{1,9},{5... | collective-permute-start | bytes 172040 | tf_op jit(solution)/shard_map/ppermute | solution.py:336
  8.3 7.9 %collective-permute-start.2 = (bf16[16,1792]{1,0:T(8,128)(2,1)S(1)}, bf16[16,1792]{1,0:T(8,128)(2,1)S(1)}, u32[]{:S(2)}, u32[]{:S(2)}) collective-permute-start(bf16[16,1792]{1,0:T(8,128)(2,1)S(1)} %get-tuple-element.20), channel_id=1, source_target_pairs={{0,12},{4,8},{8,4},{12,0},{16,28},{20,24},{24,20},{28,16},{1,13},{... | collective-permute-start | bytes 172040 | tf_op jit(solution)/shard_map/ppermute | solution.py:336
  8.3 7.9 %collective-permute-start.3 = (bf16[16,1792]{1,0:T(8,128)(2,1)S(1)}, bf16[16,1792]{1,0:T(8,128)(2,1)S(1)}, u32[]{:S(2)}, u32[]{:S(2)}) collective-permute-start(bf16[16,1792]{1,0:T(8,128)(2,1)S(1)} %get-tuple-element.21), channel_id=1, source_target_pairs={{0,16},{4,20},{8,24},{12,28},{16,0},{20,4},{24,8},{28,12},{1,17},{... | collective-permute-start | bytes 172040 | tf_op jit(solution)/shard_map/ppermute | solution.py:336
  11.3 9.2 %collective-permute-start.4 = (bf16[16,1792]{1,0:T(8,128)(2,1)S(1)}, bf16[16,1792]{1,0:T(8,128)(2,1)S(1)}, u32[]{:S(2)}, u32[]{:S(2)}) collective-permute-start(bf16[16,1792]{1,0:T(8,128)(2,1)S(1)} %get-tuple-element.22), channel_id=1, source_target_pairs={{0,20},{4,16},{8,28},{12,24},{16,4},{20,0},{24,12},{28,8},{1,21},{... | collective-permute-start | bytes 172040 | tf_op jit(solution)/shard_map/ppermute | solution.py:336
  12.6 7.9 %collective-permute-start.5 = (bf16[16,1792]{1,0:T(8,128)(2,1)S(1)}, bf16[16,1792]{1,0:T(8,128)(2,1)S(1)}, u32[]{:S(2)}, u32[]{:S(2)}) collective-permute-start(bf16[16,1792]{1,0:T(8,128)(2,1)S(1)} %get-tuple-element.23), channel_id=1, source_target_pairs={{0,24},{4,28},{8,16},{12,20},{16,8},{20,12},{24,0},{28,4},{1,25},{... | collective-permute-start | bytes 172040 | tf_op jit(solution)/shard_map/ppermute | solution.py:336
  16.2 6.9 %collective-permute-start.6 = (bf16[16,1792]{1,0:T(8,128)(2,1)S(1)}, bf16[16,1792]{1,0:T(8,128)(2,1)S(1)}, u32[]{:S(2)}, u32[]{:S(2)}) collective-permute-start(bf16[16,1792]{1,0:T(8,128)(2,1)S(1)} %get-tuple-element.24), channel_id=1, source_target_pairs={{0,28},{4,24},{8,20},{12,16},{16,12},{20,8},{24,4},{28,0},{1,29},{... | collective-permute-start | bytes 172040 | tf_op jit(solution)/shard_map/ppermute | solution.py:336
  24.1 1.6 %copy-start = (bf16[80,1792]{1,0:T(8,128)(2,1)}, bf16[80,1792]{1,0:T(8,128)(2,1)S(1)}, u32[]{:S(2)}) copy-start(bf16[80,1792]{1,0:T(8,128)(2,1)S(1)} %compact.1.after_ref.rest_0_) | copy-start | bytes 860164
  24.1 20.0 %copy-start.3 = (s32[128,30]{0,1:T(8,128)S(1)}, s32[128,30]{0,1:T(8,128)}, u32[]{:S(2)}) copy-start(s32[128,30]{0,1:T(8,128)} %param.14) | copy-start | bytes 46084
  24.1 18.3 %collective-permute-start.7 = (bf16[80,1792]{1,0:T(8,128)(2,1)S(1)}, bf16[80,1792]{1,0:T(8,128)(2,1)S(1)}, u32[]{:S(2)}, u32[]{:S(2)}) collective-permute-start(bf16[80,1792]{1,0:T(8,128)(2,1)S(1)} %compact.1.after_ref.rest_0_), channel_id=1, source_target_pairs={{0,2},{1,3},{2,0},{3,1},{4,6},{5,7},{6,4},{7,5},{8,10},{9,11},{10,... | collective-permute-start | bytes 860168 | tf_op jit(solution)/shard_map/ppermute | solution.py:388
  25.7 17.3 %collective-permute-start.8 = (bf16[80,1792]{1,0:T(8,128)(2,1)S(1)}, bf16[80,1792]{1,0:T(8,128)(2,1)S(1)}, u32[]{:S(2)}, u32[]{:S(2)}) collective-permute-start(bf16[80,1792]{1,0:T(8,128)(2,1)S(1)} %compact.1.after_ref.rest_0_), channel_id=1, source_target_pairs={{0,1},{1,0},{2,3},{3,2},{4,5},{5,4},{6,7},{7,6},{8,9},{9,8},{10,11... | collective-permute-start | bytes 860168 | tf_op jit(solution)/shard_map/ppermute | solution.py:388
  42.4 1.7 %collective-permute-start.9 = (bf16[80,1792]{1,0:T(8,128)(2,1)S(1)}, bf16[80,1792]{1,0:T(8,128)(2,1)S(1)}, u32[]{:S(2)}, u32[]{:S(2)}) collective-permute-start(bf16[80,1792]{1,0:T(8,128)(2,1)S(1)} %collective-permute-done.7.rest_2_), channel_id=1, source_target_pairs={{0,1},{1,0},{2,3},{3,2},{4,5},{5,4},{6,7},{7,6},{8,9},{9,8},{10,11... | collective-permute-start | bytes 860168 | tf_op jit(solution)/shard_map/ppermute | solution.py:388
  44.2 1.0 %copy-start.1 = (bf16[80,1792]{1,0:T(8,128)(2,1)S(1)}, bf16[80,1792]{1,0:T(8,128)(2,1)}, u32[]{:S(2)}) copy-start(bf16[80,1792]{1,0:T(8,128)(2,1)} %copy-done) | copy-start | bytes 860164
  45.1 0.7 %copy-start.5 = (s32[4,128]{1,0:T(4,128)S(1)}, s32[4,128]{1,0:T(4,128)}, u32[]{:S(2)}) copy-start(s32[4,128]{1,0:T(4,128)} %get-tuple-element.25.label_ref) | copy-start | bytes 6148

commit v3 on v2

v3 whole, which is shorter than its diff:
```python
import functools
import math

import jax
import jax.numpy as jnp
import ml_dtypes
import numpy as np
from jax import lax
from jax.experimental import pallas as pl
from jax.experimental.pallas import tpu as pltpu
from jax.sharding import PartitionSpec as P

WIN_DEV = 1024
TL = 400
CH = 30
DEC = 2
NTAP = 64
MOVE = 256
NS = 1792
NF = 896
LANE = 128
TILES = NF // LANE
BLOCK = 256
SPAN = 640
PITCH = 2 * TILES
GROUP = 3
MIB = 2**20
BF16 = jnp.bfloat16
F32 = jnp.float32


def angles(rows, columns):
    step = np.float32(2.0 * math.pi / NS)
    turns = np.arange(rows)[:, None] * np.arange(columns)[None, :] % NS
    return (turns.astype(np.float32) * step).astype(np.float64)


def order():
    low = np.arange(3 * LANE)
    high = NF - low
    high[0] = NF // 2
    rest = np.arange(3 * LANE, NF // 2)
    return np.concatenate([low, high, rest, NF - rest])


def forward_tables():
    angle = angles(NS, NF)
    cosine, sine = np.cos(angle), np.sin(angle)
    half = NF // 2
    columns = []
    for begin in range(0, half, LANE):
        end = min(begin + LANE, half)
        columns += [cosine[:, begin:end], sine[:, begin:end]]
    table = np.concatenate(columns, axis=1)
    even, odd = table[0::2].copy(), table[1::2].copy()
    even[:, LANE] = cosine[0::2, half]
    odd[:, LANE] = sine[1::2, half]
    return np.stack([even, odd]).astype(ml_dtypes.bfloat16)


def inverse_table():
    angle = angles(NF, WIN_DEV)[order()]
    return np.concatenate([np.cos(angle), -np.sin(angle)], axis=0).astype(ml_dtypes.bfloat16)


def phase_table(versions, coarse):
    angle = angles(versions * coarse, NF)[::coarse, order()]
    slab = np.zeros((versions, 16, LANE), np.float32)
    slab[:, :TILES] = np.cos(angle).reshape(versions, TILES, LANE)
    slab[:, 8 : 8 + TILES] = np.sin(angle).reshape(versions, TILES, LANE)
    return slab


def tile_of(array, column):
    return array[:, column * LANE : (column + 1) * LANE]


def butterfly(q, even, odd):
    lane = lax.broadcasted_iota(jnp.int32, (even.shape[0], LANE), 1)
    if q == 3:
        low, gap = even + odd, even - odd
        left = lane < LANE // 2
        yield 6, jnp.where(left, low, pltpu.roll(gap, LANE // 2, 1))
        yield 13, jnp.where(left, pltpu.roll(low, LANE // 2, 1), -gap)
        return
    low_cos, low_sin = tile_of(even, 0) + tile_of(odd, 0), tile_of(even, 1) + tile_of(odd, 1)
    high_cos, high_sin = tile_of(even, 0) - tile_of(odd, 0), tile_of(odd, 1) - tile_of(even, 1)
    if q == 0:
        low_sin = jnp.where(lane == 0, 0.0, low_sin)
        high_cos = jnp.where(lane == 0, tile_of(even, 1), high_cos)
        high_sin = jnp.where(lane == 0, tile_of(odd, 1), high_sin)
    yield q, low_cos
    yield 7 + q, low_sin
    yield 3 + q, high_cos
    yield 10 + q, high_sin


def columns_of(q):
    return slice(2 * q * LANE, min(2 * (q + 1) * LANE, NF))


def spectra_kernel(place_ref, raw_hbm, fir_hbm, table_hbm, *rest):
    win_count = len(rest) - 6
    outs = rest[:win_count]
    raw, fir, table, filt, tile, sems = rest[win_count:]
    slots, raw_t = raw_hbm.shape
    length = DEC * BLOCK
    blocks = raw_t // length
    raw_copy = pltpu.make_async_copy(raw_hbm, raw.at[:, 0:raw_t], sems.at[0])
    raw_copy.start()
    fir_copy = pltpu.make_async_copy(fir_hbm, fir, sems.at[1])
    fir_copy.start()
    loads = [pltpu.make_async_copy(table_hbm.at[p], table.at[p], sems.at[2 + p]) for p in range(2)]
    for load in loads:
        load.start()
    raw[:, raw_t:] = jnp.zeros((slots, SPAN - length), BF16)
    fir_copy.wait()
    taps = jnp.concatenate([fir[...].astype(F32), jnp.zeros((1, SPAN - NTAP), F32)], axis=1)
    spread = jnp.broadcast_to(taps, (BLOCK // 2, SPAN))
    even = pltpu.roll(spread, 0, 1, stride=2 * DEC, stride_axis=0)
    odd = pltpu.roll(spread, DEC, 1, stride=2 * DEC, stride_axis=0)
    band = jnp.concatenate([even, odd], axis=0).astype(BF16)
    raw_copy.wait()
    segments = jnp.concatenate([raw[:, b * length : b * length + SPAN] for b in range(blocks)], axis=0)
    result = lax.dot_general(segments, band, (((1,), (1,)), ((), ())), preferred_element_type=F32)
    filt[0 : blocks * slots] = result.astype(BF16)
    per_win = WIN_DEV // BLOCK
    per_tile = NS // BLOCK
    filt[blocks * slots :] = jnp.zeros(((per_tile - per_win) * slots, BLOCK), BF16)
    for d in range(win_count):
        first = (place_ref[0] ^ d) * per_win
        for m in range(per_tile):
            start = pl.multiple_of((first + m) * slots, slots)
            block = filt[pl.ds(start, slots), :]
            for p in range(2):
                tile[p, d * slots : (d + 1) * slots, m * LANE : (m + 1) * LANE] = tile_of(block, p)
    values = tile[...].astype(F32)
    scale = lax.rsqrt(jnp.sum(jnp.sum(values * values, axis=2, keepdims=True), axis=0) / NS + 1e-05)
    for load in loads:
        load.wait()
    for q in range(4):
        sums = [jnp.dot(tile[p], table[p, :, columns_of(q)], preferred_element_type=F32) for p in range(2)]
        for column, value in butterfly(q, *sums):
            value = (value * scale).astype(BF16)
            for d in range(win_count):
                outs[d][:, column * LANE : (column + 1) * LANE] = value[d * slots : (d + 1) * slots]


def column_ids(ids, tmpl, tmpl_count, slots):
    total = ids.shape[1]
    count = total // tmpl_count
    source = lax.broadcasted_iota(jnp.int32, (total, count), 0)
    target = lax.broadcasted_iota(jnp.int32, (total, count), 1)
    wanted = (target // slots * tmpl_count + tmpl) * slots + target % slots
    pick = jnp.where(source == wanted, 1.0, 0.0).astype(BF16)
    digits = jnp.concatenate([(ids + 1) // 64, (ids + 1) % 64], axis=0).astype(F32)
    digits = jnp.concatenate([digits, jnp.zeros((14, total), F32)], axis=0).astype(BF16)
    found = jnp.dot(digits, pick, preferred_element_type=F32)
    return found[0:1], found[1:2]


def picks(high, low, rows):
    count = high.shape[1]
    live = high + low > 0.0
    above = lax.broadcasted_iota(jnp.int32, (count, count), 0) < lax.broadcasted_iota(
        jnp.int32, (count, count), 1
    )
    marks = jnp.broadcast_to(jnp.where(live, 1.0, 0.0), (16, count)).astype(BF16)
    rank = jnp.dot(marks, jnp.where(above, 1.0, 0.0).astype(BF16), preferred_element_type=F32)
    rank = jnp.where(live, rank[0:1], -1.0)
    wanted = lax.broadcasted_iota(jnp.int32, (rows, count), 0).astype(F32)
    return jnp.where(wanted == rank, 1.0, 0.0).astype(BF16)


def compact_kernel(tmpl_count, place_ref, ids_ref, *rest):
    blocks, out_ref, data = rest[:-2], rest[-2], rest[-1]
    slots = blocks[0].shape[0]
    high, low = column_ids(ids_ref[...], place_ref[1], tmpl_count, slots)
    pick = picks(high, low, out_ref.shape[0])
    for d, block in enumerate(blocks):
        start = pl.multiple_of((place_ref[0] ^ d) * slots, slots)
        data[pl.ds(start, slots), :] = block[...]
    out_ref[...] = jnp.dot(pick, data[...], preferred_element_type=F32).astype(BF16)


def delayed(wave, shift, most):
    row = lax.broadcasted_iota(jnp.int32, (8, LANE), 0)
    fine = jnp.broadcast_to(shift & 7, (8, LANE))
    keep = row >= fine
    source = (row - fine) & 7
    zero = jnp.zeros((8, LANE), F32)
    turned = [jnp.take_along_axis(wave[i : i + 8], source, axis=0) for i in range(0, wave.shape[0], 8)]
    tiles = [jnp.where(keep, here, above) for here, above in zip(turned + [zero], [zero] + turned)]
    size = 1
    while len(tiles) < most:
        move = jnp.broadcast_to((shift & (8 * size)) != 0, (8, LANE))
        still = tiles + [zero] * size
        moved = [zero] * size + tiles
        tiles = [jnp.where(move, moved[i], still[i]) for i in range(min(len(still), most))]
        size *= 2
    return jnp.concatenate(tiles + [zero] * (-most % 2), axis=0)


def template_kernel(begin, coarse, shift_ref, after_ref, taps_ref, table_ref, u_ref, wave):
    templates = taps_ref.shape[2]
    count = u_ref.shape[0] // (templates * PITCH)
    most = (TL + coarse) // 16

    def load(index):
        halves = [[], []]
        for j in range(index * GROUP, (index + 1) * GROUP):
            wave[...] = taps_ref[j].astype(F32)
            even, odd = wave[pl.ds(0, TL // 2, stride=2), :], wave[pl.ds(1, TL // 2, stride=2), :]
            shift = shift_ref[begin + j : begin + j + 1, :] % coarse
            swap = jnp.broadcast_to((shift & 1) != 0, even.shape)
            halves[0].append(delayed(jnp.where(swap, odd, even), (shift + 1) >> 1, most))
            halves[1].append(delayed(jnp.where(swap, even, odd), shift >> 1, most))
        return [jnp.concatenate([jnp.transpose(h.astype(BF16)) for h in half], axis=0) for half in halves]

    for index in range(count // GROUP):
        halves = load(index)
        for q in range(4):
            sums = [jnp.dot(halves[p], table_ref[p, :, columns_of(q)], preferred_element_type=F32) for p in range(2)]
            for column, value in butterfly(q, *sums):
                for j in range(GROUP):
                    for g in range(templates // 8):
                        at = (g * 8 * count + index * GROUP + j) * PITCH + column
                        part = value[j * templates + g * 8 : j * templates + (g + 1) * 8]
                        u_ref[pl.ds(at, 8, stride=count * PITCH), :] = part


def index_kernel(slots, versions, coarse, ids_ref, channel_ref, shift_ref, label_ref, slab_ref):
    tmpl_count, width = label_ref.shape
    for t in range(tmpl_count):
        high, low = column_ids(ids_ref[...], t, tmpl_count, slots)
        digits = jnp.concatenate([high, low, jnp.zeros((14, high.shape[1]), F32)], axis=0).astype(BF16)
        pick = picks(high, low, width)
        row = lax.dot_general(digits, pick, (((1,), (1,)), ((), ())), preferred_element_type=F32)
        label_ref[t : t + 1, :] = (row[0:1] * 64.0 + row[1:2]).astype(jnp.int32) - 1
    slab_ref[0:CH, :] = channel_ref[...] * versions + shift_ref[...] // coarse
    slab_ref[CH:, :] = jnp.zeros((slab_ref.shape[0] - CH, slab_ref.shape[1]), jnp.int32)


def stack_kernel(live, versions, counts, in_main, place_ref, slab_ref, label_ref, inverse_hbm, phase_ref, *rest):
    u_refs, pieces = rest[: len(counts)], rest[len(counts) : -8]
    out_ref, inverse, flat, slabs, z, packed, held, sems = rest[-8:]
    templates = out_ref.shape[0]
    table_copy = pltpu.make_async_copy(inverse_hbm, inverse, sems.at[0])
    table_copy.start()
    rows = held.shape[0]
    tmpl = place_ref[1]
    flat[rows * PITCH :, :] = jnp.zeros((8, LANE), F32)
    turns = [(phase_ref[a, 0:8], phase_ref[a, 8:16]) for a in range(1, versions)]
    fetches = [pltpu.make_async_copy(pieces[d], held, sems.at[1]) for d in in_main]
    fetches[0].start()
    for d in [d for d in range(len(pieces)) if d not in in_main] + list(in_main):
        piece = pieces[d]
        if d in in_main:
            which = in_main.index(d)
            if which:
                fetches[which].start()
            fetches[which].wait()
            piece = held
        for g in range(rows // 16):
            for column in range(2 * TILES):
                value = piece[g * 16 : (g + 1) * 16, column * LANE : (column + 1) * LANE].astype(F32)
                for h in range(2):
                    flat[pl.ds((2 * g + h) * 8 * PITCH + column, 8, stride=PITCH), :] = value[h * 8 : (h + 1) * 8]
        for r in range(live):
            label = label_ref[tmpl ^ d, r] * versions
            x_cos = flat[r * PITCH : r * PITCH + 8]
            x_sin = flat[r * PITCH + TILES : r * PITCH + TILES + 8]
            slabs[label, 0:8] = x_cos
            slabs[label, 8:16] = x_sin
            for a, (cosine, sine) in enumerate(turns):
                slabs[label + a + 1, 0:8] = x_cos * cosine + x_sin * sine
                slabs[label + a + 1, 8:16] = x_sin * cosine - x_cos * sine

    step = 4

    def several(i, carry):
        for q in range(step):
            k = i * step + q
            real, imag = [None, None], [None, None]
            j = 0
            for u_ref, count in zip(u_refs, counts):
                for own in range(count):
                    c = slab_ref[i * step + (j * templates + q)]
                    at = i * (step * count * PITCH) + (q * count + own) * PITCH
                    u_cos = u_ref[pl.ds(at, 8), :]
                    u_sin = u_ref[pl.ds(at + TILES, 8), :]
                    x_cos = slabs[c, 0:8]
                    x_sin = slabs[c, 8:16]
                    re = u_cos * x_cos + u_sin * x_sin
                    im = u_sin * x_cos - u_cos * x_sin
                    p = j % 2
                    real[p] = re if real[p] is None else real[p] + re
                    imag[p] = im if imag[p] is None else imag[p] + im
                    j += 1
            z[pl.ds(k, 8, stride=templates + 1), :] = real[0] + real[1]
            z[pl.ds(k + 8 * (templates + 1), 8, stride=templates + 1), :] = imag[0] + imag[1]
        return carry

    lax.fori_loop(0, templates // step, several, 0)

    first = lax.broadcasted_iota(jnp.int32, (templates, LANE), 1) == 0
    base = jnp.float32(CH * NS)
    for column in range(2 * TILES):
        row = column if column < TILES else column - TILES + 8
        weight = jnp.float32(2.0) / base
        if column % TILES == 0:
            weight = jnp.where(first, jnp.float32(1.0), jnp.float32(2.0)) / base
        value = z[row * (templates + 1) : row * (templates + 1) + templates, :] * weight
        packed[:, column * LANE : (column + 1) * LANE] = value.astype(BF16)
    table_copy.wait()
    out_ref[...] = jnp.dot(packed[...], inverse[...], preferred_element_type=F32)


def full(space=pltpu.VMEM):
    return pl.BlockSpec(memory_space=space)


def in_hbm(array):
    return pltpu.with_memory_space_constraint(array, pltpu.HBM)


def on_device(raw, ids, fir, taps, channels, shifts):
    win_count = lax.axis_size("win")
    tmpl_count = lax.axis_size("tmpl")
    win = lax.axis_index("win")
    tmpl = lax.axis_index("tmpl")
    slots, raw_t = raw.shape
    templates = taps.shape[0]
    live = 3 * slots * win_count // 5
    rows = -(-live // 16) * 16
    chan_total = live * tmpl_count
    table = forward_tables()
    inverse = jnp.asarray(inverse_table())

    place = jnp.stack([win, tmpl]).astype(jnp.int32)
    blocks = raw_t // (DEC * BLOCK)
    extra = (NS - WIN_DEV) // BLOCK
    mine = pl.pallas_call(
        spectra_kernel,
        out_shape=[jax.ShapeDtypeStruct((slots, NS), BF16)] * win_count,
        in_specs=[full(pltpu.SMEM)] + [full(pltpu.HBM)] * 3,
        out_specs=[full()] * win_count,
        scratch_shapes=[
            pltpu.VMEM((slots, raw_t + SPAN - DEC * BLOCK), BF16),
            pltpu.VMEM((1, NTAP), BF16),
            pltpu.VMEM((2, NS // 2, NF), BF16),
            pltpu.VMEM(((blocks + extra) * slots, BLOCK), BF16),
            pltpu.VMEM((2, win_count * slots, NS // 2), BF16),
            pltpu.SemaphoreType.DMA((4,)),
        ],
        compiler_params=pltpu.CompilerParams(vmem_limit_bytes=24 * MIB),
        name="spectra",
    )(place, in_hbm(raw), in_hbm(fir[None, :]), in_hbm(jnp.asarray(table)))

    parts = [mine[0]]
    for d in range(1, win_count):
        parts.append(lax.ppermute(mine[d], "win", [(i, i ^ d) for i in range(win_count)]))

    packed_rows = pl.pallas_call(
        functools.partial(compact_kernel, tmpl_count),
        out_shape=jax.ShapeDtypeStruct((rows, NS), BF16),
        in_specs=[full(pltpu.SMEM)] + [full()] * (1 + win_count),
        out_specs=full(),
        scratch_shapes=[pltpu.VMEM((win_count * slots, NS), BF16)],
        compiler_params=pltpu.CompilerParams(vmem_limit_bytes=24 * MIB),
        name="compact",
    )(place, ids[None, :], *parts)

    small = chan_total <= 1024
    versions, coarse = (3, 112) if small else (1, MOVE)
    labels, slab_index = pl.pallas_call(
        functools.partial(index_kernel, slots, versions, coarse),
        out_shape=[
            pltpu.HBM((tmpl_count, -(-live // LANE) * LANE), jnp.int32),
            pltpu.HBM((32, templates), jnp.int32),
        ],
        in_specs=[full()] * 3,
        out_specs=[full()] * 2,
        compiler_params=pltpu.CompilerParams(vmem_limit_bytes=8 * MIB),
        name="indices",
    )(ids[None, :], channels.T, shifts.T)

    waves = taps.transpose(1, 2, 0)
    reach = -(-(TL + coarse) // 32) * 16
    counts = (18, 12)
    spectra_of = []
    for n, count in enumerate(counts):
        begin = sum(counts[:n])
        spectra_of.append(
            pl.pallas_call(
                functools.partial(template_kernel, begin, coarse),
                out_shape=jax.ShapeDtypeStruct((templates * count * PITCH + 8, LANE), F32),
                grid=(1,),
                in_specs=[
                    full(),
                    full(pltpu.HBM),
                    pl.BlockSpec((pl.Element(count), pl.Element(TL), pl.Element(templates)), lambda i, begin=begin: (begin, 0, 0)),
                    full(),
                ],
                out_specs=full(),
                scratch_shapes=[pltpu.VMEM((TL, LANE), F32)],
                compiler_params=pltpu.CompilerParams(vmem_limit_bytes=(12 if small else 40) * MIB),
                name="templates",
            )(shifts.T, in_hbm(packed_rows), in_hbm(waves), in_hbm(jnp.asarray(table[:, :reach])))
        )

    held = {0: packed_rows}
    bit = tmpl_count // 2
    while bit:
        for d in list(held):
            source = held[d]
            if d and bit == 1:
                source, spectra_of[0] = lax.optimization_barrier((source, spectra_of[0]))
            held[d | bit] = lax.ppermute(source, "tmpl", [(i, i ^ bit) for i in range(tmpl_count)])
        bit //= 2
    pieces = [held[d] for d in range(tmpl_count)]

    in_main = (0,) if small else tuple(range(tmpl_count))
    places = [pltpu.HBM if d in in_main else pltpu.VMEM for d in range(tmpl_count)]
    return pl.pallas_call(
        functools.partial(stack_kernel, live, versions, counts, in_main),
        out_shape=jax.ShapeDtypeStruct((templates, WIN_DEV), F32),
        in_specs=[full(pltpu.SMEM)] * 3
        + [full(pltpu.HBM), full()]
        + [full()] * len(counts)
        + [full(space) for space in places],
        out_specs=full(),
        scratch_shapes=[
            pltpu.VMEM((2 * NF, WIN_DEV), BF16),
            pltpu.VMEM((rows * PITCH + 8, LANE), F32),
            pltpu.VMEM((chan_total * versions, 16, LANE), F32),
            pltpu.VMEM((16 * (templates + 1), LANE), F32),
            pltpu.VMEM((templates, NS), BF16),
            pltpu.VMEM((rows, NS), BF16),
            pltpu.SemaphoreType.DMA((2,)),
        ],
        compiler_params=pltpu.CompilerParams(vmem_limit_bytes=(19 if small else 58) * MIB),
        name="stacks",
    )(
        place,
        in_hbm(slab_index.reshape(-1)),
        in_hbm(labels),
        in_hbm(inverse),
        jnp.asarray(phase_table(versions, coarse)),
        *spectra_of,
        *[in_hbm(piece) if d in in_main else piece for d, piece in enumerate(pieces)],
    )


def solution(mesh):
    return jax.shard_map(
        on_device,
        mesh=mesh,
        in_specs=(
            P(("win", "tmpl"), None),
            P(),
            P(),
            P("tmpl", None, None),
            P("tmpl", None),
            P("tmpl", None),
        ),
        out_specs=P("tmpl", "win"),
        check_vma=False,
    )
```

time: 55.5 us -> 47.7 us (0.86)
  Pallas kernels: 30.9 us -> 25.8 us
  local copies, waits for them, and re-layouts: 1.65 us -> 0.02 us
  waiting for transfers between devices: 8.06 us -> 6.87 us
    pallas_call x2 -> x4, Pallas kernels: 26.2 us -> 21.1 us  [the longest x2 10.1 us: on_device(): pl.pallas_call(functools.partial(template_kernel, begin, coarse), out_sha...]
    unnamed x12 -> x10, local copies, waits for them, and re-layouts: 1.65 us -> 0.02 us
    ppermute x3, waiting for transfers between devices: 1.2 us -> 0.01 us  [on_device(): lax.ppermute(source, 'tmpl', [(i, i ^ bit) for i in range(tmpl_count)])]
  transfers between devices with their start and end apart: 10 -> 10, of which waited for: 3 -> 2; matrix products, arithmetic and copies ran while one was open for 0% -> 0% of each run, Pallas kernels for 30% -> 25%
where the time goes in v3:
time: 47.7 us; the launch traced here: 47.5 us
  Pallas kernels  25.8 us (54%)
  starting transfers between devices  14.6 us (31%)
  waiting for transfers between devices  6.87 us (14%)
    ppermute x7, starting transfers between devices, on_device(): lax.ppermute(mine[d], 'win', [(i, i ^ d) for i in range(win_count)])  12.5 us
    pallas_call x2, Pallas kernels, on_device(): pl.pallas_call(functools.partial(template_kernel, begin, coarse), out_sha...  10.1 us
    pallas_call x1, Pallas kernels, on_device(): pl.pallas_call(functools.partial(stack_kernel, live, versions, counts, in...  9.43 us
    ppermute x7, waiting for transfers between devices, on_device(): lax.ppermute(mine[d], 'win', [(i, i ^ d) for i in range(win_count)])  6.87 us
    pallas_call x1, Pallas kernels, on_device(): pl.pallas_call(spectra_kernel, out_shape=[jax.ShapeDtypeStruct((slots, NS...  3.64 us
    ppermute x3, starting transfers between devices, on_device(): lax.ppermute(source, 'tmpl', [(i, i ^ bit) for i in range(tmpl_count)])  2.13 us
    pallas_call x1, Pallas kernels, on_device(): pl.pallas_call(functools.partial(index_kernel, slots, versions, coarse),...  1.53 us
    pallas_call x1, Pallas kernels, on_device(): pl.pallas_call(functools.partial(compact_kernel, tmpl_count), out_shape=j...  1.02 us
  transfers between devices with their start and end apart: 10, of which 2 were waited for; matrix products, arithmetic and copies ran while one was open for 0% of the time, Pallas kernels for 25%

profile of v3, /device:TPU:0, one launch (start us, length us, event | category | flops | bytes accessed | tf_op | source)
XLA Modules:
  0.0 47.5 jit_solution(3355778034385978260)
XLA Ops:
  0.0 0.0 copy-start.4
  0.0 0.0 copy-start.1
  0.0 0.1 pad_add_fusion.place_ref
  0.1 3.6 %spectra.1 = (bf16[16,1792]{1,0:T(8,128)(2,1)S(1)}, bf16[16,1792]{1,0:T(8,128)(2,1)S(1)}, bf16[16,1792]{1,0:T(8,128)(2,1)S(1)}, bf16[16,1792]{1,0:T(8,128)(2,1)S...) custom-call(s32[2]{0:T(128)S(1)} %pad_add_fusion.place_ref, ...), custom_call_target="tpu_custom_call" | custom-call | tf_op jit(solution)/shard_map/spectra/pallas_call | solution.py:343
  3.7 3.0 %collective-permute-start = (bf16[16,1792]{1,0:T(8,128)(2,1)S(1)}, bf16[16,1792]{1,0:T(8,128)(2,1)S(1)}, u32[]{:S(2)}, u32[]{:S(2)}) collective-permute-start(bf16[16,1792]{1,0:T(8,128)(2,1)S(1)} %get-tuple-element.20), channel_id=1, source_target_pairs={{0,4},{4,0},{8,12},{12,8},{16,20},{20,16},{24,28},{28,24},{1,5},{5... | collective-permute-start | bytes 172040 | tf_op jit(solution)/shard_map/ppermute | solution.py:362
  6.8 1.6 %collective-permute-start.1 = (bf16[16,1792]{1,0:T(8,128)(2,1)S(1)}, bf16[16,1792]{1,0:T(8,128)(2,1)S(1)}, u32[]{:S(2)}, u32[]{:S(2)}) collective-permute-start(bf16[16,1792]{1,0:T(8,128)(2,1)S(1)} %get-tuple-element.21), channel_id=1, source_target_pairs={{0,8},{4,12},{8,0},{12,4},{16,24},{20,28},{24,16},{28,20},{1,9},{5... | collective-permute-start | bytes 172040 | tf_op jit(solution)/shard_map/ppermute | solution.py:362
  8.3 0.0 collective-permute-start.2
  8.3 3.0 %collective-permute-start.3 = (bf16[16,1792]{1,0:T(8,128)(2,1)S(1)}, bf16[16,1792]{1,0:T(8,128)(2,1)S(1)}, u32[]{:S(2)}, u32[]{:S(2)}) collective-permute-start(bf16[16,1792]{1,0:T(8,128)(2,1)S(1)} %get-tuple-element.23), channel_id=1, source_target_pairs={{0,16},{4,20},{8,24},{12,28},{16,0},{20,4},{24,8},{28,12},{1,17},{... | collective-permute-start | bytes 172040 | tf_op jit(solution)/shard_map/ppermute | solution.py:362
  11.3 1.3 %collective-permute-start.4 = (bf16[16,1792]{1,0:T(8,128)(2,1)S(1)}, bf16[16,1792]{1,0:T(8,128)(2,1)S(1)}, u32[]{:S(2)}, u32[]{:S(2)}) collective-permute-start(bf16[16,1792]{1,0:T(8,128)(2,1)S(1)} %get-tuple-element.24), channel_id=1, source_target_pairs={{0,20},{4,16},{8,28},{12,24},{16,4},{20,0},{24,12},{28,8},{1,21},{... | collective-permute-start | bytes 172040 | tf_op jit(solution)/shard_map/ppermute | solution.py:362
  12.6 0.0 collective-permute-done.rest_1_
  12.6 3.6 %collective-permute-start.5 = (bf16[16,1792]{1,0:T(8,128)(2,1)S(1)}, bf16[16,1792]{1,0:T(8,128)(2,1)S(1)}, u32[]{:S(2)}, u32[]{:S(2)}) collective-permute-start(bf16[16,1792]{1,0:T(8,128)(2,1)S(1)} %get-tuple-element.25), channel_id=1, source_target_pairs={{0,24},{4,28},{8,16},{12,20},{16,8},{20,12},{24,0},{28,4},{1,25},{... | collective-permute-start | bytes 172040 | tf_op jit(solution)/shard_map/ppermute | solution.py:362
  16.2 0.0 collective-permute-done.1.rest_2_
  16.2 0.0 collective-permute-start.6
  16.2 0.0 collective-permute-done.2.rest_3_
  16.2 0.0 collective-permute-done.3.rest_4_
  16.2 4.3 %collective-permute-done.4.rest_5_ = bf16[16,1792]{1,0:T(8,128)(2,1)S(1)} collective-permute-done((bf16[16,1792]{1,0:T(8,128)(2,1)S(1)}, bf16[16,1792]{1,0:T(8,128)(2,1)S(1)}, u32[]{:S(2)}, u32[]{:S(2)}) %collective-permute-start.4) | collective-permute-done | bytes 57376 | tf_op jit(solution)/shard_map/ppermute | solution.py:362
  20.5 0.0 collective-permute-done.5.rest_6_
  20.5 2.6 %collective-permute-done.6.rest_7_ = bf16[16,1792]{1,0:T(8,128)(2,1)S(1)} collective-permute-done((bf16[16,1792]{1,0:T(8,128)(2,1)S(1)}, bf16[16,1792]{1,0:T(8,128)(2,1)S(1)}, u32[]{:S(2)}, u32[]{:S(2)}) %collective-permute-start.6) | collective-permute-done | bytes 57376 | tf_op jit(solution)/shard_map/ppermute | solution.py:362
  23.1 0.0 copy-done.4
  23.1 1.0 %compact.1.after_ref.rest_2_ = bf16[80,1792]{1,0:T(8,128)(2,1)S(1)} custom-call(s32[2]{0:T(128)S(1)} %pad_add_fusion.place_ref, s32[1,512]{1,0:T(1,128)S(1)} %bitcast.12, bf16[16,1792]{1,0:T(8,128)(2,1)S(1)} %get-tuple-element.19.rest_0_, bf16[16,1792]{1,0:T(8,128)(2,1)S(1)} %collective-permute-done.rest_1_, ...), custom_call_target="tpu_custom_call" | custom-call | tf_op jit(solution)/shard_map/compact/pallas_call | solution.py:364
  24.1 0.0 copy-start
  24.1 1.6 %collective-permute-start.7 = (bf16[80,1792]{1,0:T(8,128)(2,1)S(1)}, bf16[80,1792]{1,0:T(8,128)(2,1)S(1)}, u32[]{:S(2)}, u32[]{:S(2)}) collective-permute-start(bf16[80,1792]{1,0:T(8,128)(2,1)S(1)} %compact.1.after_ref.rest_2_), channel_id=1, source_target_pairs={{0,2},{1,3},{2,0},{3,1},{4,6},{5,7},{6,4},{7,5},{8,10},{9,11},{10,... | collective-permute-start | bytes 860168 | tf_op jit(solution)/shard_map/ppermute | solution.py:419
  25.7 0.0 collective-permute-start.8
  25.7 0.0 copy-done
  25.7 0.0 copy-done.1
  25.7 0.0 copy-start.3
  25.7 5.5 %templates.2.rest_0_ = f32[32264,128]{1,0:T(8,128)S(1)} custom-call(s32[30,128]{1,0:T(8,128)S(1)} %bitcast.8, bf16[80,1792]{1,0:T(8,128)(2,1)} %copy-done, bf16[30,400,128]{2,1,0:T(8,128)(2,1)} %bitcast.14, bf16[2,256,896]{2,1,0:T(8,128)(2,1)} %constant.19.clone.table_ref), custom_call_target="tpu_custom_call" | custom-call | tf_op jit(solution)/shard_map/templates/pallas_call | solution.py:395
  31.2 0.0 collective-permute-done.7.rest_4_
  31.2 0.6 %collective-permute-start.9 = (bf16[80,1792]{1,0:T(8,128)(2,1)S(1)}, bf16[80,1792]{1,0:T(8,128)(2,1)S(1)}, u32[]{:S(2)}, u32[]{:S(2)}) collective-permute-start(bf16[80,1792]{1,0:T(8,128)(2,1)S(1)} %collective-permute-done.7.rest_4_), channel_id=1, source_target_pairs={{0,1},{1,0},{2,3},{3,2},{4,5},{5,4},{6,7},{7,6},{8,9},{9,8},{10,11... | collective-permute-start | bytes 860168 | tf_op jit(solution)/shard_map/ppermute | solution.py:419
  31.8 0.0 copy-done.3
  31.8 1.5 %indices.1 = (s32[4,128]{1,0:T(4,128)}, s32[32,128]{1,0:T(8,128)}) custom-call(s32[1,512]{1,0:T(1,128)S(1)} %bitcast.13, s32[30,128]{1,0:T(8,128)S(1)} %bitcast.11, s32[30,128]{1,0:T(8,128)S(1)} %bitcast.9), custom_call_target="tpu_custom_call" | custom-call | tf_op jit(solution)/shard_map/indices/pallas_call | solution.py:376
  33.3 0.0 copy-start.2
  33.3 4.7 %templates.3.rest_1_ = f32[21512,128]{1,0:T(8,128)S(1)} custom-call(s32[30,128]{1,0:T(8,128)S(1)} %bitcast.10, bf16[80,1792]{1,0:T(8,128)(2,1)} %copy-done, bf16[30,400,128]{2,1,0:T(8,128)(2,1)} %bitcast.15, bf16[2,256,896]{2,1,0:T(8,128)(2,1)} %constant.19.clone.table_ref), custom_call_target="tpu_custom_call" | custom-call | tf_op jit(solution)/shard_map/templates/pallas_call | solution.py:395
  38.0 0.0 collective-permute-done.8.rest_3_
  38.0 0.0 collective-permute-done.9.rest_5_
  38.0 0.0 copy-done.2
  38.0 9.4 %stacks.1 = f32[128,1024]{1,0:T(8,128)} custom-call(s32[2]{0:T(128)S(1)} %pad_add_fusion.place_ref, s32[4096]{0:T(1024)} %bitcast.16, s32[4,128]{1,0:T(4,128)} %get-tuple-element.18.label_ref, bf16[1792,1024]{1,0:T(8,128)(2,1)} %constant.17.clone.inverse_hbm, f32[3,16,128]{2,1,0:T(8,128)S(1)} %copy-done.2, f32[32264,128]{1,0:T(8,128)S(1)} %templates.2.rest_0_, ...), custom_call_target="tpu_custom_call" | custom-call | tf_op jit(solution)/shard_map/stacks/pallas_call | solution.py:425
Async XLA Ops:
  0.0 23.1 %copy-start.4 = (s32[512]{0:T(512)S(1)}, s32[512]{0:T(512)}, u32[]{:S(2)}) copy-start(s32[512]{0:T(512)} %param.12) | copy-start | bytes 6148
  0.0 25.7 %copy-start.1 = (s32[128,30]{0,1:T(8,128)S(1)}, s32[128,30]{0,1:T(8,128)}, u32[]{:S(2)}) copy-start(s32[128,30]{0,1:T(8,128)} %param.16) | copy-start | bytes 46084
  3.7 8.9 %collective-permute-start = (bf16[16,1792]{1,0:T(8,128)(2,1)S(1)}, bf16[16,1792]{1,0:T(8,128)(2,1)S(1)}, u32[]{:S(2)}, u32[]{:S(2)}) collective-permute-start(bf16[16,1792]{1,0:T(8,128)(2,1)S(1)} %get-tuple-element.20), channel_id=1, source_target_pairs={{0,4},{4,0},{8,12},{12,8},{16,20},{20,16},{24,28},{28,24},{1,5},{5... | collective-permute-start | bytes 172040 | tf_op jit(solution)/shard_map/ppermute | solution.py:362
  6.8 9.5 %collective-permute-start.1 = (bf16[16,1792]{1,0:T(8,128)(2,1)S(1)}, bf16[16,1792]{1,0:T(8,128)(2,1)S(1)}, u32[]{:S(2)}, u32[]{:S(2)}) collective-permute-start(bf16[16,1792]{1,0:T(8,128)(2,1)S(1)} %get-tuple-element.21), channel_id=1, source_target_pairs={{0,8},{4,12},{8,0},{12,4},{16,24},{20,28},{24,16},{28,20},{1,9},{5... | collective-permute-start | bytes 172040 | tf_op jit(solution)/shard_map/ppermute | solution.py:362
  8.3 7.9 %collective-permute-start.2 = (bf16[16,1792]{1,0:T(8,128)(2,1)S(1)}, bf16[16,1792]{1,0:T(8,128)(2,1)S(1)}, u32[]{:S(2)}, u32[]{:S(2)}) collective-permute-start(bf16[16,1792]{1,0:T(8,128)(2,1)S(1)} %get-tuple-element.22), channel_id=1, source_target_pairs={{0,12},{4,8},{8,4},{12,0},{16,28},{20,24},{24,20},{28,16},{1,13},{... | collective-permute-start | bytes 172040 | tf_op jit(solution)/shard_map/ppermute | solution.py:362
  8.3 7.9 %collective-permute-start.3 = (bf16[16,1792]{1,0:T(8,128)(2,1)S(1)}, bf16[16,1792]{1,0:T(8,128)(2,1)S(1)}, u32[]{:S(2)}, u32[]{:S(2)}) collective-permute-start(bf16[16,1792]{1,0:T(8,128)(2,1)S(1)} %get-tuple-element.23), channel_id=1, source_target_pairs={{0,16},{4,20},{8,24},{12,28},{16,0},{20,4},{24,8},{28,12},{1,17},{... | collective-permute-start | bytes 172040 | tf_op jit(solution)/shard_map/ppermute | solution.py:362
  11.3 9.2 %collective-permute-start.4 = (bf16[16,1792]{1,0:T(8,128)(2,1)S(1)}, bf16[16,1792]{1,0:T(8,128)(2,1)S(1)}, u32[]{:S(2)}, u32[]{:S(2)}) collective-permute-start(bf16[16,1792]{1,0:T(8,128)(2,1)S(1)} %get-tuple-element.24), channel_id=1, source_target_pairs={{0,20},{4,16},{8,28},{12,24},{16,4},{20,0},{24,12},{28,8},{1,21},{... | collective-permute-start | bytes 172040 | tf_op jit(solution)/shard_map/ppermute | solution.py:362
  12.6 7.9 %collective-permute-start.5 = (bf16[16,1792]{1,0:T(8,128)(2,1)S(1)}, bf16[16,1792]{1,0:T(8,128)(2,1)S(1)}, u32[]{:S(2)}, u32[]{:S(2)}) collective-permute-start(bf16[16,1792]{1,0:T(8,128)(2,1)S(1)} %get-tuple-element.25), channel_id=1, source_target_pairs={{0,24},{4,28},{8,16},{12,20},{16,8},{20,12},{24,0},{28,4},{1,25},{... | collective-permute-start | bytes 172040 | tf_op jit(solution)/shard_map/ppermute | solution.py:362
  16.2 6.9 %collective-permute-start.6 = (bf16[16,1792]{1,0:T(8,128)(2,1)S(1)}, bf16[16,1792]{1,0:T(8,128)(2,1)S(1)}, u32[]{:S(2)}, u32[]{:S(2)}) collective-permute-start(bf16[16,1792]{1,0:T(8,128)(2,1)S(1)} %get-tuple-element.26), channel_id=1, source_target_pairs={{0,28},{4,24},{8,20},{12,16},{16,12},{20,8},{24,4},{28,0},{1,29},{... | collective-permute-start | bytes 172040 | tf_op jit(solution)/shard_map/ppermute | solution.py:362
  24.1 1.6 %copy-start = (bf16[80,1792]{1,0:T(8,128)(2,1)}, bf16[80,1792]{1,0:T(8,128)(2,1)S(1)}, u32[]{:S(2)}) copy-start(bf16[80,1792]{1,0:T(8,128)(2,1)S(1)} %compact.1.after_ref.rest_2_) | copy-start | bytes 860164
  24.1 7.1 %collective-permute-start.7 = (bf16[80,1792]{1,0:T(8,128)(2,1)S(1)}, bf16[80,1792]{1,0:T(8,128)(2,1)S(1)}, u32[]{:S(2)}, u32[]{:S(2)}) collective-permute-start(bf16[80,1792]{1,0:T(8,128)(2,1)S(1)} %compact.1.after_ref.rest_2_), channel_id=1, source_target_pairs={{0,2},{1,3},{2,0},{3,1},{4,6},{5,7},{6,4},{7,5},{8,10},{9,11},{10,... | collective-permute-start | bytes 860168 | tf_op jit(solution)/shard_map/ppermute | solution.py:419
  25.7 12.3 %collective-permute-start.8 = (bf16[80,1792]{1,0:T(8,128)(2,1)S(1)}, bf16[80,1792]{1,0:T(8,128)(2,1)S(1)}, u32[]{:S(2)}, u32[]{:S(2)}) collective-permute-start(bf16[80,1792]{1,0:T(8,128)(2,1)S(1)} %compact.1.after_ref.rest_2_), channel_id=1, source_target_pairs={{0,1},{1,0},{2,3},{3,2},{4,5},{5,4},{6,7},{7,6},{8,9},{9,8},{10,11... | collective-permute-start | bytes 860168 | tf_op jit(solution)/shard_map/ppermute | solution.py:419
  25.7 6.1 %copy-start.3 = (s32[128,30]{0,1:T(8,128)S(1)}, s32[128,30]{0,1:T(8,128)}, u32[]{:S(2)}) copy-start(s32[128,30]{0,1:T(8,128)} %param.15) | copy-start | bytes 46084
  31.2 6.8 %collective-permute-start.9 = (bf16[80,1792]{1,0:T(8,128)(2,1)S(1)}, bf16[80,1792]{1,0:T(8,128)(2,1)S(1)}, u32[]{:S(2)}, u32[]{:S(2)}) collective-permute-start(bf16[80,1792]{1,0:T(8,128)(2,1)S(1)} %collective-permute-done.7.rest_4_), channel_id=1, source_target_pairs={{0,1},{1,0},{2,3},{3,2},{4,5},{5,4},{6,7},{7,6},{8,9},{9,8},{10,11... | collective-permute-start | bytes 860168 | tf_op jit(solution)/shard_map/ppermute | solution.py:419
  33.3 4.7 %copy-start.2 = (f32[3,16,128]{2,1,0:T(8,128)S(1)}, f32[3,16,128]{2,1,0:T(8,128)}, u32[]{:S(2)}) copy-start(f32[3,16,128]{2,1,0:T(8,128)} %constant.20.clone.phase_ref) | copy-start | bytes 73732

commit v4 on v3

--- a/solution.py
+++ b/solution.py
@@ -99,10 +99,11 @@
     return slice(2 * q * LANE, min(2 * (q + 1) * LANE, NF))
 
 
-def spectra_kernel(place_ref, raw_hbm, fir_hbm, table_hbm, *rest):
+def spectra_kernel(raw_hbm, fir_hbm, table_hbm, *rest):
     win_count = len(rest) - 6
     outs = rest[:win_count]
     raw, fir, table, filt, tile, sems = rest[win_count:]
+    win = lax.axis_index("win")
     slots, raw_t = raw_hbm.shape
     length = DEC * BLOCK
     blocks = raw_t // length
@@ -128,7 +129,7 @@
     per_tile = NS // BLOCK
     filt[blocks * slots :] = jnp.zeros(((per_tile - per_win) * slots, BLOCK), BF16)
     for d in range(win_count):
-        first = (place_ref[0] ^ d) * per_win
+        first = (win ^ d) * per_win
         for m in range(per_tile):
             start = pl.multiple_of((first + m) * slots, slots)
             block = filt[pl.ds(start, slots), :]
@@ -172,13 +173,14 @@
     return jnp.where(wanted == rank, 1.0, 0.0).astype(BF16)
 
 
-def compact_kernel(tmpl_count, place_ref, ids_ref, *rest):
+def compact_kernel(ids_ref, *rest):
     blocks, out_ref, data = rest[:-2], rest[-2], rest[-1]
     slots = blocks[0].shape[0]
-    high, low = column_ids(ids_ref[...], place_ref[1], tmpl_count, slots)
+    win = lax.axis_index("win")
+    high, low = column_ids(ids_ref[...], lax.axis_index("tmpl"), lax.axis_size("tmpl"), slots)
     pick = picks(high, low, out_ref.shape[0])
     for d, block in enumerate(blocks):
-        start = pl.multiple_of((place_ref[0] ^ d) * slots, slots)
+        start = pl.multiple_of((win ^ d) * slots, slots)
         data[pl.ds(start, slots), :] = block[...]
     out_ref[...] = jnp.dot(pick, data[...], preferred_element_type=F32).astype(BF16)
 
@@ -201,15 +203,24 @@
     return jnp.concatenate(tiles + [zero] * (-most % 2), axis=0)
 
 
-def template_kernel(begin, coarse, shift_ref, after_ref, taps_ref, table_ref, u_ref, wave):
-    templates = taps_ref.shape[2]
-    count = u_ref.shape[0] // (templates * PITCH)
+def template_kernel(begin, coarse, shift_ref, after_ref, taps_hbm, table_hbm, u_ref, taps, table, wave, sems):
+    count, _, templates = taps.shape
     most = (TL + coarse) // 16
-
-    def load(index):
+    loads = []
+    for index in range(count // GROUP):
+        here = slice(index * GROUP, (index + 1) * GROUP)
+        there = slice(begin + index * GROUP, begin + (index + 1) * GROUP)
+        loads.append(pltpu.make_async_copy(taps_hbm.at[there], taps.at[here], sems.at[index + 1]))
+    table_load = pltpu.make_async_copy(table_hbm, table, sems.at[0])
+    loads[0].start()
+    table_load.start()
+    for load in loads[1:]:
+        load.start()
+
+    def halves_of(index):
         halves = [[], []]
         for j in range(index * GROUP, (index + 1) * GROUP):
-            wave[...] = taps_ref[j].astype(F32)
+            wave[...] = taps[j].astype(F32)
             even, odd = wave[pl.ds(0, TL // 2, stride=2), :], wave[pl.ds(1, TL // 2, stride=2), :]
             shift = shift_ref[begin + j : begin + j + 1, :] % coarse
             swap = jnp.broadcast_to((shift & 1) != 0, even.shape)
@@ -218,9 +229,12 @@
         return [jnp.concatenate([jnp.transpose(h.astype(BF16)) for h in half], axis=0) for half in halves]
 
     for index in range(count // GROUP):
-        halves = load(index)
+        loads[index].wait()
+        halves = halves_of(index)
+        if index == 0:
+            table_load.wait()
         for q in range(4):
-            sums = [jnp.dot(halves[p], table_ref[p, :, columns_of(q)], preferred_element_type=F32) for p in range(2)]
+            sums = [jnp.dot(halves[p], table[p, :, columns_of(q)], preferred_element_type=F32) for p in range(2)]
             for column, value in butterfly(q, *sums):
                 for j in range(GROUP):
                     for g in range(templates // 8):
@@ -241,14 +255,14 @@
     slab_ref[CH:, :] = jnp.zeros((slab_ref.shape[0] - CH, slab_ref.shape[1]), jnp.int32)
 
 
-def stack_kernel(live, versions, counts, in_main, place_ref, slab_ref, label_ref, inverse_hbm, phase_ref, *rest):
+def stack_kernel(live, versions, counts, in_main, slab_ref, label_ref, inverse_hbm, phase_ref, *rest):
     u_refs, pieces = rest[: len(counts)], rest[len(counts) : -8]
     out_ref, inverse, flat, slabs, z, packed, held, sems = rest[-8:]
     templates = out_ref.shape[0]
     table_copy = pltpu.make_async_copy(inverse_hbm, inverse, sems.at[0])
     table_copy.start()
     rows = held.shape[0]
-    tmpl = place_ref[1]
+    tmpl = lax.axis_index("tmpl")
     flat[rows * PITCH :, :] = jnp.zeros((8, LANE), F32)
     turns = [(phase_ref[a, 0:8], phase_ref[a, 8:16]) for a in range(1, versions)]
     fetches = [pltpu.make_async_copy(pieces[d], held, sems.at[1]) for d in in_main]
@@ -327,8 +341,6 @@
 def on_device(raw, ids, fir, taps, channels, shifts):
     win_count = lax.axis_size("win")
     tmpl_count = lax.axis_size("tmpl")
-    win = lax.axis_index("win")
-    tmpl = lax.axis_index("tmpl")
     slots, raw_t = raw.shape
     templates = taps.shape[0]
     live = 3 * slots * win_count // 5
@@ -337,13 +349,12 @@
     table = forward_tables()
     inverse = jnp.asarray(inverse_table())
 
-    place = jnp.stack([win, tmpl]).astype(jnp.int32)
     blocks = raw_t // (DEC * BLOCK)
     extra = (NS - WIN_DEV) // BLOCK
     mine = pl.pallas_call(
         spectra_kernel,
         out_shape=[jax.ShapeDtypeStruct((slots, NS), BF16)] * win_count,
-        in_specs=[full(pltpu.SMEM)] + [full(pltpu.HBM)] * 3,
+        in_specs=[full(pltpu.HBM)] * 3,
         out_specs=[full()] * win_count,
         scratch_shapes=[
             pltpu.VMEM((slots, raw_t + SPAN - DEC * BLOCK), BF16),
@@ -355,24 +366,55 @@
         ],
         compiler_params=pltpu.CompilerParams(vmem_limit_bytes=24 * MIB),
         name="spectra",
-    )(place, in_hbm(raw), in_hbm(fir[None, :]), in_hbm(jnp.asarray(table)))
-
-    parts = [mine[0]]
-    for d in range(1, win_count):
-        parts.append(lax.ppermute(mine[d], "win", [(i, i ^ d) for i in range(win_count)]))
+    )(in_hbm(raw), in_hbm(fir[None, :]), in_hbm(jnp.asarray(table)))
+
+    small = chan_total <= 1024
+    versions, coarse = (3, 112) if small else (1, MOVE)
+    waves = in_hbm(taps.transpose(1, 2, 0))
+    reach = -(-(TL + coarse) // 32) * 16
+    head = in_hbm(jnp.asarray(table[:, :reach]))
+    counts = (12, 18)
+
+    def template_spectra(n, after):
+        count = counts[n]
+        return pl.pallas_call(
+            functools.partial(template_kernel, sum(counts[:n]), coarse),
+            out_shape=jax.ShapeDtypeStruct((templates * count * PITCH + 8, LANE), F32),
+            in_specs=[full()] + [full(pl.ANY)] + [full(pltpu.HBM)] * 2,
+            out_specs=full(),
+            scratch_shapes=[
+                pltpu.VMEM((count, TL, templates), BF16),
+                pltpu.VMEM((2, reach, NF), BF16),
+                pltpu.VMEM((TL, LANE), F32),
+                pltpu.SemaphoreType.DMA((1 + count // GROUP,)),
+            ],
+            compiler_params=pltpu.CompilerParams(vmem_limit_bytes=(12 if small else 40) * MIB),
+            name="templates",
+        )(shifts.T, after, waves, head)
+
+    def exchanged(block, d):
+        return lax.ppermute(block, "win", [(i, i ^ d) for i in range(win_count)])
+
+    parts = {0: mine[0]}
+    for d in range(win_count - 1, 2, -1):
+        parts[d] = exchanged(mine[d], d)
+    early = template_spectra(0, mine[0])
+    *near, early = lax.optimization_barrier((mine[2], mine[1], early))
+    for d, block in zip((2, 1), near):
+        parts[d] = exchanged(block, d)
+    parts = [parts[d] for d in range(win_count)]
 
     packed_rows = pl.pallas_call(
-        functools.partial(compact_kernel, tmpl_count),
+        compact_kernel,
         out_shape=jax.ShapeDtypeStruct((rows, NS), BF16),
-        in_specs=[full(pltpu.SMEM)] + [full()] * (1 + win_count),
+        in_specs=[full()] * (1 + win_count),
         out_specs=full(),
         scratch_shapes=[pltpu.VMEM((win_count * slots, NS), BF16)],
         compiler_params=pltpu.CompilerParams(vmem_limit_bytes=24 * MIB),
         name="compact",
-    )(place, ids[None, :], *parts)
-
-    small = chan_total <= 1024
-    versions, coarse = (3, 112) if small else (1, MOVE)
+    )(ids[None, :], *parts)
+
+    late = template_spectra(1, packed_rows)
     labels, slab_index = pl.pallas_call(
         functools.partial(index_kernel, slots, versions, coarse),
         out_shape=[
@@ -385,37 +427,13 @@
         name="indices",
     )(ids[None, :], channels.T, shifts.T)
 
-    waves = taps.transpose(1, 2, 0)
-    reach = -(-(TL + coarse) // 32) * 16
-    counts = (18, 12)
-    spectra_of = []
-    for n, count in enumerate(counts):
-        begin = sum(counts[:n])
-        spectra_of.append(
-            pl.pallas_call(
-                functools.partial(template_kernel, begin, coarse),
-                out_shape=jax.ShapeDtypeStruct((templates * count * PITCH + 8, LANE), F32),
-                grid=(1,),
-                in_specs=[
-                    full(),
-                    full(pltpu.HBM),
-                    pl.BlockSpec((pl.Element(count), pl.Element(TL), pl.Element(templates)), lambda i, begin=begin: (begin, 0, 0)),
-                    full(),
-                ],
-                out_specs=full(),
-                scratch_shapes=[pltpu.VMEM((TL, LANE), F32)],
-                compiler_params=pltpu.CompilerParams(vmem_limit_bytes=(12 if small else 40) * MIB),
-                name="templates",
-            )(shifts.T, in_hbm(packed_rows), in_hbm(waves), in_hbm(jnp.asarray(table[:, :reach])))
-        )
-
     held = {0: packed_rows}
     bit = tmpl_count // 2
     while bit:
         for d in list(held):
             source = held[d]
             if d and bit == 1:
-                source, spectra_of[0] = lax.optimization_barrier((source, spectra_of[0]))
+                source, late = lax.optimization_barrier((source, late))
             held[d | bit] = lax.ppermute(source, "tmpl", [(i, i ^ bit) for i in range(tmpl_count)])
         bit //= 2
     pieces = [held[d] for d in range(tmpl_count)]
@@ -425,7 +443,7 @@
     return pl.pallas_call(
         functools.partial(stack_kernel, live, versions, counts, in_main),
         out_shape=jax.ShapeDtypeStruct((templates, WIN_DEV), F32),
-        in_specs=[full(pltpu.SMEM)] * 3
+        in_specs=[full(pltpu.SMEM)] * 2
         + [full(pltpu.HBM), full()]
         + [full()] * len(counts)
         + [full(space) for space in places],
@@ -442,12 +460,12 @@
         compiler_params=pltpu.CompilerParams(vmem_limit_bytes=(19 if small else 58) * MIB),
         name="stacks",
     )(
-        place,
         in_hbm(slab_index.reshape(-1)),
         in_hbm(labels),
         in_hbm(inverse),
         jnp.asarray(phase_table(versions, coarse)),
-        *spectra_of,
+        early,
+        late,
         *[in_hbm(piece) if d in in_main else piece for d, piece in enumerate(pieces)],
     )
 

time: 47.7 us -> 44.9 us (0.941)
  waiting for transfers between devices: 6.87 us -> 4.17 us
    ppermute x7, waiting for transfers between devices: 6.87 us -> 4.16 us  [exchanged(): return lax.ppermute(block, 'win', [(i, i ^ d) for i in range(win_count)])]
    pallas_call x1, Pallas kernels: 3.64 us -> 3.11 us  [on_device(): pl.pallas_call(spectra_kernel, out_shape=[jax.ShapeDtypeStruct((slots, NS...]
    pallas_call x3, Pallas kernels: 11.2 us -> 11.7 us  [the longest x2 11.2 us: template_spectra(): pl.pallas_call(functools.partial(template_kernel, sum(counts[:n]), coarse...]
  transfers between devices with their start and end apart: 10 -> 10, of which waited for: 2 -> 2; matrix products, arithmetic and copies ran while one was open for 0% -> 0% of each run, Pallas kernels for 25% -> 29%
where the time goes in v4:
time: 44.9 us; the launch traced here: 44.6 us
  Pallas kernels  25.9 us (58%)
  starting transfers between devices  14.4 us (32%)
  waiting for transfers between devices  4.17 us (9%)
    ppermute x7, starting transfers between devices, exchanged(): return lax.ppermute(block, 'win', [(i, i ^ d) for i in range(win_count)])  12.3 us
    pallas_call x2, Pallas kernels, template_spectra(): pl.pallas_call(functools.partial(template_kernel, sum(counts[:n]), coarse...  11.2 us
    pallas_call x1, Pallas kernels, on_device(): pl.pallas_call(functools.partial(stack_kernel, live, versions, counts, in...  9.59 us
    ppermute x7, waiting for transfers between devices, exchanged(): return lax.ppermute(block, 'win', [(i, i ^ d) for i in range(win_count)])  4.16 us
    pallas_call x1, Pallas kernels, on_device(): pl.pallas_call(spectra_kernel, out_shape=[jax.ShapeDtypeStruct((slots, NS...  3.11 us
    ppermute x3, starting transfers between devices, on_device(): lax.ppermute(source, 'tmpl', [(i, i ^ bit) for i in range(tmpl_count)])  2.14 us
    pallas_call x1, Pallas kernels, on_device(): pl.pallas_call(functools.partial(index_kernel, slots, versions, coarse),...  1.53 us
  transfers between devices with their start and end apart: 10, of which 2 were waited for; matrix products, arithmetic and copies ran while one was open for 0% of the time, Pallas kernels for 29%

profile of v4, /device:TPU:0, one launch (start us, length us, event | category | flops | bytes accessed | tf_op | source)
XLA Modules:
  0.0 44.6 jit_solution(1979643755249426141)
XLA Ops:
  0.0 0.0 copy-start.1
  0.0 3.1 %spectra.1 = (bf16[16,1792]{1,0:T(8,128)(2,1)S(1)}, bf16[16,1792]{1,0:T(8,128)(2,1)S(1)}, bf16[16,1792]{1,0:T(8,128)(2,1)S(1)}, bf16[16,1792]{1,0:T(8,128)(2,1)S...) custom-call(bf16[16,16384]{1,0:T(8,128)(2,1)} %raw_hbm.1, ...), custom_call_target="tpu_custom_call" | custom-call | tf_op jit(solution)/shard_map/spectra/pallas_call | solution.py:354
  3.1 4.0 %collective-permute-start.2 = (bf16[16,1792]{1,0:T(8,128)(2,1)S(1)}, bf16[16,1792]{1,0:T(8,128)(2,1)S(1)}, u32[]{:S(2)}, u32[]{:S(2)}) collective-permute-start(bf16[16,1792]{1,0:T(8,128)(2,1)S(1)} %get-tuple-element.28), channel_id=1, source_target_pairs={{0,12},{4,8},{8,4},{12,0},{16,28},{20,24},{24,20},{28,16},{1,13},{... | collective-permute-start | bytes 172040 | tf_op jit(solution)/shard_map/ppermute | solution.py:396
  7.2 2.6 %collective-permute-start.3 = (bf16[16,1792]{1,0:T(8,128)(2,1)S(1)}, bf16[16,1792]{1,0:T(8,128)(2,1)S(1)}, u32[]{:S(2)}, u32[]{:S(2)}) collective-permute-start(bf16[16,1792]{1,0:T(8,128)(2,1)S(1)} %get-tuple-element.29), channel_id=1, source_target_pairs={{0,16},{4,20},{8,24},{12,28},{16,0},{20,4},{24,8},{28,12},{1,17},{... | collective-permute-start | bytes 172040 | tf_op jit(solution)/shard_map/ppermute | solution.py:396
  9.8 0.3 collective-permute-start.4
  10.0 2.5 %collective-permute-start.5 = (bf16[16,1792]{1,0:T(8,128)(2,1)S(1)}, bf16[16,1792]{1,0:T(8,128)(2,1)S(1)}, u32[]{:S(2)}, u32[]{:S(2)}) collective-permute-start(bf16[16,1792]{1,0:T(8,128)(2,1)S(1)} %get-tuple-element.31), channel_id=1, source_target_pairs={{0,24},{4,28},{8,16},{12,20},{16,8},{20,12},{24,0},{28,4},{1,25},{... | collective-permute-start | bytes 172040 | tf_op jit(solution)/shard_map/ppermute | solution.py:396
  12.5 2.3 %collective-permute-start.6 = (bf16[16,1792]{1,0:T(8,128)(2,1)S(1)}, bf16[16,1792]{1,0:T(8,128)(2,1)S(1)}, u32[]{:S(2)}, u32[]{:S(2)}) collective-permute-start(bf16[16,1792]{1,0:T(8,128)(2,1)S(1)} %get-tuple-element.32), channel_id=1, source_target_pairs={{0,28},{4,24},{8,20},{12,16},{16,12},{20,8},{24,4},{28,0},{1,29},{... | collective-permute-start | bytes 172040 | tf_op jit(solution)/shard_map/ppermute | solution.py:396
  14.8 0.0 copy-done.1
  14.8 0.0 copy-start.4
  14.8 4.9 %templates.2.rest_0_ = f32[21512,128]{1,0:T(8,128)S(1)} custom-call(s32[30,128]{1,0:T(8,128)S(1)} %bitcast.6, bf16[16,1792]{1,0:T(8,128)(2,1)S(1)} %get-tuple-element.24.after_ref.rest_0_, bf16[30,400,128]{2,1,0:T(8,128)(2,1)} %bitcast.12, bf16[2,256,896]{2,1,0:T(8,128)(2,1)} %constant.10.clone.table_hbm), custom_call_target="tpu_custom_call" | custom-call | tf_op jit(solution)/shard_map/templates/pallas_call | solution.py:380
  19.7 0.0 collective-permute-done.2.rest_3_
  19.8 0.6 %collective-permute-start = (bf16[16,1792]{1,0:T(8,128)(2,1)S(1)}, bf16[16,1792]{1,0:T(8,128)(2,1)S(1)}, u32[]{:S(2)}, u32[]{:S(2)}) collective-permute-start(bf16[16,1792]{1,0:T(8,128)(2,1)S(1)} %get-tuple-element.26), channel_id=1, source_target_pairs={{0,4},{4,0},{8,12},{12,8},{16,20},{20,16},{24,28},{28,24},{1,5},{5... | collective-permute-start | bytes 172040 | tf_op jit(solution)/shard_map/ppermute | solution.py:396
  20.3 0.0 collective-permute-done.3.rest_4_
  20.3 0.0 collective-permute-start.1
  20.3 0.0 collective-permute-done.4.rest_5_
  20.3 0.0 collective-permute-done.5.rest_6_
  20.3 0.0 collective-permute-done.6.rest_7_
  20.4 3.6 %collective-permute-done.rest_1_ = bf16[16,1792]{1,0:T(8,128)(2,1)S(1)} collective-permute-done((bf16[16,1792]{1,0:T(8,128)(2,1)S(1)}, bf16[16,1792]{1,0:T(8,128)(2,1)S(1)}, u32[]{:S(2)}, u32[]{:S(2)}) %collective-permute-start) | collective-permute-done | bytes 57376 | tf_op jit(solution)/shard_map/ppermute | solution.py:396
  24.0 0.5 %collective-permute-done.1.rest_2_ = bf16[16,1792]{1,0:T(8,128)(2,1)S(1)} collective-permute-done((bf16[16,1792]{1,0:T(8,128)(2,1)S(1)}, bf16[16,1792]{1,0:T(8,128)(2,1)S(1)}, u32[]{:S(2)}, u32[]{:S(2)}) %collective-permute-start.1) | collective-permute-done | bytes 57376 | tf_op jit(solution)/shard_map/ppermute | solution.py:396
  24.5 0.0 copy-done.4
  24.5 0.5 %compact.1.after_ref.rest_2_ = bf16[80,1792]{1,0:T(8,128)(2,1)S(1)} custom-call(s32[1,512]{1,0:T(1,128)S(1)} %bitcast.10, bf16[16,1792]{1,0:T(8,128)(2,1)S(1)} %get-tuple-element.24.after_ref.rest_0_, bf16[16,1792]{1,0:T(8,128)(2,1)S(1)} %collective-permute-done.rest_1_, bf16[16,1792]{1,0:T(8,128)(2,1)S(1)} %collective-permute-done.1.rest_2_, ...), custom_call_target="tpu_custom_call" | custom-call | tf_op jit(solution)/shard_map/compact/pallas_call | solution.py:407
  25.0 0.0 copy-start
  25.0 0.0 copy-start.3
  25.0 0.0 copy-start.2
  25.0 1.6 %collective-permute-start.7 = (bf16[80,1792]{1,0:T(8,128)(2,1)S(1)}, bf16[80,1792]{1,0:T(8,128)(2,1)S(1)}, u32[]{:S(2)}, u32[]{:S(2)}) collective-permute-start(bf16[80,1792]{1,0:T(8,128)(2,1)S(1)} %compact.1.after_ref.rest_2_), channel_id=1, source_target_pairs={{0,2},{1,3},{2,0},{3,1},{4,6},{5,7},{6,4},{7,5},{8,10},{9,11},{10,... | collective-permute-start | bytes 860168 | tf_op jit(solution)/shard_map/ppermute | solution.py:437
  26.6 0.0 collective-permute-start.8
  26.6 6.3 %templates.3.rest_1_ = f32[32264,128]{1,0:T(8,128)S(1)} custom-call(s32[30,128]{1,0:T(8,128)S(1)} %bitcast.7, bf16[80,1792]{1,0:T(8,128)(2,1)S(1)} %compact.1.after_ref.rest_2_, bf16[30,400,128]{2,1,0:T(8,128)(2,1)} %bitcast.13, bf16[2,256,896]{2,1,0:T(8,128)(2,1)} %constant.10.clone.table_hbm), custom_call_target="tpu_custom_call" | custom-call | tf_op jit(solution)/shard_map/templates/pallas_call | solution.py:380
  32.9 0.0 copy-done
  32.9 0.0 collective-permute-done.7.rest_4_
  32.9 0.6 %collective-permute-start.9 = (bf16[80,1792]{1,0:T(8,128)(2,1)S(1)}, bf16[80,1792]{1,0:T(8,128)(2,1)S(1)}, u32[]{:S(2)}, u32[]{:S(2)}) collective-permute-start(bf16[80,1792]{1,0:T(8,128)(2,1)S(1)} %collective-permute-done.7.rest_4_), channel_id=1, source_target_pairs={{0,1},{1,0},{2,3},{3,2},{4,5},{5,4},{6,7},{7,6},{8,9},{9,8},{10,11... | collective-permute-start | bytes 860168 | tf_op jit(solution)/shard_map/ppermute | solution.py:437
  33.5 0.0 copy-done.3
  33.5 1.5 %indices.1 = (s32[4,128]{1,0:T(4,128)}, s32[32,128]{1,0:T(8,128)}) custom-call(s32[1,512]{1,0:T(1,128)S(1)} %bitcast.11, s32[30,128]{1,0:T(8,128)S(1)} %bitcast.9, s32[30,128]{1,0:T(8,128)S(1)} %bitcast.8), custom_call_target="tpu_custom_call" | custom-call | tf_op jit(solution)/shard_map/indices/pallas_call | solution.py:418
  35.0 0.0 collective-permute-done.8.rest_3_
  35.0 0.0 collective-permute-done.9.rest_5_
  35.0 0.0 copy-done.2
  35.0 9.6 %stacks.1 = f32[128,1024]{1,0:T(8,128)} custom-call(s32[4096]{0:T(1024)} %bitcast.14, s32[4,128]{1,0:T(4,128)} %get-tuple-element.21.label_ref, bf16[1792,1024]{1,0:T(8,128)(2,1)} %constant.8.clone.inverse_hbm, f32[3,16,128]{2,1,0:T(8,128)S(1)} %copy-done.2, f32[21512,128]{1,0:T(8,128)S(1)} %templates.2.rest_0_, f32[32264,128]{1,0:T(8,128)S(1)} %templates.3.rest_1_, ...), custom_call_target="tpu_custom_call" | custom-call | tf_op jit(solution)/shard_map/stacks/pallas_call | solution.py:443
Async XLA Ops:
  0.0 14.8 %copy-start.1 = (s32[128,30]{0,1:T(8,128)S(1)}, s32[128,30]{0,1:T(8,128)}, u32[]{:S(2)}) copy-start(s32[128,30]{0,1:T(8,128)} %param.15) | copy-start | bytes 46084
  3.1 16.6 %collective-permute-start.2 = (bf16[16,1792]{1,0:T(8,128)(2,1)S(1)}, bf16[16,1792]{1,0:T(8,128)(2,1)S(1)}, u32[]{:S(2)}, u32[]{:S(2)}) collective-permute-start(bf16[16,1792]{1,0:T(8,128)(2,1)S(1)} %get-tuple-element.28), channel_id=1, source_target_pairs={{0,12},{4,8},{8,4},{12,0},{16,28},{20,24},{24,20},{28,16},{1,13},{... | collective-permute-start | bytes 172040 | tf_op jit(solution)/shard_map/ppermute | solution.py:396
  7.2 13.2 %collective-permute-start.3 = (bf16[16,1792]{1,0:T(8,128)(2,1)S(1)}, bf16[16,1792]{1,0:T(8,128)(2,1)S(1)}, u32[]{:S(2)}, u32[]{:S(2)}) collective-permute-start(bf16[16,1792]{1,0:T(8,128)(2,1)S(1)} %get-tuple-element.29), channel_id=1, source_target_pairs={{0,16},{4,20},{8,24},{12,28},{16,0},{20,4},{24,8},{28,12},{1,17},{... | collective-permute-start | bytes 172040 | tf_op jit(solution)/shard_map/ppermute | solution.py:396
  9.8 10.6 %collective-permute-start.4 = (bf16[16,1792]{1,0:T(8,128)(2,1)S(1)}, bf16[16,1792]{1,0:T(8,128)(2,1)S(1)}, u32[]{:S(2)}, u32[]{:S(2)}) collective-permute-start(bf16[16,1792]{1,0:T(8,128)(2,1)S(1)} %get-tuple-element.30), channel_id=1, source_target_pairs={{0,20},{4,16},{8,28},{12,24},{16,4},{20,0},{24,12},{28,8},{1,21},{... | collective-permute-start | bytes 172040 | tf_op jit(solution)/shard_map/ppermute | solution.py:396
  10.0 10.3 %collective-permute-start.5 = (bf16[16,1792]{1,0:T(8,128)(2,1)S(1)}, bf16[16,1792]{1,0:T(8,128)(2,1)S(1)}, u32[]{:S(2)}, u32[]{:S(2)}) collective-permute-start(bf16[16,1792]{1,0:T(8,128)(2,1)S(1)} %get-tuple-element.31), channel_id=1, source_target_pairs={{0,24},{4,28},{8,16},{12,20},{16,8},{20,12},{24,0},{28,4},{1,25},{... | collective-permute-start | bytes 172040 | tf_op jit(solution)/shard_map/ppermute | solution.py:396
  12.5 7.8 %collective-permute-start.6 = (bf16[16,1792]{1,0:T(8,128)(2,1)S(1)}, bf16[16,1792]{1,0:T(8,128)(2,1)S(1)}, u32[]{:S(2)}, u32[]{:S(2)}) collective-permute-start(bf16[16,1792]{1,0:T(8,128)(2,1)S(1)} %get-tuple-element.32), channel_id=1, source_target_pairs={{0,28},{4,24},{8,20},{12,16},{16,12},{20,8},{24,4},{28,0},{1,29},{... | collective-permute-start | bytes 172040 | tf_op jit(solution)/shard_map/ppermute | solution.py:396
  14.8 9.7 %copy-start.4 = (s32[512]{0:T(512)S(1)}, s32[512]{0:T(512)}, u32[]{:S(2)}) copy-start(s32[512]{0:T(512)} %param.11) | copy-start | bytes 6148
  19.8 4.2 %collective-permute-start = (bf16[16,1792]{1,0:T(8,128)(2,1)S(1)}, bf16[16,1792]{1,0:T(8,128)(2,1)S(1)}, u32[]{:S(2)}, u32[]{:S(2)}) collective-permute-start(bf16[16,1792]{1,0:T(8,128)(2,1)S(1)} %get-tuple-element.26), channel_id=1, source_target_pairs={{0,4},{4,0},{8,12},{12,8},{16,20},{20,16},{24,28},{28,24},{1,5},{5... | collective-permute-start | bytes 172040 | tf_op jit(solution)/shard_map/ppermute | solution.py:396
  20.3 4.2 %collective-permute-start.1 = (bf16[16,1792]{1,0:T(8,128)(2,1)S(1)}, bf16[16,1792]{1,0:T(8,128)(2,1)S(1)}, u32[]{:S(2)}, u32[]{:S(2)}) collective-permute-start(bf16[16,1792]{1,0:T(8,128)(2,1)S(1)} %get-tuple-element.27), channel_id=1, source_target_pairs={{0,8},{4,12},{8,0},{12,4},{16,24},{20,28},{24,16},{28,20},{1,9},{5... | collective-permute-start | bytes 172040 | tf_op jit(solution)/shard_map/ppermute | solution.py:396
  25.0 7.9 %copy-start = (bf16[80,1792]{1,0:T(8,128)(2,1)}, bf16[80,1792]{1,0:T(8,128)(2,1)S(1)}, u32[]{:S(2)}) copy-start(bf16[80,1792]{1,0:T(8,128)(2,1)S(1)} %compact.1.after_ref.rest_2_) | copy-start | bytes 860164
  25.0 8.5 %copy-start.3 = (s32[128,30]{0,1:T(8,128)S(1)}, s32[128,30]{0,1:T(8,128)}, u32[]{:S(2)}) copy-start(s32[128,30]{0,1:T(8,128)} %param.14) | copy-start | bytes 46084
  25.0 10.0 %copy-start.2 = (f32[3,16,128]{2,1,0:T(8,128)S(1)}, f32[3,16,128]{2,1,0:T(8,128)}, u32[]{:S(2)}) copy-start(f32[3,16,128]{2,1,0:T(8,128)} %constant.11.clone.phase_ref) | copy-start | bytes 73732
  25.0 7.9 %collective-permute-start.7 = (bf16[80,1792]{1,0:T(8,128)(2,1)S(1)}, bf16[80,1792]{1,0:T(8,128)(2,1)S(1)}, u32[]{:S(2)}, u32[]{:S(2)}) collective-permute-start(bf16[80,1792]{1,0:T(8,128)(2,1)S(1)} %compact.1.after_ref.rest_2_), channel_id=1, source_target_pairs={{0,2},{1,3},{2,0},{3,1},{4,6},{5,7},{6,4},{7,5},{8,10},{9,11},{10,... | collective-permute-start | bytes 860168 | tf_op jit(solution)/shard_map/ppermute | solution.py:437
  26.6 8.4 %collective-permute-start.8 = (bf16[80,1792]{1,0:T(8,128)(2,1)S(1)}, bf16[80,1792]{1,0:T(8,128)(2,1)S(1)}, u32[]{:S(2)}, u32[]{:S(2)}) collective-permute-start(bf16[80,1792]{1,0:T(8,128)(2,1)S(1)} %compact.1.after_ref.rest_2_), channel_id=1, source_target_pairs={{0,1},{1,0},{2,3},{3,2},{4,5},{5,4},{6,7},{7,6},{8,9},{9,8},{10,11... | collective-permute-start | bytes 860168 | tf_op jit(solution)/shard_map/ppermute | solution.py:437
  32.9 2.1 %collective-permute-start.9 = (bf16[80,1792]{1,0:T(8,128)(2,1)S(1)}, bf16[80,1792]{1,0:T(8,128)(2,1)S(1)}, u32[]{:S(2)}, u32[]{:S(2)}) collective-permute-start(bf16[80,1792]{1,0:T(8,128)(2,1)S(1)} %collective-permute-done.7.rest_4_), channel_id=1, source_target_pairs={{0,1},{1,0},{2,3},{3,2},{4,5},{5,4},{6,7},{7,6},{8,9},{9,8},{10,11... | collective-permute-start | bytes 860168 | tf_op jit(solution)/shard_map/ppermute | solution.py:437

commit v5 on v4

--- a/solution.py
+++ b/solution.py
@@ -203,24 +203,21 @@
     return jnp.concatenate(tiles + [zero] * (-most % 2), axis=0)
 
 
-def template_kernel(begin, coarse, shift_ref, after_ref, taps_hbm, table_hbm, u_ref, taps, table, wave, sems):
-    count, _, templates = taps.shape
+def indexing_kernel(begin, coarse, index_sizes, shift_ref, *rest):
+    ids_ref, channel_ref, taps_ref, table_ref, u_ref, label_ref, slab_ref, wave = rest[-8:]
+    index_kernel(*index_sizes, coarse, ids_ref, channel_ref, shift_ref, label_ref, slab_ref)
+    template_kernel(begin, coarse, shift_ref, taps_ref, table_ref, u_ref, wave)
+
+
+def template_kernel(begin, coarse, shift_ref, *rest):
+    taps_ref, table_ref, u_ref, wave = rest[-4:]
+    count, _, templates = taps_ref.shape
     most = (TL + coarse) // 16
-    loads = []
-    for index in range(count // GROUP):
-        here = slice(index * GROUP, (index + 1) * GROUP)
-        there = slice(begin + index * GROUP, begin + (index + 1) * GROUP)
-        loads.append(pltpu.make_async_copy(taps_hbm.at[there], taps.at[here], sems.at[index + 1]))
-    table_load = pltpu.make_async_copy(table_hbm, table, sems.at[0])
-    loads[0].start()
-    table_load.start()
-    for load in loads[1:]:
-        load.start()
 
     def halves_of(index):
         halves = [[], []]
         for j in range(index * GROUP, (index + 1) * GROUP):
-            wave[...] = taps[j].astype(F32)
+            wave[...] = taps_ref[j].astype(F32)
             even, odd = wave[pl.ds(0, TL // 2, stride=2), :], wave[pl.ds(1, TL // 2, stride=2), :]
             shift = shift_ref[begin + j : begin + j + 1, :] % coarse
             swap = jnp.broadcast_to((shift & 1) != 0, even.shape)
@@ -229,12 +226,9 @@
         return [jnp.concatenate([jnp.transpose(h.astype(BF16)) for h in half], axis=0) for half in halves]
 
     for index in range(count // GROUP):
-        loads[index].wait()
         halves = halves_of(index)
-        if index == 0:
-            table_load.wait()
         for q in range(4):
-            sums = [jnp.dot(halves[p], table[p, :, columns_of(q)], preferred_element_type=F32) for p in range(2)]
+            sums = [jnp.dot(halves[p], table_ref[p, :, columns_of(q)], preferred_element_type=F32) for p in range(2)]
             for column, value in butterfly(q, *sums):
                 for j in range(GROUP):
                     for g in range(templates // 8):
@@ -373,35 +367,44 @@
     waves = in_hbm(taps.transpose(1, 2, 0))
     reach = -(-(TL + coarse) // 32) * 16
     head = in_hbm(jnp.asarray(table[:, :reach]))
-    counts = (12, 18)
-
-    def template_spectra(n, after):
+    counts = (9, 18, 3)
+    label_width = -(-live // LANE) * LANE
+
+    def template_spectra(n, *afters):
         count = counts[n]
+        kernel = functools.partial(template_kernel, sum(counts[:n]), coarse)
+        out_shape = jax.ShapeDtypeStruct((templates * count * PITCH + 8, LANE), F32)
+        more, indices, out_specs = (), [], full()
+        if n == 0:
+            kernel = functools.partial(indexing_kernel, 0, coarse, (slots, versions))
+            out_shape = [
+                out_shape,
+                pltpu.HBM((tmpl_count, label_width), jnp.int32),
+                pltpu.HBM((32, templates), jnp.int32),
+            ]
+            more, out_specs = (ids[None, :], channels.T), [full()] * 3
+        begin = sum(counts[:n])
+        taps_block = pl.BlockSpec(
+            (pl.Element(count), pl.Element(TL), pl.Element(templates)), lambda i, begin=begin: (begin, 0, 0)
+        )
         return pl.pallas_call(
-            functools.partial(template_kernel, sum(counts[:n]), coarse),
-            out_shape=jax.ShapeDtypeStruct((templates * count * PITCH + 8, LANE), F32),
-            in_specs=[full()] + [full(pl.ANY)] + [full(pltpu.HBM)] * 2,
-            out_specs=full(),
-            scratch_shapes=[
-                pltpu.VMEM((count, TL, templates), BF16),
-                pltpu.VMEM((2, reach, NF), BF16),
-                pltpu.VMEM((TL, LANE), F32),
-                pltpu.SemaphoreType.DMA((1 + count // GROUP,)),
-            ],
+            kernel,
+            out_shape=out_shape,
+            grid=(1,),
+            in_specs=[full()] + [full(pl.ANY)] * len(afters) + [full()] * len(more) + [taps_block, full()],
+            out_specs=out_specs,
+            scratch_shapes=[pltpu.VMEM((TL, LANE), F32)],
             compiler_params=pltpu.CompilerParams(vmem_limit_bytes=(12 if small else 40) * MIB),
             name="templates",
-        )(shifts.T, after, waves, head)
-
-    def exchanged(block, d):
-        return lax.ppermute(block, "win", [(i, i ^ d) for i in range(win_count)])
+        )(shifts.T, *afters, *more, waves, head)
 
     parts = {0: mine[0]}
-    for d in range(win_count - 1, 2, -1):
-        parts[d] = exchanged(mine[d], d)
-    early = template_spectra(0, mine[0])
-    *near, early = lax.optimization_barrier((mine[2], mine[1], early))
-    for d, block in zip((2, 1), near):
-        parts[d] = exchanged(block, d)
+    near = [d for d in (1, 2) if d < win_count]
+    far = [d for d in range(win_count - 1, 0, -1) if d not in near]
+    for d in near + far:
+        parts[d] = lax.ppermute(mine[d], "win", [(i, i ^ d) for i in range(win_count)])
+    early, labels, slab_index = template_spectra(0, *[parts[d] for d in near])
+    parts, early, labels, slab_index = lax.optimization_barrier((parts, early, labels, slab_index))
     parts = [parts[d] for d in range(win_count)]
 
     packed_rows = pl.pallas_call(
@@ -415,18 +418,6 @@
     )(ids[None, :], *parts)
 
     late = template_spectra(1, packed_rows)
-    labels, slab_index = pl.pallas_call(
-        functools.partial(index_kernel, slots, versions, coarse),
-        out_shape=[
-            pltpu.HBM((tmpl_count, -(-live // LANE) * LANE), jnp.int32),
-            pltpu.HBM((32, templates), jnp.int32),
-        ],
-        in_specs=[full()] * 3,
-        out_specs=[full()] * 2,
-        compiler_params=pltpu.CompilerParams(vmem_limit_bytes=8 * MIB),
-        name="indices",
-    )(ids[None, :], channels.T, shifts.T)
-
     held = {0: packed_rows}
     bit = tmpl_count // 2
     while bit:
@@ -436,6 +427,7 @@
                 source, late = lax.optimization_barrier((source, late))
             held[d | bit] = lax.ppermute(source, "tmpl", [(i, i ^ bit) for i in range(tmpl_count)])
         bit //= 2
+    last = template_spectra(2, late)
     pieces = [held[d] for d in range(tmpl_count)]
 
     in_main = (0,) if small else tuple(range(tmpl_count))
@@ -466,6 +458,7 @@
         jnp.asarray(phase_table(versions, coarse)),
         early,
         late,
+        last,
         *[in_hbm(piece) if d in in_main else piece for d, piece in enumerate(pieces)],
     )
 

time: 44.9 us -> 42.6 us (0.949)
  waiting for transfers between devices: 4.17 us -> 2.27 us
  Pallas kernels: 25.9 us -> 25.3 us
    ppermute x7, waiting for transfers between devices: 4.16 us -> 2.26 us  [on_device(): lax.ppermute(mine[d], 'win', [(i, i ^ d) for i in range(win_count)])]
    pallas_call x3, Pallas kernels: 12.7 us -> 12.2 us  [template_spectra(): pl.pallas_call(kernel, out_shape=out_shape, grid=(1,), in_specs=[full()]...]
  transfers between devices with their start and end apart: 10 -> 10, of which waited for: 2 -> 1; matrix products, arithmetic and copies ran while one was open for 0% -> 0% of each run, Pallas kernels for 29% -> 29%
where the time goes in v5:
time: 42.6 us; the launch traced here: 42.4 us
  Pallas kernels  25.3 us (59%)
  starting transfers between devices  14.6 us (34%)
  waiting for transfers between devices  2.27 us (5%)
    ppermute x7, starting transfers between devices, on_device(): lax.ppermute(mine[d], 'win', [(i, i ^ d) for i in range(win_count)])  12.5 us
    pallas_call x3, Pallas kernels, template_spectra(): pl.pallas_call(kernel, out_shape=out_shape, grid=(1,), in_specs=[full()]...  12.2 us
    pallas_call x1, Pallas kernels, on_device(): pl.pallas_call(functools.partial(stack_kernel, live, versions, counts, in...  9.53 us
    pallas_call x1, Pallas kernels, on_device(): pl.pallas_call(spectra_kernel, out_shape=[jax.ShapeDtypeStruct((slots, NS...  3.12 us
    ppermute x7, waiting for transfers between devices, on_device(): lax.ppermute(mine[d], 'win', [(i, i ^ d) for i in range(win_count)])  2.26 us
    ppermute x3, starting transfers between devices, on_device(): lax.ppermute(source, 'tmpl', [(i, i ^ bit) for i in range(tmpl_count)])  2.13 us
  transfers between devices with their start and end apart: 10, of which 1 were waited for; matrix products, arithmetic and copies ran while one was open for 0% of the time, Pallas kernels for 29%

profile of v5, /device:TPU:0, one launch (start us, length us, event | category | flops | bytes accessed | tf_op | source)
XLA Modules:
  0.0 42.4 jit_solution(422051719446780083)
XLA Ops:
  0.0 0.0 copy-start.1
  0.0 0.0 copy-start.3
  0.0 0.0 copy-start.4
  0.0 3.1 %spectra.1 = (bf16[16,1792]{1,0:T(8,128)(2,1)S(1)}, bf16[16,1792]{1,0:T(8,128)(2,1)S(1)}, bf16[16,1792]{1,0:T(8,128)(2,1)S(1)}, bf16[16,1792]{1,0:T(8,128)(2,1)S...) custom-call(bf16[16,16384]{1,0:T(8,128)(2,1)} %raw_hbm.1, ...), custom_call_target="tpu_custom_call" | custom-call | tf_op jit(solution)/shard_map/spectra/pallas_call | solution.py:348
  3.1 3.0 %collective-permute-start = (bf16[16,1792]{1,0:T(8,128)(2,1)S(1)}, bf16[16,1792]{1,0:T(8,128)(2,1)S(1)}, u32[]{:S(2)}, u32[]{:S(2)}) collective-permute-start(bf16[16,1792]{1,0:T(8,128)(2,1)S(1)} %get-tuple-element.30), channel_id=1, source_target_pairs={{0,4},{4,0},{8,12},{12,8},{16,20},{20,16},{24,28},{28,24},{1,5},{5... | collective-permute-start | bytes 172040 | tf_op jit(solution)/shard_map/ppermute | solution.py:405
  6.2 1.6 %collective-permute-start.1 = (bf16[16,1792]{1,0:T(8,128)(2,1)S(1)}, bf16[16,1792]{1,0:T(8,128)(2,1)S(1)}, u32[]{:S(2)}, u32[]{:S(2)}) collective-permute-start(bf16[16,1792]{1,0:T(8,128)(2,1)S(1)} %get-tuple-element.31), channel_id=1, source_target_pairs={{0,8},{4,12},{8,0},{12,4},{16,24},{20,28},{24,16},{28,20},{1,9},{5... | collective-permute-start | bytes 172040 | tf_op jit(solution)/shard_map/ppermute | solution.py:405
  7.8 0.0 collective-permute-start.2
  7.8 3.0 %collective-permute-start.3 = (bf16[16,1792]{1,0:T(8,128)(2,1)S(1)}, bf16[16,1792]{1,0:T(8,128)(2,1)S(1)}, u32[]{:S(2)}, u32[]{:S(2)}) collective-permute-start(bf16[16,1792]{1,0:T(8,128)(2,1)S(1)} %get-tuple-element.33), channel_id=1, source_target_pairs={{0,16},{4,20},{8,24},{12,28},{16,0},{20,4},{24,8},{28,12},{1,17},{... | collective-permute-start | bytes 172040 | tf_op jit(solution)/shard_map/ppermute | solution.py:405
  10.7 1.3 %collective-permute-start.4 = (bf16[16,1792]{1,0:T(8,128)(2,1)S(1)}, bf16[16,1792]{1,0:T(8,128)(2,1)S(1)}, u32[]{:S(2)}, u32[]{:S(2)}) collective-permute-start(bf16[16,1792]{1,0:T(8,128)(2,1)S(1)} %get-tuple-element.34), channel_id=1, source_target_pairs={{0,20},{4,16},{8,28},{12,24},{16,4},{20,0},{24,12},{28,8},{1,21},{... | collective-permute-start | bytes 172040 | tf_op jit(solution)/shard_map/ppermute | solution.py:405
  12.0 0.0 collective-permute-done.rest_0_.rest_1_
  12.0 3.6 %collective-permute-start.5 = (bf16[16,1792]{1,0:T(8,128)(2,1)S(1)}, bf16[16,1792]{1,0:T(8,128)(2,1)S(1)}, u32[]{:S(2)}, u32[]{:S(2)}) collective-permute-start(bf16[16,1792]{1,0:T(8,128)(2,1)S(1)} %get-tuple-element.35), channel_id=1, source_target_pairs={{0,24},{4,28},{8,16},{12,20},{16,8},{20,12},{24,0},{28,4},{1,25},{... | collective-permute-start | bytes 172040 | tf_op jit(solution)/shard_map/ppermute | solution.py:405
  15.6 0.0 collective-permute-done.1.rest_1_.rest_2_
  15.6 0.0 collective-permute-start.6
  15.7 0.0 copy-done.1
  15.7 0.0 copy-done.3
  15.7 0.0 copy-done.4
  15.7 4.6 %templates.3 = (f32[16136,128]{1,0:T(8,128)S(1)}, s32[4,128]{1,0:T(4,128)}, s32[32,128]{1,0:T(8,128)}) custom-call(s32[30,128]{1,0:T(8,128)S(1)} %bitcast.6, bf16[16,1792]{1,0:T(8,128)(2,1)S(1)} %collective-permute-done.rest_0_.rest_1_, bf16[16,1792]{1,0:T(8,128)(2,1)S(1)} %collective-permute-done.1.rest_1_.rest_2_, s32[1,512]{1,0:T(1,128)S(1)} %bitcast.10, ...), custom_call_target="tpu_custom_call" | custom-call | tf_op jit(solution)/shard_map/templates/pallas_call | solution.py:390
  20.2 0.0 collective-permute-done.2.rest_3_
  20.3 0.0 collective-permute-done.3.rest_4_
  20.3 0.0 collective-permute-done.4.rest_5_
  20.3 0.0 collective-permute-done.5.rest_6_
  20.3 2.2 %collective-permute-done.6.rest_7_ = bf16[16,1792]{1,0:T(8,128)(2,1)S(1)} collective-permute-done((bf16[16,1792]{1,0:T(8,128)(2,1)S(1)}, bf16[16,1792]{1,0:T(8,128)(2,1)S(1)}, u32[]{:S(2)}, u32[]{:S(2)}) %collective-permute-start.6) | collective-permute-done | bytes 57376 | tf_op jit(solution)/shard_map/ppermute | solution.py:405
  22.5 0.5 %compact.1.rest_0_.rest_3_ = bf16[80,1792]{1,0:T(8,128)(2,1)S(1)} custom-call(s32[1,512]{1,0:T(1,128)S(1)} %bitcast.11, bf16[16,1792]{1,0:T(8,128)(2,1)S(1)} %get-tuple-element.43.rest_0_, bf16[16,1792]{1,0:T(8,128)(2,1)S(1)} %collective-permute-done.rest_0_.rest_1_, bf16[16,1792]{1,0:T(8,128)(2,1)S(1)} %collective-permute-done.1.rest_1_.rest_2_, ...), custom_call_target="tpu_custom_call" | custom-call | tf_op jit(solution)/shard_map/compact/pallas_call | solution.py:410
  23.0 0.0 copy-start
  23.0 1.6 %collective-permute-start.7 = (bf16[80,1792]{1,0:T(8,128)(2,1)S(1)}, bf16[80,1792]{1,0:T(8,128)(2,1)S(1)}, u32[]{:S(2)}, u32[]{:S(2)}) collective-permute-start(bf16[80,1792]{1,0:T(8,128)(2,1)S(1)} %compact.1.rest_0_.rest_3_), channel_id=1, source_target_pairs={{0,2},{1,3},{2,0},{3,1},{4,6},{5,7},{6,4},{7,5},{8,10},{9,11},{10,... | collective-permute-start | bytes 860168 | tf_op jit(solution)/shard_map/ppermute | solution.py:428
  24.6 0.0 collective-permute-start.8
  24.6 5.5 %templates.4.rest_0_.rest_1_ = f32[32264,128]{1,0:T(8,128)S(1)} custom-call(s32[30,128]{1,0:T(8,128)S(1)} %bitcast.7, bf16[80,1792]{1,0:T(8,128)(2,1)S(1)} %compact.1.rest_0_.rest_3_, bf16[30,400,128]{2,1,0:T(8,128)(2,1)} %bitcast.13, bf16[2,256,896]{2,1,0:T(8,128)(2,1)} %constant.10.clone.rest_5_.rest_2_), custom_call_target="tpu_custom_call" | custom-call | tf_op jit(solution)/shard_map/templates/pallas_call | solution.py:390
  30.1 0.0 copy-done
  30.1 0.0 copy-start.2
  30.1 0.0 collective-permute-done.7.rest_5_
  30.1 0.6 %collective-permute-start.9 = (bf16[80,1792]{1,0:T(8,128)(2,1)S(1)}, bf16[80,1792]{1,0:T(8,128)(2,1)S(1)}, u32[]{:S(2)}, u32[]{:S(2)}) collective-permute-start(bf16[80,1792]{1,0:T(8,128)(2,1)S(1)} %collective-permute-done.7.rest_5_), channel_id=1, source_target_pairs={{0,1},{1,0},{2,3},{3,2},{4,5},{5,4},{6,7},{7,6},{8,9},{9,8},{10,11... | collective-permute-start | bytes 860168 | tf_op jit(solution)/shard_map/ppermute | solution.py:428
  30.7 2.1 %templates.5.rest_2_ = f32[5384,128]{1,0:T(8,128)S(1)} custom-call(s32[30,128]{1,0:T(8,128)S(1)} %bitcast.8, f32[32264,128]{1,0:T(8,128)S(1)} %templates.4.rest_0_.rest_1_, bf16[30,400,128]{2,1,0:T(8,128)(2,1)} %bitcast.14, bf16[2,256,896]{2,1,0:T(8,128)(2,1)} %constant.10.clone.rest_5_.rest_2_), custom_call_target="tpu_custom_call" | custom-call | tf_op jit(solution)/shard_map/templates/pallas_call | solution.py:390
  32.8 0.0 collective-permute-done.8.rest_4_
  32.8 0.0 collective-permute-done.9.rest_6_
  32.8 0.0 copy-done.2
  32.8 9.5 %stacks.1 = f32[128,1024]{1,0:T(8,128)} custom-call(s32[4096]{0:T(1024)} %bitcast.15, s32[4,128]{1,0:T(4,128)} %get-tuple-element.41.label_ref, bf16[1792,1024]{1,0:T(8,128)(2,1)} %constant.8.clone.inverse_hbm, f32[3,16,128]{2,1,0:T(8,128)S(1)} %copy-done.2, f32[16136,128]{1,0:T(8,128)S(1)} %get-tuple-element.42.rest_0_, ...), custom_call_target="tpu_custom_call" | custom-call | tf_op jit(solution)/shard_map/stacks/pallas_call | solution.py:435
Async XLA Ops:
  0.0 15.7 %copy-start.1 = (s32[128,30]{0,1:T(8,128)S(1)}, s32[128,30]{0,1:T(8,128)}, u32[]{:S(2)}) copy-start(s32[128,30]{0,1:T(8,128)} %param.15) | copy-start | bytes 46084
  0.0 15.7 %copy-start.3 = (s32[128,30]{0,1:T(8,128)S(1)}, s32[128,30]{0,1:T(8,128)}, u32[]{:S(2)}) copy-start(s32[128,30]{0,1:T(8,128)} %param.14) | copy-start | bytes 46084
  0.0 15.7 %copy-start.4 = (s32[512]{0:T(512)S(1)}, s32[512]{0:T(512)}, u32[]{:S(2)}) copy-start(s32[512]{0:T(512)} %param.11) | copy-start | bytes 6148
  3.1 8.9 %collective-permute-start = (bf16[16,1792]{1,0:T(8,128)(2,1)S(1)}, bf16[16,1792]{1,0:T(8,128)(2,1)S(1)}, u32[]{:S(2)}, u32[]{:S(2)}) collective-permute-start(bf16[16,1792]{1,0:T(8,128)(2,1)S(1)} %get-tuple-element.30), channel_id=1, source_target_pairs={{0,4},{4,0},{8,12},{12,8},{16,20},{20,16},{24,28},{28,24},{1,5},{5... | collective-permute-start | bytes 172040 | tf_op jit(solution)/shard_map/ppermute | solution.py:405
  6.2 9.5 %collective-permute-start.1 = (bf16[16,1792]{1,0:T(8,128)(2,1)S(1)}, bf16[16,1792]{1,0:T(8,128)(2,1)S(1)}, u32[]{:S(2)}, u32[]{:S(2)}) collective-permute-start(bf16[16,1792]{1,0:T(8,128)(2,1)S(1)} %get-tuple-element.31), channel_id=1, source_target_pairs={{0,8},{4,12},{8,0},{12,4},{16,24},{20,28},{24,16},{28,20},{1,9},{5... | collective-permute-start | bytes 172040 | tf_op jit(solution)/shard_map/ppermute | solution.py:405
  7.8 12.5 %collective-permute-start.2 = (bf16[16,1792]{1,0:T(8,128)(2,1)S(1)}, bf16[16,1792]{1,0:T(8,128)(2,1)S(1)}, u32[]{:S(2)}, u32[]{:S(2)}) collective-permute-start(bf16[16,1792]{1,0:T(8,128)(2,1)S(1)} %get-tuple-element.32), channel_id=1, source_target_pairs={{0,12},{4,8},{8,4},{12,0},{16,28},{20,24},{24,20},{28,16},{1,13},{... | collective-permute-start | bytes 172040 | tf_op jit(solution)/shard_map/ppermute | solution.py:405
  7.8 12.5 %collective-permute-start.3 = (bf16[16,1792]{1,0:T(8,128)(2,1)S(1)}, bf16[16,1792]{1,0:T(8,128)(2,1)S(1)}, u32[]{:S(2)}, u32[]{:S(2)}) collective-permute-start(bf16[16,1792]{1,0:T(8,128)(2,1)S(1)} %get-tuple-element.33), channel_id=1, source_target_pairs={{0,16},{4,20},{8,24},{12,28},{16,0},{20,4},{24,8},{28,12},{1,17},{... | collective-permute-start | bytes 172040 | tf_op jit(solution)/shard_map/ppermute | solution.py:405
  10.7 9.5 %collective-permute-start.4 = (bf16[16,1792]{1,0:T(8,128)(2,1)S(1)}, bf16[16,1792]{1,0:T(8,128)(2,1)S(1)}, u32[]{:S(2)}, u32[]{:S(2)}) collective-permute-start(bf16[16,1792]{1,0:T(8,128)(2,1)S(1)} %get-tuple-element.34), channel_id=1, source_target_pairs={{0,20},{4,16},{8,28},{12,24},{16,4},{20,0},{24,12},{28,8},{1,21},{... | collective-permute-start | bytes 172040 | tf_op jit(solution)/shard_map/ppermute | solution.py:405
  12.0 8.2 %collective-permute-start.5 = (bf16[16,1792]{1,0:T(8,128)(2,1)S(1)}, bf16[16,1792]{1,0:T(8,128)(2,1)S(1)}, u32[]{:S(2)}, u32[]{:S(2)}) collective-permute-start(bf16[16,1792]{1,0:T(8,128)(2,1)S(1)} %get-tuple-element.35), channel_id=1, source_target_pairs={{0,24},{4,28},{8,16},{12,20},{16,8},{20,12},{24,0},{28,4},{1,25},{... | collective-permute-start | bytes 172040 | tf_op jit(solution)/shard_map/ppermute | solution.py:405
  15.6 6.9 %collective-permute-start.6 = (bf16[16,1792]{1,0:T(8,128)(2,1)S(1)}, bf16[16,1792]{1,0:T(8,128)(2,1)S(1)}, u32[]{:S(2)}, u32[]{:S(2)}) collective-permute-start(bf16[16,1792]{1,0:T(8,128)(2,1)S(1)} %get-tuple-element.36), channel_id=1, source_target_pairs={{0,28},{4,24},{8,20},{12,16},{16,12},{20,8},{24,4},{28,0},{1,29},{... | collective-permute-start | bytes 172040 | tf_op jit(solution)/shard_map/ppermute | solution.py:405
  23.0 7.1 %copy-start = (bf16[80,1792]{1,0:T(8,128)(2,1)}, bf16[80,1792]{1,0:T(8,128)(2,1)S(1)}, u32[]{:S(2)}) copy-start(bf16[80,1792]{1,0:T(8,128)(2,1)S(1)} %compact.1.rest_0_.rest_3_) | copy-start | bytes 860164
  23.0 7.1 %collective-permute-start.7 = (bf16[80,1792]{1,0:T(8,128)(2,1)S(1)}, bf16[80,1792]{1,0:T(8,128)(2,1)S(1)}, u32[]{:S(2)}, u32[]{:S(2)}) collective-permute-start(bf16[80,1792]{1,0:T(8,128)(2,1)S(1)} %compact.1.rest_0_.rest_3_), channel_id=1, source_target_pairs={{0,2},{1,3},{2,0},{3,1},{4,6},{5,7},{6,4},{7,5},{8,10},{9,11},{10,... | collective-permute-start | bytes 860168 | tf_op jit(solution)/shard_map/ppermute | solution.py:428
  24.6 8.2 %collective-permute-start.8 = (bf16[80,1792]{1,0:T(8,128)(2,1)S(1)}, bf16[80,1792]{1,0:T(8,128)(2,1)S(1)}, u32[]{:S(2)}, u32[]{:S(2)}) collective-permute-start(bf16[80,1792]{1,0:T(8,128)(2,1)S(1)} %compact.1.rest_0_.rest_3_), channel_id=1, source_target_pairs={{0,1},{1,0},{2,3},{3,2},{4,5},{5,4},{6,7},{7,6},{8,9},{9,8},{10,11... | collective-permute-start | bytes 860168 | tf_op jit(solution)/shard_map/ppermute | solution.py:428
  30.1 2.8 %copy-start.2 = (f32[3,16,128]{2,1,0:T(8,128)S(1)}, f32[3,16,128]{2,1,0:T(8,128)}, u32[]{:S(2)}) copy-start(f32[3,16,128]{2,1,0:T(8,128)} %constant.11.clone.phase_ref) | copy-start | bytes 73732
  30.1 2.7 %collective-permute-start.9 = (bf16[80,1792]{1,0:T(8,128)(2,1)S(1)}, bf16[80,1792]{1,0:T(8,128)(2,1)S(1)}, u32[]{:S(2)}, u32[]{:S(2)}) collective-permute-start(bf16[80,1792]{1,0:T(8,128)(2,1)S(1)} %collective-permute-done.7.rest_5_), channel_id=1, source_target_pairs={{0,1},{1,0},{2,3},{3,2},{4,5},{5,4},{6,7},{7,6},{8,9},{9,8},{10,11... | collective-permute-start | bytes 860168 | tf_op jit(solution)/shard_map/ppermute | solution.py:428

commit v6 on v5

--- a/solution.py
+++ b/solution.py
@@ -249,10 +249,14 @@
     slab_ref[CH:, :] = jnp.zeros((slab_ref.shape[0] - CH, slab_ref.shape[1]), jnp.int32)
 
 
-def stack_kernel(live, versions, counts, in_main, slab_ref, label_ref, inverse_hbm, phase_ref, *rest):
-    u_refs, pieces = rest[: len(counts)], rest[len(counts) : -8]
-    out_ref, inverse, flat, slabs, z, packed, held, sems = rest[-8:]
-    templates = out_ref.shape[0]
+def stack_kernel(live, versions, counts, in_main, slab_hbm, label_hbm, inverse_hbm, phase_ref, *rest):
+    u_refs, pieces = rest[: len(counts)], rest[len(counts) : -11]
+    out_hbm, inverse, flat, slabs, z, packed, held, result, slab_ref, label_ref, sems = rest[-11:]
+    templates = result.shape[0]
+    label_copy = pltpu.make_async_copy(label_hbm, label_ref, sems.at[2])
+    label_copy.start()
+    slab_copy = pltpu.make_async_copy(slab_hbm, slab_ref, sems.at[3])
+    slab_copy.start()
     table_copy = pltpu.make_async_copy(inverse_hbm, inverse, sems.at[0])
     table_copy.start()
     rows = held.shape[0]
@@ -261,6 +265,7 @@
     turns = [(phase_ref[a, 0:8], phase_ref[a, 8:16]) for a in range(1, versions)]
     fetches = [pltpu.make_async_copy(pieces[d], held, sems.at[1]) for d in in_main]
     fetches[0].start()
+    scattered = False
     for d in [d for d in range(len(pieces)) if d not in in_main] + list(in_main):
         piece = pieces[d]
         if d in in_main:
@@ -274,6 +279,9 @@
                 value = piece[g * 16 : (g + 1) * 16, column * LANE : (column + 1) * LANE].astype(F32)
                 for h in range(2):
                     flat[pl.ds((2 * g + h) * 8 * PITCH + column, 8, stride=PITCH), :] = value[h * 8 : (h + 1) * 8]
+        if not scattered:
+            label_copy.wait()
+        scattered = True
         for r in range(live):
             label = label_ref[tmpl ^ d, r] * versions
             x_cos = flat[r * PITCH : r * PITCH + 8]
@@ -309,6 +317,7 @@
             z[pl.ds(k + 8 * (templates + 1), 8, stride=templates + 1), :] = imag[0] + imag[1]
         return carry
 
+    slab_copy.wait()
     lax.fori_loop(0, templates // step, several, 0)
 
     first = lax.broadcasted_iota(jnp.int32, (templates, LANE), 1) == 0
@@ -321,7 +330,15 @@
         value = z[row * (templates + 1) : row * (templates + 1) + templates, :] * weight
         packed[:, column * LANE : (column + 1) * LANE] = value.astype(BF16)
     table_copy.wait()
-    out_ref[...] = jnp.dot(packed[...], inverse[...], preferred_element_type=F32)
+    stores = []
+    width = 2 * LANE
+    for n in range(WIN_DEV // width):
+        part = slice(n * width, (n + 1) * width)
+        result[:, part] = jnp.dot(packed[...], inverse[:, part], preferred_element_type=F32)
+        stores.append(pltpu.make_async_copy(result.at[:, part], out_hbm.at[:, part], sems.at[4 + n]))
+        stores[-1].start()
+    for store in stores:
+        store.wait()
 
 
 def full(space=pltpu.VMEM):
@@ -435,11 +452,11 @@
     return pl.pallas_call(
         functools.partial(stack_kernel, live, versions, counts, in_main),
         out_shape=jax.ShapeDtypeStruct((templates, WIN_DEV), F32),
-        in_specs=[full(pltpu.SMEM)] * 2
-        + [full(pltpu.HBM), full()]
+        in_specs=[full(pltpu.HBM)] * 3
+        + [full()]
         + [full()] * len(counts)
         + [full(space) for space in places],
-        out_specs=full(),
+        out_specs=full(pltpu.HBM),
         scratch_shapes=[
             pltpu.VMEM((2 * NF, WIN_DEV), BF16),
             pltpu.VMEM((rows * PITCH + 8, LANE), F32),
@@ -447,7 +464,10 @@
             pltpu.VMEM((16 * (templates + 1), LANE), F32),
             pltpu.VMEM((templates, NS), BF16),
             pltpu.VMEM((rows, NS), BF16),
-            pltpu.SemaphoreType.DMA((2,)),
+            pltpu.VMEM((templates, WIN_DEV), F32),
+            pltpu.SMEM((32 * templates,), jnp.int32),
+            pltpu.SMEM((tmpl_count, label_width), jnp.int32),
+            pltpu.SemaphoreType.DMA((8,)),
         ],
         compiler_params=pltpu.CompilerParams(vmem_limit_bytes=(19 if small else 58) * MIB),
         name="stacks",

time: 42.6 us -> 41.6 us (0.977)
  Pallas kernels: 25.3 us -> 24.4 us
    pallas_call x1, Pallas kernels: 9.53 us -> 8.57 us  [on_device(): pl.pallas_call(functools.partial(stack_kernel, live, versions, counts, in...]
where the time goes in v6:
time: 41.6 us; the launch traced here: 41.4 us
  Pallas kernels  24.4 us (59%)
  starting transfers between devices  14.6 us (35%)
  waiting for transfers between devices  2.27 us (5%)
    ppermute x7, starting transfers between devices, on_device(): lax.ppermute(mine[d], 'win', [(i, i ^ d) for i in range(win_count)])  12.5 us
    pallas_call x3, Pallas kernels, template_spectra(): pl.pallas_call(kernel, out_shape=out_shape, grid=(1,), in_specs=[full()]...  12.2 us
    pallas_call x1, Pallas kernels, on_device(): pl.pallas_call(functools.partial(stack_kernel, live, versions, counts, in...  8.57 us
    pallas_call x1, Pallas kernels, on_device(): pl.pallas_call(spectra_kernel, out_shape=[jax.ShapeDtypeStruct((slots, NS...  3.12 us
    ppermute x7, waiting for transfers between devices, on_device(): lax.ppermute(mine[d], 'win', [(i, i ^ d) for i in range(win_count)])  2.26 us
    ppermute x3, starting transfers between devices, on_device(): lax.ppermute(source, 'tmpl', [(i, i ^ bit) for i in range(tmpl_count)])  2.13 us
  transfers between devices with their start and end apart: 10, of which 1 were waited for; matrix products, arithmetic and copies ran while one was open for 0% of the time, Pallas kernels for 29%

profile of v6, /device:TPU:0, one launch (start us, length us, event | category | flops | bytes accessed | tf_op | source)
XLA Modules:
  0.0 41.4 jit_solution(11595800415632056619)
XLA Ops:
  0.0 0.0 copy-start.1
  0.0 0.0 copy-start.3
  0.0 0.0 copy-start.4
  0.0 3.1 %spectra.1 = (bf16[16,1792]{1,0:T(8,128)(2,1)S(1)}, bf16[16,1792]{1,0:T(8,128)(2,1)S(1)}, bf16[16,1792]{1,0:T(8,128)(2,1)S(1)}, bf16[16,1792]{1,0:T(8,128)(2,1)S...) custom-call(bf16[16,16384]{1,0:T(8,128)(2,1)} %raw_hbm.1, ...), custom_call_target="tpu_custom_call" | custom-call | tf_op jit(solution)/shard_map/spectra/pallas_call | solution.py:365
  3.1 3.0 %collective-permute-start = (bf16[16,1792]{1,0:T(8,128)(2,1)S(1)}, bf16[16,1792]{1,0:T(8,128)(2,1)S(1)}, u32[]{:S(2)}, u32[]{:S(2)}) collective-permute-start(bf16[16,1792]{1,0:T(8,128)(2,1)S(1)} %get-tuple-element.30), channel_id=1, source_target_pairs={{0,4},{4,0},{8,12},{12,8},{16,20},{20,16},{24,28},{28,24},{1,5},{5... | collective-permute-start | bytes 172040 | tf_op jit(solution)/shard_map/ppermute | solution.py:422
  6.2 1.6 %collective-permute-start.1 = (bf16[16,1792]{1,0:T(8,128)(2,1)S(1)}, bf16[16,1792]{1,0:T(8,128)(2,1)S(1)}, u32[]{:S(2)}, u32[]{:S(2)}) collective-permute-start(bf16[16,1792]{1,0:T(8,128)(2,1)S(1)} %get-tuple-element.31), channel_id=1, source_target_pairs={{0,8},{4,12},{8,0},{12,4},{16,24},{20,28},{24,16},{28,20},{1,9},{5... | collective-permute-start | bytes 172040 | tf_op jit(solution)/shard_map/ppermute | solution.py:422
  7.8 0.0 collective-permute-start.2
  7.8 3.0 %collective-permute-start.3 = (bf16[16,1792]{1,0:T(8,128)(2,1)S(1)}, bf16[16,1792]{1,0:T(8,128)(2,1)S(1)}, u32[]{:S(2)}, u32[]{:S(2)}) collective-permute-start(bf16[16,1792]{1,0:T(8,128)(2,1)S(1)} %get-tuple-element.33), channel_id=1, source_target_pairs={{0,16},{4,20},{8,24},{12,28},{16,0},{20,4},{24,8},{28,12},{1,17},{... | collective-permute-start | bytes 172040 | tf_op jit(solution)/shard_map/ppermute | solution.py:422
  10.7 1.3 %collective-permute-start.4 = (bf16[16,1792]{1,0:T(8,128)(2,1)S(1)}, bf16[16,1792]{1,0:T(8,128)(2,1)S(1)}, u32[]{:S(2)}, u32[]{:S(2)}) collective-permute-start(bf16[16,1792]{1,0:T(8,128)(2,1)S(1)} %get-tuple-element.34), channel_id=1, source_target_pairs={{0,20},{4,16},{8,28},{12,24},{16,4},{20,0},{24,12},{28,8},{1,21},{... | collective-permute-start | bytes 172040 | tf_op jit(solution)/shard_map/ppermute | solution.py:422
  12.0 0.0 collective-permute-done.rest_0_.rest_1_
  12.0 3.6 %collective-permute-start.5 = (bf16[16,1792]{1,0:T(8,128)(2,1)S(1)}, bf16[16,1792]{1,0:T(8,128)(2,1)S(1)}, u32[]{:S(2)}, u32[]{:S(2)}) collective-permute-start(bf16[16,1792]{1,0:T(8,128)(2,1)S(1)} %get-tuple-element.35), channel_id=1, source_target_pairs={{0,24},{4,28},{8,16},{12,20},{16,8},{20,12},{24,0},{28,4},{1,25},{... | collective-permute-start | bytes 172040 | tf_op jit(solution)/shard_map/ppermute | solution.py:422
  15.6 0.0 collective-permute-done.1.rest_1_.rest_2_
  15.6 0.0 collective-permute-start.6
  15.7 0.0 copy-done.1
  15.7 0.0 copy-done.3
  15.7 0.0 copy-done.4
  15.7 4.6 %templates.3 = (f32[16136,128]{1,0:T(8,128)S(1)}, s32[4,128]{1,0:T(4,128)}, s32[32,128]{1,0:T(8,128)}) custom-call(s32[30,128]{1,0:T(8,128)S(1)} %bitcast.6, bf16[16,1792]{1,0:T(8,128)(2,1)S(1)} %collective-permute-done.rest_0_.rest_1_, bf16[16,1792]{1,0:T(8,128)(2,1)S(1)} %collective-permute-done.1.rest_1_.rest_2_, s32[1,512]{1,0:T(1,128)S(1)} %bitcast.10, ...), custom_call_target="tpu_custom_call" | custom-call | tf_op jit(solution)/shard_map/templates/pallas_call | solution.py:407
  20.2 0.0 collective-permute-done.2.rest_3_
  20.3 0.0 collective-permute-done.3.rest_4_
  20.3 0.0 collective-permute-done.4.rest_5_
  20.3 0.0 collective-permute-done.5.rest_6_
  20.3 2.2 %collective-permute-done.6.rest_7_ = bf16[16,1792]{1,0:T(8,128)(2,1)S(1)} collective-permute-done((bf16[16,1792]{1,0:T(8,128)(2,1)S(1)}, bf16[16,1792]{1,0:T(8,128)(2,1)S(1)}, u32[]{:S(2)}, u32[]{:S(2)}) %collective-permute-start.6) | collective-permute-done | bytes 57376 | tf_op jit(solution)/shard_map/ppermute | solution.py:422
  22.5 0.5 %compact.1.rest_0_.rest_3_ = bf16[80,1792]{1,0:T(8,128)(2,1)S(1)} custom-call(s32[1,512]{1,0:T(1,128)S(1)} %bitcast.11, bf16[16,1792]{1,0:T(8,128)(2,1)S(1)} %get-tuple-element.43.rest_0_, bf16[16,1792]{1,0:T(8,128)(2,1)S(1)} %collective-permute-done.rest_0_.rest_1_, bf16[16,1792]{1,0:T(8,128)(2,1)S(1)} %collective-permute-done.1.rest_1_.rest_2_, ...), custom_call_target="tpu_custom_call" | custom-call | tf_op jit(solution)/shard_map/compact/pallas_call | solution.py:427
  23.0 0.0 copy-start
  23.0 1.6 %collective-permute-start.7 = (bf16[80,1792]{1,0:T(8,128)(2,1)S(1)}, bf16[80,1792]{1,0:T(8,128)(2,1)S(1)}, u32[]{:S(2)}, u32[]{:S(2)}) collective-permute-start(bf16[80,1792]{1,0:T(8,128)(2,1)S(1)} %compact.1.rest_0_.rest_3_), channel_id=1, source_target_pairs={{0,2},{1,3},{2,0},{3,1},{4,6},{5,7},{6,4},{7,5},{8,10},{9,11},{10,... | collective-permute-start | bytes 860168 | tf_op jit(solution)/shard_map/ppermute | solution.py:445
  24.6 0.0 collective-permute-start.8
  24.6 5.5 %templates.4.rest_0_.rest_1_ = f32[32264,128]{1,0:T(8,128)S(1)} custom-call(s32[30,128]{1,0:T(8,128)S(1)} %bitcast.7, bf16[80,1792]{1,0:T(8,128)(2,1)S(1)} %compact.1.rest_0_.rest_3_, bf16[30,400,128]{2,1,0:T(8,128)(2,1)} %bitcast.13, bf16[2,256,896]{2,1,0:T(8,128)(2,1)} %constant.10.clone.rest_5_.rest_2_), custom_call_target="tpu_custom_call" | custom-call | tf_op jit(solution)/shard_map/templates/pallas_call | solution.py:407
  30.1 0.0 copy-done
  30.1 0.0 copy-start.2
  30.1 0.0 collective-permute-done.7.rest_5_
  30.1 0.6 %collective-permute-start.9 = (bf16[80,1792]{1,0:T(8,128)(2,1)S(1)}, bf16[80,1792]{1,0:T(8,128)(2,1)S(1)}, u32[]{:S(2)}, u32[]{:S(2)}) collective-permute-start(bf16[80,1792]{1,0:T(8,128)(2,1)S(1)} %collective-permute-done.7.rest_5_), channel_id=1, source_target_pairs={{0,1},{1,0},{2,3},{3,2},{4,5},{5,4},{6,7},{7,6},{8,9},{9,8},{10,11... | collective-permute-start | bytes 860168 | tf_op jit(solution)/shard_map/ppermute | solution.py:445
  30.7 2.1 %templates.5.rest_2_ = f32[5384,128]{1,0:T(8,128)S(1)} custom-call(s32[30,128]{1,0:T(8,128)S(1)} %bitcast.8, f32[32264,128]{1,0:T(8,128)S(1)} %templates.4.rest_0_.rest_1_, bf16[30,400,128]{2,1,0:T(8,128)(2,1)} %bitcast.14, bf16[2,256,896]{2,1,0:T(8,128)(2,1)} %constant.10.clone.rest_5_.rest_2_), custom_call_target="tpu_custom_call" | custom-call | tf_op jit(solution)/shard_map/templates/pallas_call | solution.py:407
  32.8 0.0 collective-permute-done.8.rest_4_
  32.8 0.0 collective-permute-done.9.rest_6_
  32.8 0.0 copy-done.2
  32.8 8.6 %stacks.1 = f32[128,1024]{1,0:T(8,128)} custom-call(s32[4096]{0:T(1024)} %bitcast.15, s32[4,128]{1,0:T(4,128)} %get-tuple-element.41.label_hbm, bf16[1792,1024]{1,0:T(8,128)(2,1)} %constant.8.clone.inverse_hbm, f32[3,16,128]{2,1,0:T(8,128)S(1)} %copy-done.2, f32[16136,128]{1,0:T(8,128)S(1)} %get-tuple-element.42.rest_0_, ...), custom_call_target="tpu_custom_call" | custom-call | tf_op jit(solution)/shard_map/stacks/pallas_call | solution.py:452
Async XLA Ops:
  0.0 15.7 %copy-start.1 = (s32[128,30]{0,1:T(8,128)S(1)}, s32[128,30]{0,1:T(8,128)}, u32[]{:S(2)}) copy-start(s32[128,30]{0,1:T(8,128)} %param.15) | copy-start | bytes 46084
  0.0 15.7 %copy-start.3 = (s32[128,30]{0,1:T(8,128)S(1)}, s32[128,30]{0,1:T(8,128)}, u32[]{:S(2)}) copy-start(s32[128,30]{0,1:T(8,128)} %param.14) | copy-start | bytes 46084
  0.0 15.7 %copy-start.4 = (s32[512]{0:T(512)S(1)}, s32[512]{0:T(512)}, u32[]{:S(2)}) copy-start(s32[512]{0:T(512)} %param.11) | copy-start | bytes 6148
  3.1 8.9 %collective-permute-start = (bf16[16,1792]{1,0:T(8,128)(2,1)S(1)}, bf16[16,1792]{1,0:T(8,128)(2,1)S(1)}, u32[]{:S(2)}, u32[]{:S(2)}) collective-permute-start(bf16[16,1792]{1,0:T(8,128)(2,1)S(1)} %get-tuple-element.30), channel_id=1, source_target_pairs={{0,4},{4,0},{8,12},{12,8},{16,20},{20,16},{24,28},{28,24},{1,5},{5... | collective-permute-start | bytes 172040 | tf_op jit(solution)/shard_map/ppermute | solution.py:422
  6.2 9.5 %collective-permute-start.1 = (bf16[16,1792]{1,0:T(8,128)(2,1)S(1)}, bf16[16,1792]{1,0:T(8,128)(2,1)S(1)}, u32[]{:S(2)}, u32[]{:S(2)}) collective-permute-start(bf16[16,1792]{1,0:T(8,128)(2,1)S(1)} %get-tuple-element.31), channel_id=1, source_target_pairs={{0,8},{4,12},{8,0},{12,4},{16,24},{20,28},{24,16},{28,20},{1,9},{5... | collective-permute-start | bytes 172040 | tf_op jit(solution)/shard_map/ppermute | solution.py:422
  7.8 12.5 %collective-permute-start.2 = (bf16[16,1792]{1,0:T(8,128)(2,1)S(1)}, bf16[16,1792]{1,0:T(8,128)(2,1)S(1)}, u32[]{:S(2)}, u32[]{:S(2)}) collective-permute-start(bf16[16,1792]{1,0:T(8,128)(2,1)S(1)} %get-tuple-element.32), channel_id=1, source_target_pairs={{0,12},{4,8},{8,4},{12,0},{16,28},{20,24},{24,20},{28,16},{1,13},{... | collective-permute-start | bytes 172040 | tf_op jit(solution)/shard_map/ppermute | solution.py:422
  7.8 12.5 %collective-permute-start.3 = (bf16[16,1792]{1,0:T(8,128)(2,1)S(1)}, bf16[16,1792]{1,0:T(8,128)(2,1)S(1)}, u32[]{:S(2)}, u32[]{:S(2)}) collective-permute-start(bf16[16,1792]{1,0:T(8,128)(2,1)S(1)} %get-tuple-element.33), channel_id=1, source_target_pairs={{0,16},{4,20},{8,24},{12,28},{16,0},{20,4},{24,8},{28,12},{1,17},{... | collective-permute-start | bytes 172040 | tf_op jit(solution)/shard_map/ppermute | solution.py:422
  10.7 9.5 %collective-permute-start.4 = (bf16[16,1792]{1,0:T(8,128)(2,1)S(1)}, bf16[16,1792]{1,0:T(8,128)(2,1)S(1)}, u32[]{:S(2)}, u32[]{:S(2)}) collective-permute-start(bf16[16,1792]{1,0:T(8,128)(2,1)S(1)} %get-tuple-element.34), channel_id=1, source_target_pairs={{0,20},{4,16},{8,28},{12,24},{16,4},{20,0},{24,12},{28,8},{1,21},{... | collective-permute-start | bytes 172040 | tf_op jit(solution)/shard_map/ppermute | solution.py:422
  12.0 8.2 %collective-permute-start.5 = (bf16[16,1792]{1,0:T(8,128)(2,1)S(1)}, bf16[16,1792]{1,0:T(8,128)(2,1)S(1)}, u32[]{:S(2)}, u32[]{:S(2)}) collective-permute-start(bf16[16,1792]{1,0:T(8,128)(2,1)S(1)} %get-tuple-element.35), channel_id=1, source_target_pairs={{0,24},{4,28},{8,16},{12,20},{16,8},{20,12},{24,0},{28,4},{1,25},{... | collective-permute-start | bytes 172040 | tf_op jit(solution)/shard_map/ppermute | solution.py:422
  15.6 6.9 %collective-permute-start.6 = (bf16[16,1792]{1,0:T(8,128)(2,1)S(1)}, bf16[16,1792]{1,0:T(8,128)(2,1)S(1)}, u32[]{:S(2)}, u32[]{:S(2)}) collective-permute-start(bf16[16,1792]{1,0:T(8,128)(2,1)S(1)} %get-tuple-element.36), channel_id=1, source_target_pairs={{0,28},{4,24},{8,20},{12,16},{16,12},{20,8},{24,4},{28,0},{1,29},{... | collective-permute-start | bytes 172040 | tf_op jit(solution)/shard_map/ppermute | solution.py:422
  23.0 7.1 %copy-start = (bf16[80,1792]{1,0:T(8,128)(2,1)}, bf16[80,1792]{1,0:T(8,128)(2,1)S(1)}, u32[]{:S(2)}) copy-start(bf16[80,1792]{1,0:T(8,128)(2,1)S(1)} %compact.1.rest_0_.rest_3_) | copy-start | bytes 860164
  23.0 7.1 %collective-permute-start.7 = (bf16[80,1792]{1,0:T(8,128)(2,1)S(1)}, bf16[80,1792]{1,0:T(8,128)(2,1)S(1)}, u32[]{:S(2)}, u32[]{:S(2)}) collective-permute-start(bf16[80,1792]{1,0:T(8,128)(2,1)S(1)} %compact.1.rest_0_.rest_3_), channel_id=1, source_target_pairs={{0,2},{1,3},{2,0},{3,1},{4,6},{5,7},{6,4},{7,5},{8,10},{9,11},{10,... | collective-permute-start | bytes 860168 | tf_op jit(solution)/shard_map/ppermute | solution.py:445
  24.6 8.2 %collective-permute-start.8 = (bf16[80,1792]{1,0:T(8,128)(2,1)S(1)}, bf16[80,1792]{1,0:T(8,128)(2,1)S(1)}, u32[]{:S(2)}, u32[]{:S(2)}) collective-permute-start(bf16[80,1792]{1,0:T(8,128)(2,1)S(1)} %compact.1.rest_0_.rest_3_), channel_id=1, source_target_pairs={{0,1},{1,0},{2,3},{3,2},{4,5},{5,4},{6,7},{7,6},{8,9},{9,8},{10,11... | collective-permute-start | bytes 860168 | tf_op jit(solution)/shard_map/ppermute | solution.py:445
  30.1 2.8 %copy-start.2 = (f32[3,16,128]{2,1,0:T(8,128)S(1)}, f32[3,16,128]{2,1,0:T(8,128)}, u32[]{:S(2)}) copy-start(f32[3,16,128]{2,1,0:T(8,128)} %constant.11.clone.phase_ref) | copy-start | bytes 73732
  30.1 2.7 %collective-permute-start.9 = (bf16[80,1792]{1,0:T(8,128)(2,1)S(1)}, bf16[80,1792]{1,0:T(8,128)(2,1)S(1)}, u32[]{:S(2)}, u32[]{:S(2)}) collective-permute-start(bf16[80,1792]{1,0:T(8,128)(2,1)S(1)} %collective-permute-done.7.rest_5_), channel_id=1, source_target_pairs={{0,1},{1,0},{2,3},{3,2},{4,5},{5,4},{6,7},{7,6},{8,9},{9,8},{10,11... | collective-permute-start | bytes 860168 | tf_op jit(solution)/shard_map/ppermute | solution.py:445
